TPU v7x, 32 devices: a whole 2x2x4 slice. The times are simulated.
32 devices in a mesh: dp: 8 (over y, x, core), mp: 4 (over z).
Axes of the slice: x: 2, y: 2, z: 4, core: 2. Of those that a mesh axis runs over, the one named last changes fastest.
Arguments:
- patches: bfloat16 [16384, 1152], P(('dp', 'mp')), may hold values from -2.5 to 2.5
- cotangent: bfloat16 [16384, 1152], P(('dp', 'mp')), may hold values from -2.5 to 2.5
- conditioning: bfloat16 [40, 1152], P('dp'), may hold values from -2.5 to 2.5
- segment: int32 [16384], P('dp'), may hold values from 0 to 3, as said below
- image_ids: int32 [16384], P(('dp', 'mp')), may hold values from 0 to 39, as said below
- w_ada: bfloat16 [1152, 6912], P(None, ('dp', 'mp')), may hold values from -0.1875 to 0.1875
- b_ada: bfloat16 [6912], P(('dp', 'mp')), may hold values from -0.75 to 0.75
- w_qkv: bfloat16 [3, 1152, 1152], P(None, None, 'mp'), may hold values from -0.1875 to 0.1875
- b_qv: bfloat16 [2, 1152], P(None, 'mp'), may hold values from -0.75 to 0.75
- w_out: bfloat16 [1152, 1152], P('mp'), may hold values from -0.75 to 0.75
- b_out: bfloat16 [1152], replicated, may hold values from -0.75 to 0.75
- w_fc1: bfloat16 [1152, 4608], P(None, 'mp'), may hold values from -0.1875 to 0.1875
- b_fc1: bfloat16 [4608], P('mp'), may hold values from -0.75 to 0.75
- w_fc2: bfloat16 [4608, 1152], P('mp'), may hold values from -0.09375 to 0.09375
- b_fc2: bfloat16 [1152], replicated, may hold values from -0.75 to 0.75
Outputs:
- output: bfloat16 [16384, 1152], P(('dp', 'mp'))
- grad_patches: float32 [16384, 1152], P(('dp', 'mp'))
- grad_conditioning: float32 [40, 1152], P('dp')
- grad_w_ada: float32 [1152, 6912], P(None, ('dp', 'mp'))
- grad_b_ada: float32 [6912], P(('dp', 'mp'))
- grad_w_qkv: float32 [3, 1152, 1152], P(None, None, 'mp')
- grad_b_qv: float32 [2, 1152], P(None, 'mp')
- grad_w_out: float32 [1152, 1152], P('mp')
- grad_b_out: float32 [1152], replicated
- grad_w_fc1: float32 [1152, 4608], P(None, 'mp')
- grad_b_fc1: float32 [4608], P('mp')
- grad_w_fc2: float32 [4608, 1152], P('mp')
- grad_b_fc2: float32 [1152], replicated
Inputs may be any that keep to these rules, and one draw needn't show every extreme that they name: Each packed row of 1024 patches holds either one image, all its patches with segment 0, or four images of 256 patches with segments 0, 1, 2, 3 in order; half of the 16 rows are of each kind. `image_ids`: all patches of one image carry one number, and each number of 0 to 39 belongs to exactly one image.
All inputs are finite; a program needn't handle non-finite values.
Results may differ from a plain program's by a relative error of at most 0.017.
The roundings to bfloat16 on the way count: a program that leaves them out, or rounds other values in their place, can miss the bound.
Values may be sent and summed in bfloat16 or wider, within the bound.
A program may use at most 192 MiB of HBM per device.

v0:
```python
import math

import jax
import jax.numpy as jnp
from jax import lax
from jax.sharding import PartitionSpec as P

HD = 72
L = 1024


def layer_norm(vector):
    centred = vector - jnp.mean(vector, axis=-1, keepdims=True)
    spread = jnp.mean(centred * centred, axis=-1, keepdims=True)
    return centred * lax.rsqrt(spread + 1e-06)


def modulate(input_rows, shift_in, scale_in):
    return layer_norm(input_rows) * (1.0 + scale_in) + shift_in


def gelu_tanh(values_in):
    inner_arg = math.sqrt(2.0 / math.pi) * (
        values_in + 0.044715 * values_in * values_in * values_in
    )
    return 0.5 * values_in * (1.0 + jnp.tanh(inner_arg))


def silu_fn(values_in):
    return values_in * jax.nn.sigmoid(values_in)


def gather_rows(values_in):
    return lax.all_gather(values_in, "mp", axis=0, tiled=True)


def reduce_rows(term_fn, row_count):
    return lax.psum_scatter(
        term_fn(jnp.int32(0), row_count * lax.axis_size("mp")).astype(jnp.bfloat16),
        "mp",
        scatter_dimension=0,
        tiled=True,
    ).astype(jnp.float32)


def block_scores(query_block, keys, seg_block, segment_rows):
    scores = jnp.einsum(
        "qhd,khd->hqk", query_block, keys, preferred_element_type=jnp.float32
    ) * HD ** (-0.5)
    allowed = seg_block[:, None] == segment_rows[None, :]
    return jnp.where(allowed[None], scores, -1e30)


def attend_forward(row_in):
    queries, keys, values, segment_rows = row_in
    query_len = min(512, L)
    num_blocks = L // query_len
    num_heads = queries.shape[1]

    def one_block(block_in):
        query_block, seg_block = block_in
        scores = block_scores(query_block, keys, seg_block, segment_rows)
        highest = jnp.max(scores, axis=-1, keepdims=True)
        exponent = jnp.exp(scores - highest)
        totals = jnp.sum(exponent, axis=-1, keepdims=True)
        weights_low = (exponent / totals).astype(jnp.bfloat16)
        context = jnp.einsum(
            "hqk,khd->qhd", weights_low, values, preferred_element_type=jnp.float32
        ).astype(jnp.bfloat16)
        return (context, (highest + jnp.log(totals))[..., 0])

    context, log_total = lax.map(
        one_block,
        (
            queries.reshape(num_blocks, query_len, num_heads, HD),
            segment_rows.reshape(num_blocks, query_len),
        ),
    )
    return (context.reshape(L, num_heads, HD), log_total)


def attend_backward(row_in):
    queries, keys, values, segment_rows, log_total, grad_context = row_in
    query_len = min(512, L)
    num_blocks = L // query_len
    num_heads = queries.shape[1]

    def one_block(totals, block_in):
        query_block, seg_block, block_total, grad_block = block_in
        scores = block_scores(query_block, keys, seg_block, segment_rows)
        weights_soft = jnp.exp(scores - block_total[..., None])
        weights_low = weights_soft.astype(jnp.bfloat16)
        grad_values = totals[1] + jnp.einsum(
            "hqk,qhd->khd", weights_low, grad_block, preferred_element_type=jnp.float32
        )
        grad_weights = jnp.einsum(
            "qhd,khd->hqk", grad_block, values, preferred_element_type=jnp.float32
        )
        inner_sum = jnp.sum(weights_soft * grad_weights, axis=-1, keepdims=True)
        grad_scores = (weights_soft * (grad_weights - inner_sum)).astype(jnp.bfloat16)
        grad_query = jnp.einsum(
            "hqk,khd->qhd", grad_scores, keys, preferred_element_type=jnp.float32
        ) * HD ** (-0.5)
        grad_keys = totals[0] + jnp.einsum(
            "hqk,qhd->khd", grad_scores, query_block, preferred_element_type=jnp.float32
        ) * HD ** (-0.5)
        return ((grad_keys, grad_values), grad_query)

    zero_init = jnp.zeros(keys.shape, jnp.float32)
    blocks_in = (
        queries.reshape(num_blocks, query_len, num_heads, HD),
        segment_rows.reshape(num_blocks, query_len),
        log_total,
        grad_context.reshape(num_blocks, query_len, num_heads, HD),
    )
    (grad_keys, grad_values), grad_query = lax.scan(one_block, (zero_init, zero_init), blocks_in)
    return (grad_query.reshape(keys.shape), grad_keys, grad_values)


def attention_forward(attn_full, w_qkv, b_qv, segment):
    projected = jnp.einsum("td,ndc->ntc", attn_full, w_qkv, preferred_element_type=jnp.float32)
    zero_bias = jnp.zeros_like(b_qv[0])
    biases = jnp.stack([b_qv[0], zero_bias, b_qv[1]]).astype(jnp.float32)
    projected = (projected + biases[:, None, :]).astype(jnp.bfloat16)
    num_rows = attn_full.shape[0] // L
    num_heads = w_qkv.shape[2] // HD
    shaped = projected.reshape(3, num_rows, L, num_heads, HD)
    context, log_total = lax.map(
        attend_forward, (shaped[0], shaped[1], shaped[2], segment.reshape(num_rows, L))
    )
    return (shaped, context.reshape(num_rows * L, num_heads * HD), log_total)


def attention_backward(shaped, segment, log_total, grad_context):
    num_rows = shaped.shape[1]
    num_heads = shaped.shape[3]
    grad_rows = grad_context.reshape(num_rows, L, num_heads, HD)
    grad_query, grad_keys, grad_values = lax.map(
        attend_backward,
        (shaped[0], shaped[1], shaped[2], segment.reshape(num_rows, L), log_total, grad_rows),
    )
    stacked = jnp.stack([grad_query, grad_keys, grad_values])
    return stacked.reshape(3, num_rows * L, num_heads * HD).astype(jnp.bfloat16)


def mlp_hidden(mlp_full, w_fc1, b_fc1):
    pre_act = jnp.dot(mlp_full, w_fc1, preferred_element_type=jnp.float32) + b_fc1.astype(
        jnp.float32
    )
    return (pre_act, gelu_tanh(pre_act).astype(jnp.bfloat16))


def on_device(
    patches,
    cotangent,
    conditioning,
    segment,
    image_ids,
    w_ada,
    b_ada,
    w_qkv,
    b_qv,
    w_out,
    b_out,
    w_fc1,
    b_fc1,
    w_fc2,
    b_fc2,
):
    patch_wide = patches.astype(jnp.float32)
    grad_output = cotangent.astype(jnp.float32)
    rows_here = patches.shape[0]
    cond_all = lax.all_gather(conditioning, "dp", axis=0, tiled=True)
    image_count = cond_all.shape[0]
    silu_cond = silu_fn(cond_all.astype(jnp.float32)).astype(jnp.bfloat16)
    weight_all, bias_all = (
        lax.all_gather(w_ada, ("dp", "mp"), axis=1, tiled=True),
        lax.all_gather(b_ada, ("dp", "mp"), axis=0, tiled=True),
    )
    modulation_lookup = (
        jnp.dot(silu_cond, weight_all, preferred_element_type=jnp.float32)
        + bias_all.astype(jnp.float32)
    ).astype(jnp.bfloat16)
    modulation = jnp.take(modulation_lookup, image_ids, axis=0).astype(jnp.float32)
    shift_attn, scale_attn, gate_attn, shift_mlp, scale_mlp, gate_mlp = jnp.split(
        modulation, 6, axis=1
    )
    attn_in = modulate(patch_wide, shift_attn, scale_attn).astype(jnp.bfloat16)
    attn_full = gather_rows(attn_in)
    shaped, context, log_total = attention_forward(attn_full, w_qkv, b_qv, segment)

    def out_term(start_row, row_count):
        return jnp.dot(context, w_out, preferred_element_type=jnp.float32)

    attn_out = reduce_rows(out_term, rows_here) + b_out.astype(jnp.float32)
    resid = patch_wide + gate_attn * attn_out
    mlp_in = modulate(resid, shift_mlp, scale_mlp).astype(jnp.bfloat16)
    mlp_full = gather_rows(mlp_in)
    pre_act, hidden = mlp_hidden(mlp_full, w_fc1, b_fc1)

    def fc2_term(start_row, row_count):
        return jnp.dot(hidden, w_fc2, preferred_element_type=jnp.float32)

    mlp_out = reduce_rows(fc2_term, rows_here) + b_fc2.astype(jnp.float32)
    output = (resid + gate_mlp * mlp_out).astype(jnp.bfloat16)
    grad_gate_mlp = grad_output * mlp_out
    grad_mlp_low = (gate_mlp * grad_output).astype(jnp.bfloat16)
    grad_mlp_full = gather_rows(grad_mlp_low)
    mlp_again = lax.optimization_barrier((mlp_in, grad_mlp_low))[0]
    mlp_full = gather_rows(mlp_again)
    pre_act, hidden = mlp_hidden(mlp_full, w_fc1, b_fc1)
    grad_w_fc2 = jnp.einsum("tf,td->fd", hidden, grad_mlp_full, preferred_element_type=jnp.float32)
    grad_b_fc2 = jnp.sum(grad_mlp_full, axis=0, dtype=jnp.float32)
    grad_hidden = jnp.einsum("td,fd->tf", grad_mlp_full, w_fc2, preferred_element_type=jnp.float32)
    _, gelu_back = jax.vjp(gelu_tanh, pre_act)
    grad_pre = gelu_back(grad_hidden)[0].astype(jnp.bfloat16)
    grad_w_fc1 = jnp.einsum("td,tf->df", mlp_full, grad_pre, preferred_element_type=jnp.float32)
    grad_b_fc1 = jnp.sum(grad_pre, axis=0, dtype=jnp.float32)

    def fc1_term(start_row, row_count):
        return jnp.einsum("tf,df->td", grad_pre, w_fc1, preferred_element_type=jnp.float32)

    grad_mlp_in = reduce_rows(fc1_term, rows_here)
    _, mlp_back = jax.vjp(modulate, resid, shift_mlp, scale_mlp)
    grad_resid_norm, grad_shift_mlp, grad_scale_mlp = mlp_back(grad_mlp_in)
    grad_resid = grad_output + grad_resid_norm
    grad_gate_attn = grad_resid * attn_out
    grad_attn_low = (gate_attn * grad_resid).astype(jnp.bfloat16)
    grad_attn_full = gather_rows(grad_attn_low)
    attn_again = lax.optimization_barrier((attn_in, grad_attn_low))[0]
    attn_full = gather_rows(attn_again)
    shaped, context, log_total = attention_forward(attn_full, w_qkv, b_qv, segment)
    grad_w_out = jnp.einsum(
        "tc,td->cd", context, grad_attn_full, preferred_element_type=jnp.float32
    )
    grad_b_out = jnp.sum(grad_attn_full, axis=0, dtype=jnp.float32)
    grad_context = jnp.einsum(
        "td,cd->tc", grad_attn_full, w_out, preferred_element_type=jnp.float32
    ).astype(jnp.bfloat16)
    grad_proj = attention_backward(shaped, segment, log_total, grad_context)
    grad_w_qkv = jnp.einsum("td,ntc->ndc", attn_full, grad_proj, preferred_element_type=jnp.float32)
    grad_b_qv = jnp.stack(
        [
            jnp.sum(grad_proj[0], axis=0, dtype=jnp.float32),
            jnp.sum(grad_proj[2], axis=0, dtype=jnp.float32),
        ]
    )

    def qkv_term(start_row, row_count):
        return jnp.einsum("ntc,ndc->td", grad_proj, w_qkv, preferred_element_type=jnp.float32)

    grad_attn_in = reduce_rows(qkv_term, rows_here)
    _, attn_back = jax.vjp(modulate, patch_wide, shift_attn, scale_attn)
    grad_input_norm, grad_shift_attn, grad_scale_attn = attn_back(grad_attn_in)
    grad_patches = grad_resid + grad_input_norm
    grad_mods = jnp.concatenate(
        [
            grad_shift_attn,
            grad_scale_attn,
            grad_gate_attn,
            grad_shift_mlp,
            grad_scale_mlp,
            grad_gate_mlp,
        ],
        axis=1,
    )
    per_image = jax.ops.segment_sum(grad_mods, image_ids, num_segments=image_count)
    grad_columns = lax.psum_scatter(
        per_image, ("dp", "mp"), scatter_dimension=1, tiled=True
    ).astype(jnp.bfloat16)
    grad_w_ada = jnp.einsum(
        "id,ic->dc", silu_cond, grad_columns, preferred_element_type=jnp.float32
    )
    grad_b_ada = jnp.sum(grad_columns, axis=0, dtype=jnp.float32)
    grad_silu_part = jnp.einsum(
        "ic,dc->id", grad_columns, w_ada, preferred_element_type=jnp.float32
    )
    grad_silu_rows = lax.psum_scatter(grad_silu_part, "dp", scatter_dimension=0, tiled=True)
    grad_silu = lax.psum(grad_silu_rows, "mp")
    _, silu_back = jax.vjp(silu_fn, conditioning.astype(jnp.float32))
    grad_cond = silu_back(grad_silu)[0]
    reduced = lax.psum(
        (
            grad_w_qkv,
            grad_b_qv,
            grad_w_out,
            grad_b_out,
            grad_w_fc1,
            grad_b_fc1,
            grad_w_fc2,
            grad_b_fc2,
        ),
        "dp",
    )
    return (
        output,
        grad_patches,
        grad_cond,
        grad_w_ada,
        grad_b_ada,
        reduced[0],
        reduced[1],
        reduced[2],
        reduced[3],
        reduced[4],
        reduced[5],
        reduced[6],
        reduced[7],
    )


def solution(mesh):
    in_specs = (
        P(("dp", "mp"), None),
        P(("dp", "mp"), None),
        P("dp", None),
        P("dp"),
        P(("dp", "mp")),
        P(None, ("dp", "mp")),
        P(("dp", "mp")),
        P(None, None, "mp"),
        P(None, "mp"),
        P("mp", None),
        P(),
        P(None, "mp"),
        P("mp"),
        P("mp", None),
        P(),
    )
    out_specs = (
        P(("dp", "mp"), None),
        P(("dp", "mp"), None),
        P("dp", None),
        P(None, ("dp", "mp")),
        P(("dp", "mp")),
        P(None, None, "mp"),
        P(None, "mp"),
        P("mp", None),
        P(),
        P(None, "mp"),
        P("mp"),
        P("mp", None),
        P(),
    )
    return jax.shard_map(
        on_device, mesh=mesh, in_specs=in_specs, out_specs=out_specs, check_vma=False
    )
```

profile of v0, /device:TPU:0, one launch (start us, length us, event | category | flops | bytes accessed | tf_op | source)
XLA Modules:
  0.0 1710.8 jit_solution(10610457725668222538)
XLA Ops:
  8.9 43.0 %all-reduce = bf16[6912]{0:T(1024)(128)(2,1)S(1)} all-reduce(bf16[6912]{0:T(1024)(128)(2,1)S(1)} %dynamic-update-slice), channel_id=1, replica_groups=mesh['dp'=8,'mp'=4] {'dp','mp'}, use_global_device_ids=true, to_apply=%add | all-reduce | flops 6912 | bytes 27648
  51.8 10.1 all-gather
  66.5 59.9 %all-gather.9.cloned.1.call-done = bf16[1152,6912]{0,1:T(8,128)(2,1)} async-done(((bf16[1152,216]{0,1:T(8,128)(2,1)}), bf16[1152,6912]{0,1:T(8,128)(2,1)}) %all-gather.9.cloned.1.call-update) | async-done | bytes 15925264 | tf_op jit(solution)/shard_map/all_gather | solution.py:177
  126.4 10.8 fusion.82
  137.2 6.7 gather_fusion
  143.9 9.2 select_convert_fusion
  157.5 87.3 %all-gather.11.cloned.1.call-done = bf16[2048,1152]{1,0:T(8,128)(2,1)} async-done(((bf16[512,1152]{1,0:T(8,128)(2,1)}), bf16[2048,1152]{1,0:T(8,128)(2,1)}) %all-gather.11.cloned.1.call-update) | async-done | bytes 4718608 | tf_op jit(solution)/shard_map/all_gather | solution.py:34
  244.8 7.7 fusion.93
  276.0 81.4 %while.74 = (s32[]{:T(128)}, bf16[2,1024,4,72]{3,2,1,0:T(4,128)(2,1)}, bf16[2,1024,4,72]{1,3,2,0:T(8,128)(2,1)}, s32[2,1024]{1,0:T(2,128)S(1)}, bf16[2,1024,4,72...) while((s32[]{:T(128)}, ...), condition=%wide.region_7.8_spmd, body=%wide.region_2.7_spmd.sunk | while | flops 617235456 | bytes 28817712 | solution.py:128
  285.0 27.1 %while.79 = (s32[]{:T(128)}, bf16[2,512,4,72]{1,3,2,0:T(8,128)(2,1)}, s32[2,512]{1,0:T(2,128)S(1)}, s32[1024]{0:T(1024)S(1)}, bf16[2,512,4,72]{1,3,2,0:T(8,128)(...) while((s32[]{:T(128)}, bf16[2,512,4,72]{1,3,2,0:T(8,128)(2,1)}, ...), condition=%wide.region_6.6_spmd, body=%wide.region_3.5_spmd.sunk | while | flops 617235456 | bytes 19621992 | solution.py:72
  285.4 7.5 fusion.237
  298.9 7.6 fusion.237
  306.5 5.6 fusion.238
  325.5 27.1 %while.79 = (s32[]{:T(128)}, bf16[2,512,4,72]{1,3,2,0:T(8,128)(2,1)}, s32[2,512]{1,0:T(2,128)S(1)}, s32[1024]{0:T(1024)S(1)}, bf16[2,512,4,72]{1,3,2,0:T(8,128)(...) while((s32[]{:T(128)}, bf16[2,512,4,72]{1,3,2,0:T(8,128)(2,1)}, ...), condition=%wide.region_6.6_spmd, body=%wide.region_3.5_spmd.sunk | while | flops 617235456 | bytes 19621992 | solution.py:72
  325.9 7.5 fusion.237
  333.4 5.6 fusion.238
  339.4 7.5 fusion.237
  347.0 5.6 fusion.238
  357.5 6.3 copy.80
  370.6 83.2 %reduce-scatter.6.cloned.1.call-done = bf16[512,1152]{1,0:T(8,128)(2,1)} async-done(((bf16[2048,1152]{1,0:T(8,128)(2,1)}), bf16[512,1152]{1,0:T(8,128)(2,1)}) %reduce-scatter.6.cloned.1.call-update) | async-done | bytes 1179664 | tf_op jit(solution)/shard_map/reduce_scatter | solution.py:38
  465.1 88.9 %all-gather.15.cloned.1.call-done = bf16[2048,1152]{1,0:T(8,128)(2,1)} async-done(((bf16[512,1152]{1,0:T(8,128)(2,1)}), bf16[2048,1152]{1,0:T(8,128)(2,1)}) %all-gather.15.cloned.1.call-update) | async-done | bytes 4718608 | tf_op jit(solution)/shard_map/all_gather | solution.py:34
  553.9 11.8 fusion.146
  565.8 78.0 %all-gather.17.cloned.1.call-done = bf16[2048,1152]{1,0:T(8,128)(2,1)} async-done(((bf16[512,1152]{1,0:T(8,128)(2,1)}), bf16[2048,1152]{1,0:T(8,128)(2,1)}) %all-gather.17.cloned.1.call-update) | async-done | bytes 4718608 | tf_op jit(solution)/shard_map/all_gather | solution.py:34
  643.8 18.3 %convert_reduce_fusion.1 = (f32[1152]{0:T(1024)}, bf16[2048,1152]{1,0:T(8,128)(2,1)S(1)}, f32[2048,1152]{1,0:T(8,128)}) fusion(f32[2048,1152]{1,0:T(8,128)} %fusion.146, f32[1152]{0:T(1024)S(1)} %convert_element_type.167, bf16[2048,1152]{1,0:T(8,128)(2,1)} %all-gather.17.cloned.1.call-done, bf16[1152,1152]{1,0:T(8,128)(2,1)S(1)} %copy-done), kind=kOutput, calls=%fused_computation.116 | convolution fusion | flops 5499517952 | bytes 30974976 | tf_op jit(solution)/shard_map/dot_general | solution.py:147
  664.3 8.6 convolution_convert_fusion
  672.9 60.8 %all-gather.13.cloned.1.call-done = bf16[2048,1152]{1,0:T(8,128)(2,1)} async-done(((bf16[512,1152]{1,0:T(8,128)(2,1)}), bf16[2048,1152]{1,0:T(8,128)(2,1)}) %all-gather.13.cloned.1.call-update) | async-done | bytes 4718608 | tf_op jit(solution)/shard_map/all_gather | solution.py:34
  733.7 17.9 %convolution_convert_fusion.1 = bf16[2048,1152]{1,0:T(8,128)(2,1)} fusion(bf16[1152,1152]{1,0:T(8,128)(2,1)} %param.40, bf16[2048,1152]{1,0:T(8,128)(2,1)} %all-gather.13.cloned.1.call-done, bf16[1152,1152]{1,0:T(8,128)(2,1)S(1)} %copy-done, f32[1152]{0:T(1024)S(1)} %convert_element_type.167), kind=kOutput, calls=%fused_computation.122 | convolution fusion | flops 10897588224 | bytes 14750208 | tf_op jit(solution)/shard_map/dot_general | solution.py:202
  752.9 67.4 %reduce-scatter.10.cloned.1.call-done = bf16[512,1152]{1,0:T(8,128)(2,1)} async-done(((bf16[2048,1152]{1,0:T(8,128)(2,1)}), bf16[512,1152]{1,0:T(8,128)(2,1)}) %reduce-scatter.10.cloned.1.call-update) | async-done | bytes 1179664 | tf_op jit(solution)/shard_map/reduce_scatter | solution.py:38
  823.5 85.5 %reduce-scatter.8.cloned.1.call-done = bf16[512,1152]{1,0:T(8,128)(2,1)} async-done(((bf16[2048,1152]{1,0:T(8,128)(2,1)}), bf16[512,1152]{1,0:T(8,128)(2,1)}) %reduce-scatter.8.cloned.1.call-update) | async-done | bytes 1179664 | tf_op jit(solution)/shard_map/reduce_scatter | solution.py:38
  918.6 89.4 %all-gather.21.cloned.1.call-done = bf16[2048,1152]{1,0:T(8,128)(2,1)} async-done(((bf16[512,1152]{1,0:T(8,128)(2,1)}), bf16[2048,1152]{1,0:T(8,128)(2,1)}) %all-gather.21.cloned.1.call-update) | async-done | bytes 4718608 | tf_op jit(solution)/shard_map/all_gather | solution.py:34
  1014.7 83.1 %all-gather.19.cloned.1.call-done = bf16[2048,1152]{1,0:T(8,128)(2,1)} async-done(((bf16[512,1152]{1,0:T(8,128)(2,1)}), bf16[2048,1152]{1,0:T(8,128)(2,1)}) %all-gather.19.cloned.1.call-update) | async-done | bytes 4718608 | tf_op jit(solution)/shard_map/all_gather | solution.py:34
  1097.9 7.7 fusion.94
  1118.8 53.0 %while.76 = (s32[]{:T(128)}, bf16[2,1024,4,72]{3,2,1,0:T(4,128)(2,1)}, f32[2,2,4,512]{3,2,1,0:T(4,128)}, bf16[2,1024,4,72]{1,3,2,0:T(8,128)(2,1)S(1)}, s32[2,102...) while((s32[]{:T(128)}, ...), condition=%wide.region_20.21_spmd, body=%wide.region_15.20_spmd.sunk | while | flops 629815296 | bytes 45087196 | solution.py:128
  1122.5 18.5 %while.80 = (s32[]{:T(128)}, bf16[2,512,4,72]{1,3,2,0:T(8,128)(2,1)}, f32[2,4,512]{2,1,0:T(4,128)}, s32[2,512]{1,0:T(2,128)S(1)}, s32[1024]{0:T(1024)S(1)}, /*in...) while((s32[]{:T(128)}, ...), condition=%wide.region_19.19_spmd, body=%wide.region_16.18_spmd.sunk | while | flops 629815296 | bytes 36317440 | solution.py:72
  1149.0 18.5 %while.80 = (s32[]{:T(128)}, bf16[2,512,4,72]{1,3,2,0:T(8,128)(2,1)}, f32[2,4,512]{2,1,0:T(4,128)}, s32[2,512]{1,0:T(2,128)S(1)}, s32[1024]{0:T(1024)S(1)}, /*in...) while((s32[]{:T(128)}, ...), condition=%wide.region_19.19_spmd, body=%wide.region_16.18_spmd.sunk | while | flops 629815296 | bytes 36317440 | solution.py:72
  1171.8 79.4 %while.78 = (s32[]{:T(128)}, bf16[2,1024,4,72]{3,2,1,0:T(4,128)(2,1)}, bf16[2,1024,4,72]{1,3,2,0:T(8,128)(2,1)}, bf16[2,1024,4,72]{1,3,2,0:T(8,128)(2,1)}, bf16[...) while((s32[]{:T(128)}, ...), condition=%wide.region_25.26_spmd, body=%wide.region_21.25_spmd.sunk | while | flops 1543550976 | bytes 132897584 | solution.py:138
  1178.6 27.8 %while.81 = (s32[]{:T(128)}, f32[1024,4,72]{0,2,1:T(8,128)S(1)}, f32[1024,4,72]{0,2,1:T(8,128)}, bf16[2,512,4,72]{1,3,2,0:T(8,128)(2,1)}, bf16[2,512,4,72]{1,3,2...) while((s32[]{:T(128)}, f32[1024,4,72]{0,2,1:T(8,128)S(1)}, ...), condition=%wide.region_24.24_spmd.clone, body=%wide.region_22.23_spmd.clone.sunk | while | flops 1543550976 | bytes 87492888 | solution.py:116
  1218.1 27.8 %while.81 = (s32[]{:T(128)}, f32[1024,4,72]{0,2,1:T(8,128)S(1)}, f32[1024,4,72]{0,2,1:T(8,128)}, bf16[2,512,4,72]{1,3,2,0:T(8,128)(2,1)}, bf16[2,512,4,72]{1,3,2...) while((s32[]{:T(128)}, f32[1024,4,72]{0,2,1:T(8,128)S(1)}, ...), condition=%wide.region_24.24_spmd.clone, body=%wide.region_22.23_spmd.clone.sunk | while | flops 1543550976 | bytes 87492888 | solution.py:116
  1270.0 7.1 bitcast_convert_fusion
  1277.6 15.6 fusion.89
  1293.3 11.3 fusion.149
  1315.4 8.7 fusion.90
  1324.1 37.0 %reduce-scatter.12.cloned.1.call-done = bf16[512,1152]{1,0:T(8,128)(2,1)} async-done(((bf16[2048,1152]{1,0:T(8,128)(2,1)}), bf16[512,1152]{1,0:T(8,128)(2,1)}) %reduce-scatter.12.cloned.1.call-update) | async-done | bytes 1179664 | tf_op jit(solution)/shard_map/reduce_scatter | solution.py:38
  1378.7 22.1 %scatter_custom_fusion = f32[40,6912]{1,0:T(8,128)S(1)} fusion(s32[512]{0:T(512)} %param.31, f32[512,6912]{1,0:T(8,128)} %fusion.109, f32[]{:T(128)} %constant.153.clone.1), kind=kCustom, calls=%fused_computation.179 | custom fusion | flops 3538944 | bytes 1106432 | tf_op jit(solution)/shard_map/scatter-add | solution.py:267
  1400.8 53.7 %all-reduce.9 = bf16[40,6912]{1,0:T(8,128)(2,1)} all-reduce(f32[40,6912]{1,0:T(8,128)S(1)} %scatter_custom_fusion), channel_id=6, replica_groups=mesh['dp'=8,'mp'=4] {'dp','mp'}, use_global_device_ids=true, to_apply=%region_30.31.clone | all-reduce | flops 276480 | bytes 1658880
  1466.6 24.8 %all-reduce.3 = (f32[2,288]{1,0:T(2,128)}, f32[1152]{0:T(1024)}, f32[1152]{0:T(1024)}, f32[1152]{0:T(1024)}) all-reduce(f32[2,288]{1,0:T(2,128)S(1)} %pad_maximum_fusion, f32[1152]{0:T(1024)S(1)} %convert_reduce_fusion.2, f32[1152]{0:T(1024)S(1)} %copy-done.57, f32[1152]{0:T(1024)S(1)} %convert_reduce_fusion), channel_id=1, replica_groups=mesh['dp'=8,'mp'=4] {'dp'}, use_global_device_ids=true, to_apply=%region_37.38 | all-reduce | flops 4032 | bytes 32256 | tf_op jit(solution)/shard_map/psum | solution.py:282
  1492.8 176.2 %all-reduce.8.cloned.1.call-done = (f32[40,1152]{1,0:T(8,128)}, f32[3,1152,288]{1,2,0:T(8,128)}, f32[288,1152]{1,0:T(8,128)}, f32[1152,1152]{1,0:T(8,128)}, f32[1152,1152]{1,0:T(8,128)}) async-done(((f32[40,1152]{1,0:T(8,128)}, f32[3,1152,288]{1,2,0:T(8,128)}, f32[288,1152]{1,0:T(8,128)}, f32[1152,1152]{1,0:T(8,128)}, f32[1152,1152]{1,0:T(8,128)}), (f32[40,1152]{1,0:T(8,128)}, f32[3,1152,288]{1,2,0:T(8,128)}, ...) | async-done | bytes 16109584
  1669.9 19.4 %psum.63 = f32[5,1152]{1,0:T(8,128)S(1)} all-reduce(f32[5,1152]{1,0:T(8,128)S(1)} %constant_dynamic-slice_fusion.10), channel_id=1, replica_groups=mesh['dp'=8,'mp'=4] {'mp'}, use_global_device_ids=true, to_apply=%region_32.33 | all-reduce | flops 5760 | bytes 46080 | tf_op jit(solution)/shard_map/psum | solution.py:279
  (491 shorter events, 328.2 us)
Async XLA Ops:
  7.2 636.6 %copy-start = (bf16[1152,1152]{1,0:T(8,128)(2,1)S(1)}, bf16[1152,1152]{1,0:T(8,128)(2,1)}, u32[]{:S(2)}) copy-start(bf16[1152,1152]{1,0:T(8,128)(2,1)} %param.38) | copy-start | bytes 7962628
  7.2 58.7 %copy-start.58 = (s32[512]{0:T(512)S(1)}, s32[512]{0:T(512)}, u32[]{:S(2)}) copy-start(s32[512]{0:T(512)} %param.31) | copy-start | bytes 6148
  7.2 119.2 %all-gather.9.cloned.1.call-start = ((), (), s32[]{:S(2)}) async-start(), calls=%async_computation.4 | async-start | bytes 16422912 | tf_op jit(solution)/shard_map/all_gather | solution.py:177
  7.9 236.8 %all-gather.11.cloned.1.call-start = ((), (), s32[]{:S(2)}) async-start(), calls=%async_computation.5 | async-start | bytes 5898240 | tf_op jit(solution)/shard_map/all_gather | solution.py:34
  61.9 75.2 %copy-start.30 = (f32[40,1152]{1,0:T(8,128)}, f32[40,1152]{1,0:T(8,128)S(1)}, u32[]{:S(2)}) copy-start(f32[40,1152]{1,0:T(8,128)S(1)} %reshape.320) | copy-start | bytes 552964
  64.2 88.8 %copy-start.45 = (f32[512]{0:T(512)}, f32[512]{0:T(512)S(1)}, u32[]{:S(2)}) copy-start(f32[512]{0:T(512)S(1)} %broadcast_multiply_fusion.1) | copy-start | bytes 6148
  66.5 86.5 %copy-start.53 = (f32[512]{0:T(512)}, f32[512]{0:T(512)S(1)}, u32[]{:S(2)}) copy-start(f32[512]{0:T(512)S(1)} %fusion.120) | copy-start | bytes 6148
  143.9 9.2 copy-start.7
  157.0 296.7 %reduce-scatter.6.cloned.1.call-start = ((), (), s32[]{:S(2)}) async-start(), calls=%async_computation.6 | async-start | bytes 5898240 | tf_op jit(solution)/shard_map/reduce_scatter | solution.py:38
  157.5 95.1 %copy-start.60 = (f32[3,288]{1,0:T(4,128)}, f32[3,288]{1,0:T(4,128)S(1)}, u32[]{:S(2)}) copy-start(f32[3,288]{1,0:T(4,128)S(1)} %maximum_convert_fusion) | copy-start | bytes 10372
  357.5 7.9 copy-start.67
  369.9 184.0 %all-gather.15.cloned.1.call-start = ((), (), s32[]{:S(2)}) async-start(), calls=%async_computation.9 | async-start | bytes 5898240 | tf_op jit(solution)/shard_map/all_gather | solution.py:34
  370.6 86.1 %copy-start.41 = (f32[1152]{0:T(1024)}, f32[1152]{0:T(1024)S(1)}, u32[]{:S(2)}) copy-start(f32[1152]{0:T(1024)S(1)} %convert_element_type.165) | copy-start | bytes 13828
  456.6 7.2 copy-start.2
  456.7 452.3 %copy-start.39 = (f32[512]{0:T(512)}, f32[512]{0:T(512)S(1)}, u32[]{:S(2)}) copy-start(f32[512]{0:T(512)S(1)} %broadcast_multiply_fusion) | copy-start | bytes 6148
  457.0 6.7 copy-start.51
  458.8 450.2 %copy-start.47 = (f32[512]{0:T(512)}, f32[512]{0:T(512)S(1)}, u32[]{:S(2)}) copy-start(f32[512]{0:T(512)S(1)} %fusion.121) | copy-start | bytes 6148
  463.8 180.0 %all-gather.17.cloned.1.call-start = ((), (), s32[]{:S(2)}) async-start(), calls=%async_computation.10 | async-start | bytes 5898240 | tf_op jit(solution)/shard_map/all_gather | solution.py:34
  464.4 269.3 %all-gather.13.cloned.1.call-start = ((), (), s32[]{:S(2)}) async-start(), calls=%async_computation.7 | async-start | bytes 5898240 | tf_op jit(solution)/shard_map/all_gather | solution.py:34
  465.0 355.3 %reduce-scatter.10.cloned.1.call-start = ((), (), s32[]{:S(2)}) async-start(), calls=%async_computation.11 | async-start | bytes 5898240 | tf_op jit(solution)/shard_map/reduce_scatter | solution.py:38
  672.9 236.1 %reduce-scatter.8.cloned.1.call-start = ((), (), s32[]{:S(2)}) async-start(), calls=%async_computation.8 | async-start | bytes 5898240 | tf_op jit(solution)/shard_map/reduce_scatter | solution.py:38
  751.6 68.7 %copy-start.3 = (f32[512,1152]{1,0:T(8,128)S(1)}, f32[512,1152]{1,0:T(8,128)}, u32[]{:S(2)}) copy-start(f32[512,1152]{1,0:T(8,128)} %copy-done.2) | copy-start | bytes 7077892
  751.6 256.4 %all-gather.21.cloned.1.call-start = ((), (), s32[]{:S(2)}) async-start(), calls=%async_computation.13 | async-start | bytes 5898240 | tf_op jit(solution)/shard_map/all_gather | solution.py:34
  820.3 88.7 %copy-start.16 = (bf16[512,1152]{1,0:T(8,128)(2,1)S(1)}, bf16[512,1152]{1,0:T(8,128)(2,1)}, u32[]{:S(2)}) copy-start(bf16[512,1152]{1,0:T(8,128)(2,1)} %reduce-scatter.10.cloned.1.call-done) | copy-start | bytes 3538948
  909.0 5.7 copy-start.19
  917.9 90.1 %copy-start.68 = (bf16[288,1152]{1,0:T(8,128)(2,1)S(1)}, bf16[288,1152]{1,0:T(8,128)(2,1)}, u32[]{:S(2)}) copy-start(bf16[288,1152]{1,0:T(8,128)(2,1)} %param.36) | copy-start | bytes 1990660
  917.9 180.0 %all-gather.19.cloned.1.call-start = ((), (), s32[]{:S(2)}) async-start(), calls=%async_computation.12 | async-start | bytes 5898240 | tf_op jit(solution)/shard_map/all_gather | solution.py:34
  918.5 442.6 %reduce-scatter.12.cloned.1.call-start = ((), (), s32[]{:S(2)}) async-start(), calls=%async_computation.14 | async-start | bytes 5898240 | tf_op jit(solution)/shard_map/reduce_scatter | solution.py:38
  1012.0 85.8 %copy-start.61 = (f32[3,288]{1,0:T(4,128)S(1)}, f32[3,288]{1,0:T(4,128)}, u32[]{:S(2)}) copy-start(f32[3,288]{1,0:T(4,128)} %copy-done.60) | copy-start | bytes 10372
  1172.0 4.4 copy-start.5
  1211.5 4.4 copy-start.5
  1277.1 16.1 slice-start.4
  1277.2 391.8 %all-reduce.8.cloned.1.call-start = ((), (), s32[]{:S(2)}) async-start(), calls=%async_computation.15 | async-start | bytes 32219136
  1277.6 15.6 slice-start.5
  1310.1 5.3 copy-start.38
  1315.4 45.7 %copy-start.8 = (bf16[512,1152]{1,0:T(8,128)(2,1)S(1)}, bf16[512,1152]{1,0:T(8,128)(2,1)}, u32[]{:S(2)}) copy-start(bf16[512,1152]{1,0:T(8,128)(2,1)} %param.27) | copy-start | bytes 3538948
  1315.4 45.7 %copy-start.46 = (f32[512]{0:T(512)S(1)}, f32[512]{0:T(512)}, u32[]{:S(2)}) copy-start(f32[512]{0:T(512)} %copy-done.45) | copy-start | bytes 6148
  1324.1 41.2 %copy-start.50 = (f32[512]{0:T(512)S(1)}, f32[512]{0:T(512)}, u32[]{:S(2)}) copy-start(f32[512]{0:T(512)} %copy-done.49) | copy-start | bytes 6148
  1324.1 41.2 %copy-start.54 = (f32[512]{0:T(512)S(1)}, f32[512]{0:T(512)}, u32[]{:S(2)}) copy-start(f32[512]{0:T(512)} %copy-done.53) | copy-start | bytes 6148
  1365.3 4.4 copy-start.15
  1365.3 4.4 copy-start.20
  1365.3 4.4 copy-start.27
  1365.3 4.4 copy-start.42
  1463.5 27.9 %copy-start.31 = (f32[40,1152]{1,0:T(8,128)S(1)}, f32[40,1152]{1,0:T(8,128)}, u32[]{:S(2)}) copy-start(f32[40,1152]{1,0:T(8,128)} %copy-done.30) | copy-start | bytes 552964
  1463.5 225.8 %copy-start.44 = (bf16[5,1152]{1,0:T(8,128)(2,1)S(1)}, bf16[5,1152]{1,0:T(8,128)(2,1)}, u32[]{:S(2)}) copy-start(bf16[5,1152]{1,0:T(8,128)(2,1)} %param.29) | copy-start | bytes 34564
  1689.3 6.6 slice-start.2
  1690.0 4.8 copy-start.32
  1690.0 5.9 slice-start.3
  (76 other events, 161.7 us)
Sparse Core Ops, SparseCore 0:
  10.9 115.4 all-gather.8
  157.2 87.5 all-gather.10
  370.0 83.6 reduce-scatter.5
  463.9 89.9 all-gather.14
  555.9 87.8 all-gather.16
  645.8 87.8 all-gather.12
  736.6 83.6 reduce-scatter.9
  823.2 85.7 reduce-scatter.7
  918.0 89.9 all-gather.20
  1010.0 87.8 all-gather.18
  1277.3 83.7 reduce-scatter.11
  1458.0 210.8 all-reduce.7
where the time goes:
time: 1720 us; the launch traced here: 1710 us
  waiting for transfers between devices  999 us (58%)
  matrix products  254 us (15%)
  local copies, waits for them, and re-layouts  177 us (10%)
  blocking collectives  151 us (9%)
  other arithmetic  110 us (6%)
    all_gather x6, waiting for transfers between devices, gather_rows(): return lax.all_gather(values_in, 'mp', axis=0, tiled=True)  488 us
    reduce_scatter x4, waiting for transfers between devices, reduce_rows(): lax.psum_scatter(term_fn(jnp.int32(0), row_count * lax.axis_size('mp')).a...  273 us
    unnamed x13, waiting for transfers between devices  179 us
    unnamed x2, blocking collectives  96.7 us
    all_gather x1, waiting for transfers between devices, on_device(): lax.all_gather(w_ada, ('dp', 'mp'), axis=1, tiled=True)  59.9 us
    dot_general x8, matrix products, one_block(): jnp.einsum('hqk,khd->qhd', weights_low, values, preferred_element_type=jn...  35 us
  transfers between devices with their start and end apart: 12, of which 12 were waited for; matrix products, arithmetic and copies ran while one was open for 7% of the time, Pallas kernels for 0%

commit v1 on v0

v1 whole, which is shorter than its diff:
```python
import math

import jax
import jax.numpy as jnp
from jax import lax
from jax.experimental import pallas as pl
from jax.experimental.pallas import tpu as pltpu
from jax.sharding import PartitionSpec as P

HD = 72
HP = 80
L = 1024
BLOCK = 256
BF = jnp.bfloat16
F32 = jnp.float32
SCALE = HD**-0.5
SCALE2 = SCALE * math.log2(math.e)
MASKED = -1e30


def swap(value, axis, bit):
    n = lax.axis_size(axis)
    return lax.ppermute(value, axis, [(i, i ^ bit) for i in range(n)])


def dot(a, b, ca, cb):
    return lax.dot_general(
        a, b, (((ca,), (cb,)), ((), ())), preferred_element_type=F32
    )


def layer_norm(vector):
    centred = vector - jnp.mean(vector, axis=-1, keepdims=True)
    spread = jnp.mean(centred * centred, axis=-1, keepdims=True)
    rsig = lax.rsqrt(spread + 1e-06)
    return centred * rsig, rsig


def norm_back(grad_in, normed, rsig, scale):
    u = grad_in * (1.0 + scale)
    mean_u = jnp.mean(u, axis=-1, keepdims=True)
    mean_un = jnp.mean(u * normed, axis=-1, keepdims=True)
    return (u - mean_u - normed * mean_un) * rsig


def gelu_parts(u):
    a = math.sqrt(2.0 / math.pi)
    t = jnp.tanh(a * (u + 0.044715 * u * u * u))
    return 0.5 * u * (1.0 + t), 0.5 * (1.0 + t) + 0.5 * u * (1.0 - t * t) * (
        a * (1.0 + 3 * 0.044715 * u * u)
    )


def silu_fn(values_in):
    return values_in * jax.nn.sigmoid(values_in)


def head_window(h, width):
    start = h * HP
    base = jnp.minimum((start // 128) * 128, width - 256)
    return pl.multiple_of(base, 128), start - base


def attn_fwd_kernel(q_ref, k_ref, v_ref, ctx_ref, lse_ref, vt, ct):
    rows, width = q_ref.shape
    heads = width // HP
    qb = 256
    vt[...] = v_ref[...].T

    def head(h, carry):
        base, lo = head_window(h, width)
        lane = lax.broadcasted_iota(jnp.int32, (rows, 256), 1)
        here = (lane >= lo) & (lane < lo + HP)
        km = jnp.where(here, k_ref[:, pl.ds(base, 256)], jnp.zeros((), BF))
        vth = vt[pl.ds(pl.multiple_of(h * HP, 16), HP), :]
        for j in range(rows // qb):
            at = slice(j * qb, (j + 1) * qb)
            s = dot(km, q_ref[at, pl.ds(base, 256)], 1, 1)
            m = jnp.max(s, axis=0, keepdims=True) * SCALE2
            e = jnp.exp2(s * SCALE2 - m)
            total = jnp.sum(e, axis=0, keepdims=True)
            c = dot(vth, e.astype(BF), 1, 0)
            ct[pl.ds(pl.multiple_of(h * HP, 8), HP), at] = c / total
            lse_ref[h, :, at] = m + jnp.log2(total)
        return carry

    lax.fori_loop(0, heads, head, 0)
    ctx_ref[...] = ct[...].T.astype(BF)


def attn_fwd(q, k, v):
    rows, width = q.shape
    heads = width // HP
    return pl.pallas_call(
        attn_fwd_kernel,
        out_shape=(
            jax.ShapeDtypeStruct((rows, width), BF),
            jax.ShapeDtypeStruct((heads, 1, rows), F32),
        ),
        in_specs=[pl.BlockSpec(memory_space=pltpu.VMEM)] * 3,
        out_specs=[pl.BlockSpec(memory_space=pltpu.VMEM)] * 2,
        scratch_shapes=[
            pltpu.VMEM((width, rows), BF),
            pltpu.VMEM((width, rows), F32),
        ],
        compiler_params=pltpu.CompilerParams(vmem_limit_bytes=48 << 20),
        cost_estimate=pl.CostEstimate(
            flops=4 * rows * rows * 256 * heads,
            bytes_accessed=8 * rows * width,
            transcendentals=rows * rows * heads,
        ),
    )(q, k, v)


def attn_bwd_kernel(
    q_ref, k_ref, v_ref, g_ref, lse_ref, dq_ref, dk_ref, dv_ref, kt, dqt, dk_acc, dv_acc
):
    rows, width = q_ref.shape
    heads = width // HP
    qb = 512
    kt[...] = k_ref[...].T
    dk_acc[...] = jnp.zeros_like(dk_acc)
    dv_acc[...] = jnp.zeros_like(dv_acc)

    def head(h, carry):
        base, lo = head_window(h, width)
        win = pl.ds(base, 256)
        zero = jnp.zeros((), BF)
        lane = lax.broadcasted_iota(jnp.int32, (rows, 256), 1)
        here = (lane >= lo) & (lane < lo + HP)
        km = jnp.where(here, k_ref[:, win], zero)
        vm = jnp.where(here, v_ref[:, win], zero)
        kth = kt[pl.ds(pl.multiple_of(h * HP, 16), HP), :]
        row = lax.broadcasted_iota(jnp.int32, (HP, rows), 0)
        kth = jnp.where(row < HD, kth, zero)
        lane_b = lax.broadcasted_iota(jnp.int32, (qb, 256), 1)
        real = (lane_b >= lo) & (lane_b < lo + HD)
        for j in range(rows // qb):
            at = slice(j * qb, (j + 1) * qb)
            q_blk = q_ref[at, win]
            g_blk = g_ref[at, win]
            s = dot(km, q_blk, 1, 1)
            p = jnp.exp2(s * SCALE2 - lse_ref[h, :, at])
            dp = dot(vm, g_blk, 1, 1)
            delta = jnp.sum(p * dp, axis=0, keepdims=True)
            ds = (p * (dp - delta)).astype(BF)
            dv_acc[:, win] += dot(p.astype(BF), jnp.where(real, g_blk, zero), 1, 0)
            dk_acc[:, win] += dot(ds, jnp.where(real, q_blk, zero), 1, 0)
            dqt[pl.ds(pl.multiple_of(h * HP, 8), HP), at] = dot(kth, ds, 1, 0)
        return carry

    lax.fori_loop(0, heads, head, 0)
    dq_ref[...] = (dqt[...].T * SCALE).astype(BF)
    dk_ref[...] = (dk_acc[...] * SCALE).astype(BF)
    dv_ref[...] = dv_acc[...].astype(BF)


def attn_bwd(q, k, v, g, lse):
    rows, width = q.shape
    heads = width // HP
    shape = jax.ShapeDtypeStruct((rows, width), BF)
    return pl.pallas_call(
        attn_bwd_kernel,
        out_shape=(shape, shape, shape),
        in_specs=[pl.BlockSpec(memory_space=pltpu.VMEM)] * 5,
        out_specs=[pl.BlockSpec(memory_space=pltpu.VMEM)] * 3,
        scratch_shapes=[
            pltpu.VMEM((width, rows), BF),
            pltpu.VMEM((width, rows), F32),
            pltpu.VMEM((rows, width), F32),
            pltpu.VMEM((rows, width), F32),
        ],
        compiler_params=pltpu.CompilerParams(vmem_limit_bytes=56 << 20),
        cost_estimate=pl.CostEstimate(
            flops=10 * rows * rows * 256 * heads,
            bytes_accessed=14 * rows * width,
            transcendentals=rows * rows * heads,
        ),
    )(q, k, v, g, lse)


def pad_heads(rows_in):
    *lead, n, width = rows_in.shape
    split = rows_in.reshape(*lead, n // HD, HD, width)
    pads = [(0, 0)] * (len(lead) + 1) + [(0, HP - HD), (0, 0)]
    return jnp.pad(split, pads).reshape(*lead, n // HD * HP, width)


def drop_pads(rows_in):
    *lead, n, width = rows_in.shape
    split = rows_in.reshape(*lead, n // HP, HP, width)[..., :HD, :]
    return split.reshape(*lead, n // HP * HD, width)


def on_device(
    patches,
    cotangent,
    conditioning,
    segment,
    image_ids,
    w_ada,
    b_ada,
    w_qkv,
    b_qv,
    w_out,
    b_out,
    w_fc1,
    b_fc1,
    w_fc2,
    b_fc2,
):
    n_dp, n_mp = lax.axis_size("dp"), lax.axis_size("mp")
    n_all = n_dp * n_mp
    z = lax.axis_index("mp")
    d = lax.axis_index("dp")
    core = d & 1
    everyone = ("dp", "mp")
    tokens, width = patches.shape
    n_blocks = tokens // BLOCK
    shard = w_fc2.shape[0]
    hidden_n = shard * n_mp

    part = shard // n_dp
    w1t_own = w_fc1.T
    w1_all = lax.all_gather(
        lax.dynamic_slice_in_dim(w1t_own, d * part, part, 0), ("mp", "dp"), axis=0, tiled=True
    )
    w2_all = lax.all_gather(
        lax.dynamic_slice_in_dim(w_fc2, d * part, part, 0), ("mp", "dp"), axis=0, tiled=True
    )

    heads_shard = w_out.shape[0]
    watt_own = jnp.concatenate(
        [w_qkv.transpose(0, 2, 1), w_out[None]], axis=0
    )
    half = heads_shard // 2
    sent_half = lax.dynamic_slice_in_dim(watt_own, core * half, half, 1)
    got_half = swap(sent_half, "mp", 2)
    got_other = swap(got_half, "dp", 1)
    first = jnp.where(core == 0, got_half, got_other)
    second = jnp.where(core == 0, got_other, got_half)
    watt_other = jnp.concatenate([first, second], axis=1)
    bqv_other = swap(b_qv, "mp", 2)
    watt = jnp.concatenate([pad_heads(watt_own), pad_heads(watt_other)], axis=1)
    wide = watt.shape[1]
    wqkv_t = watt[:3].reshape(3 * wide, width)
    wout_p = watt[3]
    bqv2 = jnp.concatenate(
        [pad_heads(b_qv[..., None])[..., 0], pad_heads(bqv_other[..., None])[..., 0]],
        axis=1,
    ).astype(F32)

    cond_all = lax.all_gather(conditioning, "dp", axis=0, tiled=True)
    n_img = cond_all.shape[0]
    silu_cond = silu_fn(cond_all.astype(F32)).astype(BF)
    table_cols = (dot(silu_cond, w_ada, 1, 0) + b_ada.astype(F32)).astype(BF)
    cols = table_cols.shape[1]
    table = lax.all_to_all(
        jnp.broadcast_to(table_cols[None], (n_all, n_img, cols)), everyone, 0, 0
    )
    ids = image_ids.reshape(n_blocks, BLOCK)[:, 0]
    mods = jnp.stack(
        [
            lax.dynamic_slice(table, (0, ids[b], 0), (n_all, 1, cols)).reshape(6, width)
            for b in range(n_blocks)
        ]
    ).astype(F32)
    shift_attn, scale_attn, gate_attn, shift_mlp, scale_mlp, gate_mlp = [
        mods[:, i, None, :] for i in range(6)
    ]

    def blocks(v):
        return v.reshape(n_blocks, BLOCK, width)

    def flat(v):
        return v.reshape(tokens, width)

    patch_wide = blocks(patches.astype(F32))
    grad_output = blocks(cotangent.astype(F32))
    norm_a, rsig_a = layer_norm(patch_wide)
    attn_in = flat((norm_a * (1.0 + scale_attn) + shift_attn).astype(BF))
    x_row = jnp.concatenate([attn_in, swap(attn_in, "mp", 1)], axis=0)

    seg_own = lax.dynamic_slice_in_dim(segment, z * tokens, tokens, 0)
    seg_peer = lax.dynamic_slice_in_dim(segment, (z ^ 1) * tokens, tokens, 0)
    seg = jnp.concatenate([seg_own, seg_peer])[:, None]
    slot = lax.broadcasted_iota(jnp.int32, (1, wide), 1) % HP - HD
    mark_q = jnp.where(slot == seg, 1.0, 0.0)
    mark_k = jnp.where((slot >= 0) & (slot < 4) & (slot != seg), MASKED, 0.0)
    proj = dot(x_row, wqkv_t, 1, 1)
    q = (proj[:, :wide] + bqv2[0] + mark_q).astype(BF)
    k = (proj[:, wide : 2 * wide] + mark_k).astype(BF)
    v = (proj[:, 2 * wide :] + bqv2[1]).astype(BF)
    ctx, lse = attn_fwd(q, k, v)

    out_peer = swap(dot(ctx[tokens:], wout_p, 1, 0).astype(BF), "mp", 1)
    attn_out = blocks(
        dot(ctx[:tokens], wout_p, 1, 0) + out_peer.astype(F32) + b_out.astype(F32)
    )
    resid = patch_wide + gate_attn * attn_out
    norm_m, rsig_m = layer_norm(resid)
    mlp_in = flat((norm_m * (1.0 + scale_mlp) + shift_mlp).astype(BF))

    b1_all = lax.all_gather(b_fc1, "mp", axis=0, tiled=True).astype(F32)
    pre = dot(mlp_in, w1_all, 1, 1) + b1_all
    act, act_grad = gelu_parts(pre)
    hidden = act.astype(BF)
    mlp_out = blocks(dot(hidden, w2_all, 1, 0) + b_fc2.astype(F32))
    output = flat((resid + gate_mlp * mlp_out).astype(BF))
    g_gate_mlp = jnp.sum(grad_output * mlp_out, axis=1)
    gmo = flat((gate_mlp * grad_output).astype(BF))
    grad_w2 = dot(hidden, gmo, 0, 0).astype(BF)
    grad_b2 = jnp.sum(gmo, axis=0, dtype=F32)
    grad_pre = (dot(gmo, w2_all, 1, 1) * act_grad).astype(BF)
    grad_w1t = dot(grad_pre, mlp_in, 0, 0).astype(BF)
    grad_b1 = jnp.sum(grad_pre, axis=0, dtype=F32)
    red_w2 = lax.psum_scatter(grad_w2, ("mp", "dp"), scatter_dimension=0, tiled=True)
    red_w1 = lax.psum_scatter(grad_w1t, ("mp", "dp"), scatter_dimension=0, tiled=True)
    out_w2 = lax.all_gather(red_w2, "dp", axis=0, tiled=True)
    out_w1 = lax.all_gather(red_w1, "dp", axis=0, tiled=True)

    g_mlp_in = blocks(dot(grad_pre, w1_all, 1, 0))
    g_shift_mlp = jnp.sum(g_mlp_in, axis=1)
    g_scale_mlp = jnp.sum(g_mlp_in * norm_m, axis=1)
    grad_resid = grad_output + norm_back(g_mlp_in, norm_m, rsig_m, scale_mlp)
    g_gate_attn = jnp.sum(grad_resid * attn_out, axis=1)
    gao = flat((gate_attn * grad_resid).astype(BF))
    grad_bout = jnp.sum(gao, axis=0, dtype=F32)
    gao_row = jnp.concatenate([gao, swap(gao, "mp", 1)], axis=0)

    grad_ctx = dot(gao_row, wout_p, 1, 1).astype(BF)
    grad_wout = dot(ctx, gao_row, 0, 0)
    dq, dk, dv = attn_bwd(q, k, v, grad_ctx, lse)
    dqkv = jnp.concatenate([dq, dk, dv], axis=1)
    g_peer = swap(dot(dqkv[tokens:], wqkv_t, 1, 0).astype(BF), "mp", 1)
    g_attn_in = blocks(dot(dqkv[:tokens], wqkv_t, 1, 0) + g_peer.astype(F32))
    grad_wqkv = dot(dqkv, x_row, 0, 0)
    grad_att = drop_pads(
        jnp.concatenate([grad_wqkv, grad_wout], axis=0).astype(BF).reshape(4, 2, wide // 2, width)
    )
    grad_att = grad_att.transpose(1, 0, 2, 3).reshape(2, 4 * heads_shard, width)
    red_att = lax.psum_scatter(grad_att, "dp", scatter_dimension=1, tiled=True)
    red_own = red_att[0].astype(F32) + swap(red_att[1], "mp", 2).astype(F32)
    out_att = lax.all_gather(red_own.astype(BF), "dp", axis=0, tiled=True)
    out_att = out_att.reshape(4, heads_shard, width)

    g_shift_attn = jnp.sum(g_attn_in, axis=1)
    g_scale_attn = jnp.sum(g_attn_in * norm_a, axis=1)
    grad_patches = flat(grad_resid + norm_back(g_attn_in, norm_a, rsig_a, scale_attn))
    sums = jnp.concatenate(
        [g_shift_attn, g_scale_attn, g_gate_attn, g_shift_mlp, g_scale_mlp, g_gate_mlp],
        axis=1,
    )
    to_owner = sums.reshape(n_blocks, n_all, cols).transpose(1, 0, 2)
    with_ids = jnp.concatenate(
        [to_owner, jnp.broadcast_to(ids.astype(F32)[None, :, None], (n_all, n_blocks, 1))],
        axis=2,
    )
    got = lax.all_to_all(with_ids, everyone, 0, 0).reshape(n_all * n_blocks, cols + 1)
    belongs = (
        got[:, cols].astype(jnp.int32)[None, :]
        == lax.broadcasted_iota(jnp.int32, (n_img, 1), 0)
    ).astype(F32)
    grad_cols = lax.dot_general(
        belongs,
        got[:, :cols],
        (((1,), (0,)), ((), ())),
        precision=lax.Precision.HIGHEST,
        preferred_element_type=F32,
    ).astype(BF)
    grad_w_ada = dot(silu_cond, grad_cols, 0, 0)
    grad_b_ada = jnp.sum(grad_cols, axis=0, dtype=F32)
    silu_part = dot(grad_cols, w_ada, 1, 1)

    bq = jnp.sum(dq, axis=0, dtype=F32)
    bv = jnp.sum(dv, axis=0, dtype=F32)
    bqv_g = drop_pads(jnp.stack([bq, bv]).reshape(2, 2, wide // 2)[..., None])[..., 0]
    bqv_g = bqv_g.transpose(1, 0, 2)
    shards = jnp.arange(n_mp)[:, None, None]
    bqv_all = jnp.where(shards == z, bqv_g[0][None], 0.0) + jnp.where(
        shards == (z ^ 2), bqv_g[1][None], 0.0
    )
    images_here = n_img // n_dp
    payload = jnp.concatenate(
        [
            jnp.broadcast_to(
                silu_part.reshape(n_dp, 1, images_here * width),
                (n_dp, n_mp, images_here * width),
            ),
            jnp.broadcast_to(
                jnp.concatenate([grad_bout, grad_b2])[None, None], (n_dp, n_mp, 2 * width)
            ),
            jnp.broadcast_to(grad_b1.reshape(1, n_mp, shard), (n_dp, n_mp, shard)),
            jnp.broadcast_to(
                bqv_all.reshape(1, n_mp, 2 * heads_shard), (n_dp, n_mp, 2 * heads_shard)
            ),
        ],
        axis=2,
    ).reshape(n_all, -1)
    summed = jnp.sum(lax.all_to_all(payload, everyone, 0, 0), axis=0)
    at = images_here * width
    grad_silu = summed[:at].reshape(images_here, width)
    _, silu_back = jax.vjp(silu_fn, conditioning.astype(F32))
    grad_cond = silu_back(grad_silu)[0]
    out_bout = summed[at : at + width]
    out_b2 = summed[at + width : at + 2 * width]
    at += 2 * width
    out_b1 = summed[at : at + shard]
    out_bqv = summed[at + shard :].reshape(2, heads_shard)

    return (
        output,
        grad_patches,
        grad_cond,
        grad_w_ada,
        grad_b_ada,
        out_att[:3].transpose(0, 2, 1).astype(F32),
        out_bqv,
        out_att[3].astype(F32),
        out_bout,
        out_w1.T.astype(F32),
        out_b1,
        out_w2.astype(F32),
        out_b2,
    )


def solution(mesh):
    rows = P(("dp", "mp"), None)
    in_specs = (
        rows,
        rows,
        P("dp", None),
        P("dp"),
        P(("dp", "mp")),
        P(None, ("dp", "mp")),
        P(("dp", "mp")),
        P(None, None, "mp"),
        P(None, "mp"),
        P("mp", None),
        P(),
        P(None, "mp"),
        P("mp"),
        P("mp", None),
        P(),
    )
    out_specs = (
        rows,
        rows,
        P("dp", None),
        P(None, ("dp", "mp")),
        P(("dp", "mp")),
        P(None, None, "mp"),
        P(None, "mp"),
        P("mp", None),
        P(),
        P(None, "mp"),
        P("mp"),
        P("mp", None),
        P(),
    )
    return jax.shard_map(
        on_device, mesh=mesh, in_specs=in_specs, out_specs=out_specs, check_vma=False
    )
```

time: 1720 us -> 875 us (0.51)
  waiting for transfers between devices: 999 us -> 491 us
  local copies, waits for them, and re-layouts: 177 us -> 38.7 us
  matrix products: 254 us -> 123 us
  blocking collectives: 151 us -> 74.1 us
  other arithmetic: 110 us -> 43.9 us
  Pallas kernels: 0 us -> 55.2 us
  starting transfers between devices: 1.1 us -> 24.1 us
    all_gather x7 -> x5, waiting for transfers between devices: 547 us -> 70.7 us  [the longest x1 27.1 us: on_device(): out_w1 = lax.all_gather(red_w1, 'dp', axis=0, tiled=True)]
    unnamed x13 -> x8, waiting for transfers between devices: 179 us -> 0.13 us
    ppermute x0 -> x8, waiting for transfers between devices: none -> 173 us  [swap(): return lax.ppermute(value, axis, [(i, i ^ bit) for i in range(n)])]
    dot_general x48 -> x18, matrix products: 224 us -> 123 us  [the longest x17 122 us: dot(): lax.dot_general(a, b, (((ca,), (cb,)), ((), ())), preferred_element_type=...]
    unnamed x2 -> x0, blocking collectives: 96.7 us -> none
    all_gather x0 -> x1, blocking collectives: none -> 64.9 us  [on_device(): b1_all = lax.all_gather(b_fc1, 'mp', axis=0, tiled=True).astype(F32)]
    pallas_call x0 -> x2, Pallas kernels: none -> 55.2 us  [the longest x1 33.2 us: attn_bwd(): pl.pallas_call(attn_bwd_kernel, out_shape=(shape, shape, shape), in_specs...]
    while x127 -> x0, local copies, waits for them, and re-layouts: 47.1 us -> none  [the longest x7 23.6 us: attention_forward(): lax.map(attend_forward, (shaped[0], shaped[1], shaped[2], segment.reshape...]
  transfers between devices with their start and end apart: 12 -> 19, of which waited for: 12 -> 12; matrix products, arithmetic and copies ran while one was open for 7% -> 14% of each run, Pallas kernels for 0% -> 3%
where the time goes in v1:
time: 875 us; the launch traced here: 870 us
  waiting for transfers between devices  491 us (56%)
  matrix products  123 us (14%)
  blocking collectives  74.1 us (8%)
  Pallas kernels  55.2 us (6%)
  other arithmetic  43.9 us (5%)
  local copies, waits for them, and re-layouts  38.7 us (4%)
  starting transfers between devices  24.1 us (3%)
  between operations  19.5 us (2%)
    ppermute x8, waiting for transfers between devices, swap(): return lax.ppermute(value, axis, [(i, i ^ bit) for i in range(n)])  173 us
    reduce_scatter x1, waiting for transfers between devices, on_device(): lax.psum_scatter(grad_w2, ('mp', 'dp'), scatter_dimension=0, tiled=True)  127 us
    dot_general x17, matrix products, dot(): lax.dot_general(a, b, (((ca,), (cb,)), ((), ())), preferred_element_type=...  122 us
    reduce_scatter x1, waiting for transfers between devices, on_device(): lax.psum_scatter(grad_w1t, ('mp', 'dp'), scatter_dimension=0, tiled=True)  83 us
    all_gather x1, blocking collectives, on_device(): b1_all = lax.all_gather(b_fc1, 'mp', axis=0, tiled=True).astype(F32)  64.9 us
    pallas_call x1, Pallas kernels, attn_bwd(): pl.pallas_call(attn_bwd_kernel, out_shape=(shape, shape, shape), in_specs...  33.2 us
    reduce_scatter x1, waiting for transfers between devices, on_device(): red_att = lax.psum_scatter(grad_att, 'dp', scatter_dimension=1, tiled=True)  30.2 us
    all_gather x1, waiting for transfers between devices, on_device(): out_w1 = lax.all_gather(red_w1, 'dp', axis=0, tiled=True)  27.1 us
  transfers between devices with their start and end apart: 19, of which 12 were waited for; matrix products, arithmetic and copies ran while one was open for 14% of the time, Pallas kernels for 3%

profile of v1, /device:TPU:0, one launch (start us, length us, event | category | flops | bytes accessed | tf_op | source)
XLA Modules:
  0.0 870.0 jit_solution(11551897242109274070)
XLA Ops:
  15.2 4.1 collective-permute-start.1
  19.3 9.3 %all-gather = bf16[8,5,1152]{2,1,0:T(8,128)(2,1)S(1)} all-gather(bf16[1,5,1152]{2,1,0:T(8,128)(2,1)S(1)} %bitcast.181), channel_id=1, replica_groups=mesh['dp'=8,'mp'=4] {'dp'}, dimensions={0}, use_global_device_ids=true | all-gather | bytes 103680 | tf_op jit(solution)/shard_map/all_gather | solution.py:253
  30.9 3.3 all-to-all-start
  34.3 2.7 collective-permute-start.3
  38.4 67.9 %collective-permute-done.1 = bf16[4,144,1152]{2,1,0:T(8,128)(2,1)S(1)} collective-permute-done((bf16[4,144,1152]{2,1,0:T(8,128)(2,1)}, bf16[4,144,1152]{2,1,0:T(8,128)(2,1)S(1)}, u32[]{:S(2)}, u32[]{:S(2)}) %collective-permute-start.1) | collective-permute-done | bytes 1327136 | tf_op jit(solution)/shard_map/ppermute | solution.py:23
  106.3 3.4 fusion.11
  116.4 2.5 collective-permute-start
  122.7 3.3 fusion.10
  126.0 40.7 %collective-permute-done = bf16[512,1152]{1,0:T(8,128)(2,1)S(1)} collective-permute-done((bf16[512,1152]{1,0:T(8,128)(2,1)S(1)}, bf16[512,1152]{1,0:T(8,128)(2,1)S(1)}, u32[]{:S(2)}, u32[]{:S(2)}) %collective-permute-start) | collective-permute-done | bytes 1179680 | tf_op jit(solution)/shard_map/ppermute | solution.py:23
  166.7 5.5 fusion.34
  173.8 22.0 %shard_map.246 = (bf16[1024,640]{1,0:T(8,128)(2,1)S(1)}, f32[8,1,1024]{2,1,0:T(1,128)S(1)}) custom-call(bf16[1024,640]{1,0:T(8,128)(2,1)S(1)} %get-tuple-element.101.q_ref, bf16[1024,640]{1,0:T(8,128)(2,1)S(1)} %get-tuple-element.100.k_ref, bf16[1024,640]{1,0:T(8,128)(2,1)S(1)} %get-tuple-element.102.v_ref), custom_call_target="tpu_custom_call" | custom-call | flops 8589934592 | bytes 5242880 | tf_op jit(solution)/shard_map/pallas_call | solution.py:94
  196.9 2.2 convolution_convert_fusion.5
  199.6 64.9 %all-gather.1 = bf16[4,1,1152]{2,1,0:T(2,128)(2,1)S(1)} all-gather(bf16[1,1,1152]{2,1,0:T(2,128)(2,1)S(1)} %reshape.396), channel_id=1, replica_groups=mesh['dp'=8,'mp'=4] {'mp'}, dimensions={0}, use_global_device_ids=true | all-gather | bytes 11520 | tf_op jit(solution)/shard_map/all_gather | solution.py:304
  264.6 2.6 convert_reduce_fusion.3
  267.2 4.3 fusion.65
  274.6 11.6 %fusion.70 = f32[512,4608]{1,0:T(8,128)} fusion(bf16[512,1152]{1,0:T(8,128)(2,1)} %fusion.24, bf16[4608,1152]{1,0:T(8,128)(2,1)} %all-gather.8.cloned.1.call-done), kind=kOutput, calls=%fused_computation.186 | convolution fusion | flops 5435817984 | bytes 21233664 | tf_op jit(solution)/shard_map/dot_general | solution.py:27
  286.2 16.6 %convert_reduce_fusion = (f32[4608]{0:T(1024)S(1)}, bf16[512,4608]{1,0:T(8,128)(2,1)}) fusion(f32[512,4608]{1,0:T(8,128)} %fusion.70, f32[4608]{0:T(1024)S(1)} %reshape.399, bf16[512,1152]{1,0:T(8,128)(2,1)} %get-tuple-element.97, bf16[4608,1152]{1,0:T(8,128)(2,1)} %all-gather.10.cloned.1.call-done), kind=kOutput, calls=%fused_computation.12 | convolution fusion | flops 5487717888 | bytes 25989120 | tf_op jit(solution)/shard_map/dot_general | solution.py:27
  302.8 12.5 %fusion.28 = (f32[512]{0:T(512)S(1)}, f32[512]{0:T(512)S(1)}, f32[512,1152]{1,0:T(8,128)}) fusion(f32[2,1152]{1,0:T(2,128)S(1)} %bitcast.176, f32[512]{0:T(512)S(1)} %add_rsqrt_fusion, f32[512,1152]{1,0:T(8,128)S(1)} %copy-done.11, f32[512]{0:T(512)S(1)} %broadcast_multiply_fusion.4, bf16[512,4608]{1,0:T(8,128)(2,1)} %get-tuple-element.124, ...), kind=kOutput, calls=%fused_computation.83 | convolution fusion | flops 5439355904 | bytes 20071424 | tf_op jit(solution)/shard_map/dot_general | solution.py:27
  315.4 14.7 %convert_reduce_fusion.4 = (f32[1152]{0:T(1024)S(1)}, bf16[512,1152]{1,0:T(8,128)(2,1)}, f32[512,1152]{1,0:T(8,128)}, bf16[512,1152]{1,0:T(8,128)(2,1)}, f32[512,1152]{1,0:T(8,128)}) fusion(f32[2,1152]{1,0:T(2,128)S(1)} %get-tuple-element.128, f32[512]{0:T(512)S(1)} %broadcast_multiply_fusion.2, f32[512]{0:T(512)S(1)} %add_rsqrt_fusion, ...), kind=kOutput, calls=%fused_computation.67 | convolution fusion | flops 5469436928 | bytes 33093632 | tf_op jit(solution)/shard_map/dot_general | solution.py:27
  331.2 24.7 %collective-permute-done.5 = bf16[512,1152]{1,0:T(8,128)(2,1)S(1)} collective-permute-done((bf16[512,1152]{1,0:T(8,128)(2,1)}, bf16[512,1152]{1,0:T(8,128)(2,1)S(1)}, u32[]{:S(2)}, u32[]{:S(2)}) %collective-permute-start.5) | collective-permute-done | bytes 1179680 | tf_op jit(solution)/shard_map/ppermute | solution.py:23
  355.9 4.5 convolution_convert_fusion.6.g_ref
  360.4 33.2 %shard_map.247 = (bf16[1024,640]{1,0:T(8,128)(2,1)}, bf16[1024,640]{1,0:T(8,128)(2,1)}, bf16[1024,640]{1,0:T(8,128)(2,1)}) custom-call(bf16[1024,640]{1,0:T(8,128)(2,1)} %copy-done.3, bf16[1024,640]{1,0:T(8,128)(2,1)} %copy-done.2, bf16[1024,640]{1,0:T(8,128)(2,1)} %copy-done.4, bf16[1024,640]{1,0:T(8,128)(2,1)} %convolution_convert_fusion.6.g_ref, ...), custom_call_target="tpu_custom_call" | custom-call | flops 21474836480 | bytes 9175040 | tf_op jit(solution)/shard_map/pallas_call | solution.py:162
  396.7 3.0 convolution_convert_fusion.3
  400.1 5.8 convolution_convert_fusion.2
  406.8 2.8 copy.38
  410.9 12.1 %convolution_convert_fusion.1 = bf16[4608,1152]{1,0:T(8,128)(2,1)} fusion(bf16[512,4608]{1,0:T(8,128)(2,1)} %get-tuple-element.124, bf16[512,1152]{1,0:T(8,128)(2,1)S(1)} %copy-done.33), kind=kOutput, calls=%fused_computation.1 | convolution fusion | flops 5441126400 | bytes 16515072 | tf_op jit(solution)/shard_map/dot_general | solution.py:27
  424.5 13.0 %convolution_convert_fusion = bf16[4608,1152]{1,0:T(8,128)(2,1)} fusion(bf16[512,1152]{1,0:T(8,128)(2,1)S(1)} %copy-done.30, f32[512,4608]{1,0:T(8,128)} %fusion.70, f32[4608]{0:T(1024)S(1)} %reshape.399), kind=kOutput, calls=%fused_computation | convolution fusion | flops 5464719360 | bytes 21252096 | tf_op jit(solution)/shard_map/dot_general | solution.py:27
  437.6 30.2 %reduce-scatter.4.cloned.1.call-done = bf16[2,144,1152]{2,1,0:T(8,128)(2,1)} async-done(((bf16[2,1152,1152]{2,1,0:T(8,128)(2,1)}), bf16[2,144,1152]{2,1,0:T(8,128)(2,1)}) %reduce-scatter.4.cloned.1.call-update) | async-done | bytes 663568 | tf_op jit(solution)/shard_map/reduce_scatter | solution.py:342
  468.8 2.5 collective-permute-start.7
  471.3 15.1 %collective-permute-done.7 = bf16[144,1152]{1,0:T(8,128)(2,1)S(1)} collective-permute-done((bf16[144,1152]{1,0:T(8,128)(2,1)S(1)}, bf16[144,1152]{1,0:T(8,128)(2,1)S(1)}, u32[]{:S(2)}, u32[]{:S(2)}) %collective-permute-start.7) | collective-permute-done | bytes 331808 | tf_op jit(solution)/shard_map/ppermute | solution.py:23
  488.3 7.1 convolution_convert_fusion.4
  498.6 24.2 %collective-permute-done.6 = bf16[512,1152]{1,0:T(8,128)(2,1)} collective-permute-done((bf16[512,1152]{1,0:T(8,128)(2,1)}, bf16[512,1152]{1,0:T(8,128)(2,1)}, u32[]{:S(2)}, u32[]{:S(2)}) %collective-permute-start.6) | collective-permute-done | bytes 1179680 | tf_op jit(solution)/shard_map/ppermute | solution.py:23
  522.7 6.3 fusion.27
  529.1 3.1 fusion.26
  532.3 83.0 %reduce-scatter.6.cloned.1.call-done = bf16[144,1152]{1,0:T(8,128)(2,1)} async-done(((bf16[4608,1152]{1,0:T(8,128)(2,1)}), bf16[144,1152]{1,0:T(8,128)(2,1)}) %reduce-scatter.6.cloned.1.call-update) | async-done | bytes 331792 | tf_op jit(solution)/shard_map/reduce_scatter | solution.py:318
  616.4 4.0 all-to-all-start.1
  620.5 7.4 all-to-all-done.1
  629.6 2.5 all_to_all.14
  632.1 2.7 all-to-all-start.2
  634.8 127.4 %reduce-scatter.8.cloned.1.call-done = bf16[144,1152]{1,0:T(8,128)(2,1)} async-done(((bf16[4608,1152]{1,0:T(8,128)(2,1)}), bf16[144,1152]{1,0:T(8,128)(2,1)}) %reduce-scatter.8.cloned.1.call-update) | async-done | bytes 331792 | tf_op jit(solution)/shard_map/reduce_scatter | solution.py:317
  762.2 4.6 multiply_add_fusion.1
  770.8 23.0 %all-gather.12.cloned.1.call-done = bf16[1152,1152]{1,0:T(8,128)(2,1)} async-done(((bf16[144,1152]{1,0:T(8,128)(2,1)}), bf16[1152,1152]{1,0:T(8,128)(2,1)}) %all-gather.12.cloned.1.call-update) | async-done | bytes 2654224 | tf_op jit(solution)/shard_map/all_gather | solution.py:344
  796.7 2.2 convert_bitcast_fusion.1
  798.9 27.1 %all-gather.14.cloned.1.call-done = bf16[1152,1152]{1,0:T(8,128)(2,1)} async-done(((bf16[144,1152]{1,0:T(8,128)(2,1)}), bf16[1152,1152]{1,0:T(8,128)(2,1)}) %all-gather.14.cloned.1.call-update) | async-done | bytes 2654224 | tf_op jit(solution)/shard_map/all_gather | solution.py:320
  826.0 4.5 convert_bitcast_fusion
  830.5 7.1 copy.39
  837.5 20.6 %all-gather.16.cloned.1.call-done = bf16[1152,1152]{1,0:T(8,128)(2,1)} async-done(((bf16[144,1152]{1,0:T(8,128)(2,1)}), bf16[1152,1152]{1,0:T(8,128)(2,1)}) %all-gather.16.cloned.1.call-update) | async-done | bytes 2654224 | tf_op jit(solution)/shard_map/all_gather | solution.py:319
  858.2 4.5 convert_element_type.229
  (260 shorter events, 48.1 us)
Async XLA Ops:
  7.2 267.4 %all-gather.8.cloned.1.call-start = ((), (), s32[]{:S(2)}) async-start(), calls=%async_computation.6 | async-start | bytes 10948608 | tf_op jit(solution)/shard_map/all_gather | solution.py:225
  12.2 274.0 %all-gather.10.cloned.1.call-start = ((), (), s32[]{:S(2)}) async-start(), calls=%async_computation.7 | async-start | bytes 10948608 | tf_op jit(solution)/shard_map/all_gather | solution.py:228
  14.0 14.6 %copy-start.56 = (bf16[216]{0:T(256)(128)(2,1)S(1)}, bf16[216]{0:T(256)(128)(2,1)}, u32[]{:S(2)}) copy-start(bf16[216]{0:T(256)(128)(2,1)} %param.21) | copy-start | bytes 1300
  15.2 19.1 %copy-start.53 = (bf16[2,288]{1,0:T(2,128)(2,1)S(1)}, bf16[2,288]{1,0:T(2,128)(2,1)}, u32[]{:S(2)}) copy-start(bf16[2,288]{1,0:T(2,128)(2,1)} %param.23) | copy-start | bytes 3460
  15.2 21.8 %copy-start.52 = (s32[512]{0:T(512)S(1)}, s32[512]{0:T(512)}, u32[]{:S(2)}) copy-start(s32[512]{0:T(512)} %param.19) | copy-start | bytes 6148
  15.2 21.8 %copy-start.51 = (s32[2048]{0:T(1024)S(1)}, s32[2048]{0:T(1024)}, u32[]{:S(2)}) copy-start(s32[2048]{0:T(1024)} %param.18) | copy-start | bytes 24580
  15.2 22.4 %copy-start.8 = (bf16[512,1152]{1,0:T(8,128)(2,1)S(1)}, bf16[512,1152]{1,0:T(8,128)(2,1)}, u32[]{:S(2)}) copy-start(bf16[512,1152]{1,0:T(8,128)(2,1)} %param.15) | copy-start | bytes 3538948
  15.2 91.1 %collective-permute-start.1 = (bf16[4,144,1152]{2,1,0:T(8,128)(2,1)}, bf16[4,144,1152]{2,1,0:T(8,128)(2,1)S(1)}, u32[]{:S(2)}, u32[]{:S(2)}) collective-permute-start(bf16[4,144,1152]{2,1,0:T(8,128)(2,1)} %fusion.36), channel_id=1, source_target_pairs={{0,2},{1,3},{2,0},{3,1},{4,6},{5,7},{6,4},{7,5},{8,10},{9,11},{10,... | collective-permute-start | bytes 3981320 | tf_op jit(solution)/shard_map/ppermute | solution.py:23
  30.9 83.2 %all-to-all-start = ((bf16[32,40,216]{2,1,0:T(8,128)(2,1)}), bf16[32,40,216]{2,1,0:T(8,128)(2,1)}, u32[]{:S(2)}, u32[]{:S(2)}) async-start(bf16[32,40,216]{2,1,0:T(8,128)(2,1)} %broadcast_in_dim.102), calls=%async_computation | async-start | bytes 1310720 | tf_op jit(solution)/shard_map/all_to_all | solution.py:258
  34.3 433.5 %reduce-scatter.4.cloned.1.call-start = ((), (), s32[]{:S(2)}) async-start(), calls=%async_computation.8 | async-start | bytes 5971968 | tf_op jit(solution)/shard_map/reduce_scatter | solution.py:342
  34.3 79.5 %collective-permute-start.3 = (bf16[2,288]{1,0:T(2,128)(2,1)S(1)}, bf16[2,288]{1,0:T(2,128)(2,1)S(1)}, u32[]{:S(2)}, u32[]{:S(2)}) collective-permute-start(bf16[2,288]{1,0:T(2,128)(2,1)S(1)} %copy-done.53), channel_id=1, source_target_pairs={{0,2},{1,3},{2,0},{3,1},{4,6},{5,7},{6,4},{7,5},{8,10},{9,11},{10,... | collective-permute-start | bytes 3464 | tf_op jit(solution)/shard_map/ppermute | solution.py:23
  37.0 72.7 %copy-start.46 = (s32[2,256]{1,0:T(2,128)}, s32[2,256]{1,0:T(2,128)S(1)}, u32[]{:S(2)}) copy-start(s32[2,256]{1,0:T(2,128)S(1)} %reshape.375) | copy-start | bytes 6148
  37.9 77.8 %copy-start.42 = (f32[512]{0:T(512)}, f32[512]{0:T(512)S(1)}, u32[]{:S(2)}) copy-start(f32[512]{0:T(512)S(1)} %broadcast_multiply_fusion.5) | copy-start | bytes 6148
  38.4 77.3 %copy-start.44 = (f32[512]{0:T(512)}, f32[512]{0:T(512)S(1)}, u32[]{:S(2)}) copy-start(f32[512]{0:T(512)S(1)} %add_rsqrt_fusion.1) | copy-start | bytes 6148
  106.3 12.6 %collective-permute-start.2 = (bf16[4,144,1152]{2,1,0:T(8,128)(2,1)S(1)}, bf16[4,144,1152]{2,1,0:T(8,128)(2,1)}, u32[]{:S(2)}, u32[]{:S(2)}) collective-permute-start(bf16[4,144,1152]{2,1,0:T(8,128)(2,1)S(1)} %collective-permute-done.1), channel_id=1, source_target_pairs={{0,4},{4,0},{8,12},{12,8},{16,20},{20,16},{24,28},{28,24},{1,5},{5... | collective-permute-start | bytes 3981320 | tf_op jit(solution)/shard_map/ppermute | solution.py:23
  116.4 50.3 %copy-start.31 = (bf16[512,1152]{1,0:T(8,128)(2,1)}, bf16[512,1152]{1,0:T(8,128)(2,1)S(1)}, u32[]{:S(2)}) copy-start(bf16[512,1152]{1,0:T(8,128)(2,1)S(1)} %fusion.19) | copy-start | bytes 3538948
  116.4 50.3 %collective-permute-start = (bf16[512,1152]{1,0:T(8,128)(2,1)S(1)}, bf16[512,1152]{1,0:T(8,128)(2,1)S(1)}, u32[]{:S(2)}, u32[]{:S(2)}) collective-permute-start(bf16[512,1152]{1,0:T(8,128)(2,1)S(1)} %fusion.19), channel_id=1, source_target_pairs={{0,1},{1,0},{2,3},{3,2},{4,5},{5,4},{6,7},{7,6},{8,9},{9,8},{10,11... | collective-permute-start | bytes 3538952 | tf_op jit(solution)/shard_map/ppermute | solution.py:23
  122.6 73.3 %copy-start.22 = (bf16[640,1152]{1,0:T(8,128)(2,1)}, bf16[640,1152]{1,0:T(8,128)(2,1)S(1)}, u32[]{:S(2)}) copy-start(bf16[640,1152]{1,0:T(8,128)(2,1)S(1)} %fusion.35) | copy-start | bytes 4423684
  126.0 46.2 %copy-start.14 = (bf16[3,640,1152]{2,1,0:T(8,128)(2,1)}, bf16[3,640,1152]{2,1,0:T(8,128)(2,1)S(1)}, u32[]{:S(2)}) copy-start(bf16[3,640,1152]{2,1,0:T(8,128)(2,1)S(1)} %fusion.10) | copy-start | bytes 13271044
  173.8 22.1 %copy-start.2 = (bf16[1024,640]{1,0:T(8,128)(2,1)}, bf16[1024,640]{1,0:T(8,128)(2,1)S(1)}, u32[]{:S(2)}) copy-start(bf16[1024,640]{1,0:T(8,128)(2,1)S(1)} %get-tuple-element.100.k_ref) | copy-start | bytes 3932164
  173.8 22.1 %copy-start.3 = (bf16[1024,640]{1,0:T(8,128)(2,1)}, bf16[1024,640]{1,0:T(8,128)(2,1)S(1)}, u32[]{:S(2)}) copy-start(bf16[1024,640]{1,0:T(8,128)(2,1)S(1)} %get-tuple-element.101.q_ref) | copy-start | bytes 3932164
  173.8 22.1 %copy-start.4 = (bf16[1024,640]{1,0:T(8,128)(2,1)}, bf16[1024,640]{1,0:T(8,128)(2,1)S(1)}, u32[]{:S(2)}) copy-start(bf16[1024,640]{1,0:T(8,128)(2,1)S(1)} %get-tuple-element.102.v_ref) | copy-start | bytes 3932164
  195.9 68.6 %copy-start.49 = (bf16[1152]{0:T(1024)(128)(2,1)S(1)}, bf16[1152]{0:T(1024)(128)(2,1)}, u32[]{:S(2)}) copy-start(bf16[1152]{0:T(1024)(128)(2,1)} %param.29) | copy-start | bytes 6916
  199.1 68.1 %copy-start.6 = (bf16[1024,640]{1,0:T(8,128)(2,1)S(1)}, bf16[1024,640]{1,0:T(8,128)(2,1)}, u32[]{:S(2)}) copy-start(bf16[1024,640]{1,0:T(8,128)(2,1)} %copy-done.5) | copy-start | bytes 3932164
  199.1 68.1 %copy-start.9 = (bf16[512,1152]{1,0:T(8,128)(2,1)S(1)}, bf16[512,1152]{1,0:T(8,128)(2,1)}, u32[]{:S(2)}) copy-start(bf16[512,1152]{1,0:T(8,128)(2,1)} %param.15) | copy-start | bytes 3538948
  199.1 68.1 %collective-permute-start.4 = (bf16[512,1152]{1,0:T(8,128)(2,1)}, bf16[512,1152]{1,0:T(8,128)(2,1)}, u32[]{:S(2)}, u32[]{:S(2)}) collective-permute-start(bf16[512,1152]{1,0:T(8,128)(2,1)} %convolution_convert_fusion.5), channel_id=1, source_target_pairs={{0,1},{1,0},{2,3},{3,2},{4,5},{5,4},{6,7},{7,6},{8,9},{9,8},{10,11... | collective-permute-start | bytes 3538952 | tf_op jit(solution)/shard_map/ppermute | solution.py:23
  286.2 16.6 %copy-start.11 = (f32[512,1152]{1,0:T(8,128)S(1)}, f32[512,1152]{1,0:T(8,128)}, u32[]{:S(2)}) copy-start(f32[512,1152]{1,0:T(8,128)} %copy-done.10) | copy-start | bytes 7077892
  302.8 12.6 %slice-start = ((s8[9437184]{0:T(1024)(128)(4,1)}), s8[4194304]{0:T(1024)(128)(4,1)S(1)}, s32[]{:S(2)}) async-start(s8[9437184]{0:T(1024)(128)(4,1)} %bitcast.163), calls=%async_computation.14 | async-start | bytes 8388608
  302.8 12.6 %copy-start.15 = (bf16[512,1152]{1,0:T(8,128)(2,1)S(1)}, bf16[512,1152]{1,0:T(8,128)(2,1)}, u32[]{:S(2)}) copy-start(bf16[512,1152]{1,0:T(8,128)(2,1)} %param.16) | copy-start | bytes 3538948
  302.8 12.6 %slice-start.1 = ((s8[9437184]{0:T(1024)(128)(4,1)}), s8[4194304]{0:T(1024)(128)(4,1)S(1)}, s32[]{:S(2)}) async-start(s8[9437184]{0:T(1024)(128)(4,1)} %bitcast.163), calls=%async_computation.15 | async-start | bytes 8388608
  315.4 40.5 %copy-start.23 = (bf16[640,1152]{1,0:T(8,128)(2,1)S(1)}, bf16[640,1152]{1,0:T(8,128)(2,1)}, u32[]{:S(2)}) copy-start(bf16[640,1152]{1,0:T(8,128)(2,1)} %copy-done.22) | copy-start | bytes 4423684
  330.1 25.8 %collective-permute-start.5 = (bf16[512,1152]{1,0:T(8,128)(2,1)}, bf16[512,1152]{1,0:T(8,128)(2,1)S(1)}, u32[]{:S(2)}, u32[]{:S(2)}) collective-permute-start(bf16[512,1152]{1,0:T(8,128)(2,1)} %get-tuple-element.94), channel_id=1, source_target_pairs={{0,1},{1,0},{2,3},{3,2},{4,5},{5,4},{6,7},{7,6},{8,9},{9,8},{10,11... | collective-permute-start | bytes 3538952 | tf_op jit(solution)/shard_map/ppermute | solution.py:23
  409.6 205.7 %reduce-scatter.6.cloned.1.call-start = ((), (), s32[]{:S(2)}) async-start(), calls=%async_computation.10 | async-start | bytes 10948608 | tf_op jit(solution)/shard_map/reduce_scatter | solution.py:318
  423.0 339.1 %reduce-scatter.8.cloned.1.call-start = ((), (), s32[]{:S(2)}) async-start(), calls=%async_computation.12 | async-start | bytes 10948608 | tf_op jit(solution)/shard_map/reduce_scatter | solution.py:317
  437.5 356.3 %all-gather.12.cloned.1.call-start = ((), (), s32[]{:S(2)}) async-start(), calls=%async_computation.9 | async-start | bytes 2985984 | tf_op jit(solution)/shard_map/all_gather | solution.py:344
  468.8 17.6 %collective-permute-start.7 = (bf16[144,1152]{1,0:T(8,128)(2,1)S(1)}, bf16[144,1152]{1,0:T(8,128)(2,1)S(1)}, u32[]{:S(2)}, u32[]{:S(2)}) collective-permute-start(bf16[144,1152]{1,0:T(8,128)(2,1)S(1)} %slice_bitcast_fusion), channel_id=1, source_target_pairs={{0,2},{1,3},{2,0},{3,1},{4,6},{5,7},{6,4},{7,5},{8,10},{9,11},{10,... | collective-permute-start | bytes 995336 | tf_op jit(solution)/shard_map/ppermute | solution.py:23
  488.3 337.7 %all-gather.14.cloned.1.call-start = ((), (), s32[]{:S(2)}) async-start(), calls=%async_computation.11 | async-start | bytes 2985984 | tf_op jit(solution)/shard_map/all_gather | solution.py:320
  495.5 27.3 %copy-start.39 = (f32[2,1,1152]{2,0,1:T(2,128)S(1)}, f32[2,1,1152]{2,0,1:T(2,128)}, u32[]{:S(2)}) copy-start(f32[2,1,1152]{2,0,1:T(2,128)} %copy-done.38) | copy-start | bytes 27652
  495.5 27.3 %collective-permute-start.6 = (bf16[512,1152]{1,0:T(8,128)(2,1)}, bf16[512,1152]{1,0:T(8,128)(2,1)}, u32[]{:S(2)}, u32[]{:S(2)}) collective-permute-start(bf16[512,1152]{1,0:T(8,128)(2,1)} %convolution_convert_fusion.4), channel_id=1, source_target_pairs={{0,1},{1,0},{2,3},{3,2},{4,5},{5,4},{6,7},{7,6},{8,9},{9,8},{10,11... | collective-permute-start | bytes 3538952 | tf_op jit(solution)/shard_map/ppermute | solution.py:23
  498.6 30.5 %copy-start.16 = (bf16[512,1152]{1,0:T(8,128)(2,1)S(1)}, bf16[512,1152]{1,0:T(8,128)(2,1)}, u32[]{:S(2)}) copy-start(bf16[512,1152]{1,0:T(8,128)(2,1)} %param.16) | copy-start | bytes 3538948
  498.6 30.5 %copy-start.17 = (f32[512,1152]{1,0:T(8,128)S(1)}, f32[512,1152]{1,0:T(8,128)}, u32[]{:S(2)}) copy-start(f32[512,1152]{1,0:T(8,128)} %get-tuple-element.119) | copy-start | bytes 7077892
  498.6 30.5 %copy-start.18 = (f32[512,1152]{1,0:T(8,128)S(1)}, f32[512,1152]{1,0:T(8,128)}, u32[]{:S(2)}) copy-start(f32[512,1152]{1,0:T(8,128)} %get-tuple-element.120) | copy-start | bytes 7077892
  498.6 30.5 %copy-start.19 = (f32[512,1152]{1,0:T(8,128)S(1)}, f32[512,1152]{1,0:T(8,128)}, u32[]{:S(2)}) copy-start(f32[512,1152]{1,0:T(8,128)} %get-tuple-element.121) | copy-start | bytes 7077892
  529.1 99.7 %copy-start.37 = (bf16[1152,216]{0,1:T(8,128)(2,1)S(1)}, bf16[1152,216]{0,1:T(8,128)(2,1)}, u32[]{:S(2)}) copy-start(bf16[1152,216]{0,1:T(8,128)(2,1)} %param.20) | copy-start | bytes 1492996
  616.4 11.5 %all-to-all-start.1 = ((f32[32,2,217]{2,1,0:T(2,128)}), f32[32,2,217]{2,1,0:T(2,128)S(1)}, u32[]{:S(2)}, u32[]{:S(2)}) async-start(f32[32,2,217]{2,1,0:T(2,128)} %copy.37), calls=%async_computation.1 | async-start | bytes 131072 | tf_op jit(solution)/shard_map/all_to_all | solution.py:359
  632.1 136.1 %all-to-all-start.2 = ((f32[32,1,9792]{2,1,0:T(1,128)}), f32[32,1,9792]{2,1,0:T(1,128)S(1)}, u32[]{:S(2)}, u32[]{:S(2)}) async-start(f32[32,1,9792]{2,1,0:T(1,128)} %all_to_all.14), calls=%async_computation.2 | async-start | bytes 2523136 | tf_op jit(solution)/shard_map/all_to_all | solution.py:400
  634.8 223.4 %all-gather.16.cloned.1.call-start = ((), (), s32[]{:S(2)}) async-start(), calls=%async_computation.13 | async-start | bytes 2985984 | tf_op jit(solution)/shard_map/all_gather | solution.py:319
  830.5 32.2 %copy-start.1 = (bf16[1152,1152]{1,0:T(8,128)(2,1)S(1)}, bf16[1152,1152]{1,0:T(8,128)(2,1)}, u32[]{:S(2)}) copy-start(bf16[1152,1152]{1,0:T(8,128)(2,1)} %param.26) | copy-start | bytes 7962628
  (32 other events, 139.1 us)
Sparse Core Ops, SparseCore 0:
  12.3 148.1 all-gather.7
  163.4 103.2 all-gather.9
  409.7 57.9 reduce-scatter.3
  473.7 141.6 reduce-scatter.5
  621.3 140.8 reduce-scatter.7
  764.5 29.2 all-gather.11
  795.7 30.2 all-gather.13
  827.9 30.2 all-gather.15

commit v2 on v1

v2 whole, which is shorter than its diff:
```python
import functools
import math

import jax
import jax.numpy as jnp
from jax import lax
from jax.experimental import pallas as pl
from jax.experimental.pallas import tpu as pltpu
from jax.sharding import PartitionSpec as P

HD = 72
HP = 80
L = 1024
BLOCK = 256
BF = jnp.bfloat16
F32 = jnp.float32
SCALE = HD**-0.5
SCALE2 = SCALE * math.log2(math.e)
MASKED = -1e30
ORDER = (0, 1, 3, 2)


def swap(value, axis, bit):
    n = lax.axis_size(axis)
    return lax.ppermute(value, axis, [(i, i ^ bit) for i in range(n)])


def dot(a, b, ca, cb):
    return lax.dot_general(
        a, b, (((ca,), (cb,)), ((), ())), preferred_element_type=F32
    )


def after(value, *earlier):
    return lax.optimization_barrier((value, *earlier))[0]


def pick(stacked, index):
    return lax.dynamic_index_in_dim(stacked, index, 0, keepdims=False)


def layer_norm(vector):
    centred = vector - jnp.mean(vector, axis=-1, keepdims=True)
    spread = jnp.mean(centred * centred, axis=-1, keepdims=True)
    rsig = lax.rsqrt(spread + 1e-06)
    return centred * rsig, rsig


def norm_back(grad_in, normed, rsig, scale):
    u = grad_in * (1.0 + scale)
    mean_u = jnp.mean(u, axis=-1, keepdims=True)
    mean_un = jnp.mean(u * normed, axis=-1, keepdims=True)
    return (u - mean_u - normed * mean_un) * rsig


def gelu_parts(u):
    a = math.sqrt(2.0 / math.pi)
    t = jnp.tanh(a * (u + 0.044715 * u * u * u))
    return 0.5 * u * (1.0 + t), 0.5 * (1.0 + t) + 0.5 * u * (1.0 - t * t) * (
        a * (1.0 + 3 * 0.044715 * u * u)
    )


def silu_fn(values_in):
    return values_in * jax.nn.sigmoid(values_in)


def head_windows(width):
    found = []
    for h in range(width // HP):
        base = h * HP // 128 * 128
        end = min(-(-(h + 1) * HP // 128) * 128, width)
        found.append((base, end - base, h * HP - base))
    return found


def attn_fwd_kernel(q_ref, k_ref, v_ref, ctx_ref, lse_ref, vt, ct):
    rows, width = q_ref.shape
    qb = 512
    vt[...] = v_ref[...].T
    for h, (base, size, lo) in enumerate(head_windows(width)):
        win = slice(base, base + size)
        lane = lax.broadcasted_iota(jnp.int32, (rows, size), 1)
        here = (lane >= lo) & (lane < lo + HP)
        km = jnp.where(here, k_ref[:, win], jnp.zeros((), BF))
        head = slice(h * HP, (h + 1) * HP)
        vth = vt[head, :]

        def block(j, carry):
            at = pl.ds(pl.multiple_of(j * qb, qb), qb)
            s = dot(km, q_ref[at, win], 1, 1)
            m = jnp.max(s, axis=0, keepdims=True) * SCALE2
            e = jnp.exp2(s * SCALE2 - m)
            total = jnp.sum(e, axis=0, keepdims=True)
            c = dot(vth, e.astype(BF), 1, 0)
            ct[head, at] = c / total
            lse_ref[h, :, at] = m + jnp.log2(total)
            return carry

        lax.fori_loop(0, rows // qb, block, 0)
    ctx_ref[...] = ct[...].T.astype(BF)


def attn_fwd(q, k, v):
    rows, width = q.shape
    heads = width // HP
    return pl.pallas_call(
        attn_fwd_kernel,
        out_shape=(
            jax.ShapeDtypeStruct((rows, width), BF),
            jax.ShapeDtypeStruct((heads, 1, rows), F32),
        ),
        in_specs=[pl.BlockSpec(memory_space=pltpu.VMEM)] * 3,
        out_specs=[pl.BlockSpec(memory_space=pltpu.VMEM)] * 2,
        scratch_shapes=[
            pltpu.VMEM((width, rows), BF),
            pltpu.VMEM((width, rows), F32),
        ],
        compiler_params=pltpu.CompilerParams(vmem_limit_bytes=40 << 20),
        cost_estimate=pl.CostEstimate(
            flops=4 * rows * rows * 256 * heads,
            bytes_accessed=8 * rows * width,
            transcendentals=rows * rows * heads,
        ),
    )(q, k, v)


def attn_bwd_kernel(
    q_ref, k_ref, v_ref, g_ref, lse_ref, dq_ref, dk_ref, dv_ref, kt, dqt, dk_acc, dv_acc
):
    rows, width = q_ref.shape
    qb = 512
    kt[...] = k_ref[...].T
    dk_acc[...] = jnp.zeros_like(dk_acc)
    dv_acc[...] = jnp.zeros_like(dv_acc)
    zero = jnp.zeros((), BF)
    for h, (base, size, lo) in enumerate(head_windows(width)):
        win = slice(base, base + size)
        lane = lax.broadcasted_iota(jnp.int32, (rows, size), 1)
        here = (lane >= lo) & (lane < lo + HP)
        km = jnp.where(here, k_ref[:, win], zero)
        vm = jnp.where(here, v_ref[:, win], zero)
        head = slice(h * HP, (h + 1) * HP)
        row = lax.broadcasted_iota(jnp.int32, (HP, rows), 0)
        kth = jnp.where(row < HD, kt[head, :], zero)
        lane_b = lax.broadcasted_iota(jnp.int32, (qb, size), 1)
        real = (lane_b >= lo) & (lane_b < lo + HD)

        def block(j, carry):
            at = pl.ds(pl.multiple_of(j * qb, qb), qb)
            q_blk = q_ref[at, win]
            g_blk = g_ref[at, win]
            s = dot(km, q_blk, 1, 1)
            p = jnp.exp2(s * SCALE2 - lse_ref[h, :, at])
            dp = dot(vm, g_blk, 1, 1)
            delta = jnp.sum(p * dp, axis=0, keepdims=True)
            ds = (p * (dp - delta)).astype(BF)
            dv_acc[:, win] += dot(p.astype(BF), jnp.where(real, g_blk, zero), 1, 0)
            dk_acc[:, win] += dot(ds, jnp.where(real, q_blk, zero), 1, 0)
            dqt[head, at] = dot(kth, ds, 1, 0)
            return carry

        lax.fori_loop(0, rows // qb, block, 0)
    dq_ref[...] = (dqt[...].T * SCALE).astype(BF)
    dk_ref[...] = (dk_acc[...] * SCALE).astype(BF)
    dv_ref[...] = dv_acc[...].astype(BF)


def attn_bwd(q, k, v, g, lse):
    rows, width = q.shape
    heads = width // HP
    shape = jax.ShapeDtypeStruct((rows, width), BF)
    return pl.pallas_call(
        attn_bwd_kernel,
        out_shape=(shape, shape, shape),
        in_specs=[pl.BlockSpec(memory_space=pltpu.VMEM)] * 5,
        out_specs=[pl.BlockSpec(memory_space=pltpu.VMEM)] * 3,
        scratch_shapes=[
            pltpu.VMEM((width, rows), BF),
            pltpu.VMEM((width, rows), F32),
            pltpu.VMEM((rows, width), F32),
            pltpu.VMEM((rows, width), F32),
        ],
        compiler_params=pltpu.CompilerParams(vmem_limit_bytes=40 << 20),
        cost_estimate=pl.CostEstimate(
            flops=10 * rows * rows * 256 * heads,
            bytes_accessed=14 * rows * width,
            transcendentals=rows * rows * heads,
        ),
    )(q, k, v, g, lse)


def coords(index, n_mp):
    return index // n_mp, lax.rem(index, n_mp)


def wait_all(ref, count, sem):
    whole = ref.at[pl.ds(0, count)]
    pltpu.make_async_copy(whole, whole, sem).wait()


def modulation_kernel(
    per_dp, cond, ids, bias, w_ada, b_ada, mods, silu_out, ids_out, b1_out, bqv_out,
    cond_all, ids_all, bias_all, send, land, sems,
):
    n_dp, n_all, n_mp = cond_all.shape[0], ids_all.shape[0], bias_all.shape[0]
    d, z = lax.axis_index("dp"), lax.axis_index("mp")
    me = d * n_mp + z
    barrier = pltpu.get_barrier_semaphore()

    def greet(t, carry):
        to = coords(lax.rem(me + t, n_all), n_mp)
        pl.semaphore_signal(barrier, inc=1, device_id=to, device_id_type=pl.DeviceIdType.MESH)
        return carry

    lax.fori_loop(1, n_all, greet, 0)
    pl.semaphore_wait(barrier, n_all - 1)

    def copy(src, dst, k, to):
        return pltpu.make_async_remote_copy(
            src_ref=src, dst_ref=dst, send_sem=sems.at[2 * k], recv_sem=sems.at[2 * k + 1],
            device_id=to, device_id_type=pl.DeviceIdType.MESH,
        )

    def send_cond(t, carry):
        copy(cond, cond_all.at[d], 0, (lax.rem(d + t, n_dp), z)).start()
        return carry

    def send_ids(t, carry):
        copy(ids, ids_all.at[me], 1, coords(lax.rem(me + t, n_all), n_mp)).start()
        return carry

    def send_bias(t, carry):
        copy(bias, bias_all.at[z], 2, (d, lax.rem(z + t, n_mp))).start()
        return carry

    lax.fori_loop(1, n_dp, send_cond, 0)
    lax.fori_loop(1, n_all, send_ids, 0)
    lax.fori_loop(1, n_mp, send_bias, 0)
    cond_all[d] = cond[...]
    ids_all[me] = ids[...]
    bias_all[z] = bias[...]
    for k, (ref, n) in enumerate(((cond_all, n_dp), (ids_all, n_all), (bias_all, n_mp))):
        wait_all(ref, n - 1, sems.at[2 * k + 1])

    rows = n_dp * 8
    c = cond_all[...].reshape(rows, cond_all.shape[2])
    silu = (c * (1.0 / (1.0 + jnp.exp(-c)))).astype(BF)
    silu_out[...] = silu
    table = (dot(silu, w_ada[...], 1, 0) + b_ada[...]).astype(BF)
    k = lax.broadcasted_iota(jnp.int32, (n_all * 8, rows), 1)
    image = jnp.where(lax.rem(k, 8) < per_dp, k // 8 * per_dp + lax.rem(k, 8), -2)
    found = ids_all[...].reshape(n_all * 8, 128)[:, :1] == image.astype(F32)
    picked = dot(jnp.where(found, 1.0, 0.0).astype(BF), table, 1, 0)
    send[...] = picked.reshape(send.shape)

    def send_rows(t, carry):
        other = lax.rem(me + t, n_all)
        copy(send.at[other], land.at[me], 3, coords(other, n_mp)).start()
        return carry

    lax.fori_loop(1, n_all, send_rows, 0)
    land[me] = send[me]
    ids_out[...] = ids_all[...]
    sixth = b1_out.shape[1]
    core, q = lax.rem(d, 2), lax.rem(d // 2, 4)
    at = 0
    for i in ORDER:
        for j in range(n_mp):
            quarter = jnp.bitwise_xor(q, i)
            shard = jnp.bitwise_xor(z, j)
            b1_out[at : at + 1, :] = bias_all[shard, pl.ds(core * 4 + quarter, 1), :sixth]
            at += 1
    bqv_out[...] = bias_all[jnp.bitwise_xor(z, 2), 8:, :]
    wait_all(land, n_all - 1, sems.at[7])
    mods[...] = land[...]
    for k, (ref, n) in enumerate(
        ((cond_all, n_dp), (ids_all, n_all), (bias_all, n_mp), (land, n_all))
    ):
        wait_all(ref, n - 1, sems.at[2 * k])


def modulation_rows(cond, ids, bias, w_ada, b_ada, n_dp, n_mp, sixth):
    n_all, per_dp, width, cols = n_dp * n_mp, cond.shape[0], cond.shape[1], w_ada.shape[1]
    cond8 = jnp.pad(cond.astype(F32), ((0, 8 - per_dp), (0, 0)))
    ids8 = jnp.pad(ids.astype(F32), (0, 8 - ids.shape[0]), constant_values=-1.0)
    shapes = (
        jax.ShapeDtypeStruct((n_all, 8, cols), F32),
        jax.ShapeDtypeStruct((n_dp * 8, width), BF),
        jax.ShapeDtypeStruct((n_all, 8, 128), F32),
        jax.ShapeDtypeStruct((16, sixth), F32),
        jax.ShapeDtypeStruct((8, bias.shape[1]), F32),
    )
    return pl.pallas_call(
        functools.partial(modulation_kernel, per_dp),
        out_shape=shapes,
        in_specs=[pl.BlockSpec(memory_space=pltpu.VMEM)] * 5,
        out_specs=[pl.BlockSpec(memory_space=pltpu.VMEM)] * 5,
        scratch_shapes=[
            pltpu.VMEM((n_dp, 8, width), F32),
            pltpu.VMEM((n_all, 8, 128), F32),
            pltpu.VMEM((n_mp, *bias.shape), F32),
            pltpu.VMEM((n_all, 8, cols), F32),
            pltpu.VMEM((n_all, 8, cols), F32),
            pltpu.SemaphoreType.DMA((8,)),
        ],
        compiler_params=pltpu.CompilerParams(
            collective_id=0, has_side_effects=True, vmem_limit_bytes=32 << 20
        ),
    )(
        cond8,
        jnp.broadcast_to(ids8[:, None], (8, 128)),
        bias,
        w_ada,
        b_ada.astype(F32)[None],
    )


def pad_heads(rows_in):
    *lead, n, width = rows_in.shape
    split = rows_in.reshape(*lead, n // HD, HD, width)
    pads = [(0, 0)] * (len(lead) + 1) + [(0, HP - HD), (0, 0)]
    return jnp.pad(split, pads).reshape(*lead, n // HD * HP, width)


def drop_pads(rows_in):
    *lead, n, width = rows_in.shape
    split = rows_in.reshape(*lead, n // HP, HP, width)[..., :HD, :]
    return split.reshape(*lead, n // HP * HD, width)


def on_device(
    patches,
    cotangent,
    conditioning,
    segment,
    image_ids,
    w_ada,
    b_ada,
    w_qkv,
    b_qv,
    w_out,
    b_out,
    w_fc1,
    b_fc1,
    w_fc2,
    b_fc2,
):
    n_dp, n_mp = lax.axis_size("dp"), lax.axis_size("mp")
    n_all = n_dp * n_mp
    z = lax.axis_index("mp")
    d = lax.axis_index("dp")
    core = d & 1
    everyone = ("dp", "mp")
    tokens, width = patches.shape
    n_blocks = tokens // BLOCK
    shard = w_fc2.shape[0]
    hidden_n = shard * n_mp

    q = (d >> 1) & 3
    sixth = shard // 8

    def quarter(w1, w2, i):
        at = (core * 4 + (q ^ i)) * sixth
        return jnp.stack(
            [
                lax.dynamic_slice_in_dim(w1, at, sixth, 1).T,
                lax.dynamic_slice_in_dim(w2, at, sixth, 0),
            ]
        )

    first = quarter(w_fc1, w_fc2, 0)

    heads_shard = w_out.shape[0]
    watt_own = jnp.concatenate([w_qkv.transpose(0, 2, 1), w_out[None]], axis=0)
    p2 = d & 3
    got0 = swap(pick(watt_own, p2), "mp", 2)
    got1 = swap(got0, "dp", 1)
    got23 = swap(jnp.stack([got0, got1]), "dp", 2)
    got = jnp.stack([got0, got1, got23[0], got23[1]])
    watt_other = jnp.stack([pick(got, p2 ^ m) for m in range(4)])
    watts = [pad_heads(watt_own), pad_heads(watt_other)]
    wide = watts[0].shape[1]

    z1 = swap(first, "mp", 1)
    later = after(first, got0)
    groups = [z1[:, None], jnp.stack([swap(later, "mp", 2), swap(later, "mp", 3)], axis=1)]

    def over_plane(group):
        from_x = swap(group, "dp", 2)
        from_y = swap(group, "dp", 4)
        return from_x, from_y

    def far_side(from_x, from_y):
        return swap(from_x[0], "dp", 4), swap(from_y[1], "dp", 2)

    near_1 = over_plane(groups[0])
    far_1 = far_side(*near_1)

    ids = image_ids.reshape(n_blocks, BLOCK)[:, 0]
    cols = w_ada.shape[1]
    bias = jnp.concatenate(
        [
            jnp.pad(b_fc1.astype(F32).reshape(8, sixth), ((0, 0), (0, heads_shard - sixth))),
            jnp.pad(b_qv.astype(F32), ((0, 6), (0, 0))),
        ]
    )
    mod_rows, silu_cond, ids_all, b1_rel, bqv_other = modulation_rows(
        conditioning, ids, bias, w_ada, b_ada, n_dp, n_mp, sixth
    )
    b1_all = b1_rel.reshape(16 * sixth)
    bqvs = [pad_heads(v[..., None])[..., 0].astype(F32) for v in (b_qv, bqv_other[:2])]
    mods = mod_rows[:, :n_blocks].transpose(1, 0, 2).reshape(n_blocks, 6, width)
    shift_attn, scale_attn, gate_attn, shift_mlp, scale_mlp, gate_mlp = [
        mods[:, i, None, :] for i in range(6)
    ]

    def blocks(v):
        return v.reshape(n_blocks, BLOCK, width)

    def flat(v):
        return v.reshape(tokens, width)

    patch_wide = blocks(patches.astype(F32))
    grad_output = blocks(cotangent.astype(F32))
    norm_a, rsig_a = layer_norm(patch_wide)
    attn_in = flat((norm_a * (1.0 + scale_attn) + shift_attn).astype(BF))
    x_row = jnp.concatenate([attn_in, swap(attn_in, "mp", 1)], axis=0)

    seg_own = lax.dynamic_slice_in_dim(segment, z * tokens, tokens, 0)
    seg_peer = lax.dynamic_slice_in_dim(segment, (z ^ 1) * tokens, tokens, 0)
    seg = jnp.concatenate([seg_own, seg_peer])[:, None]
    slot = lax.broadcasted_iota(jnp.int32, (1, wide), 1) % HP - HD
    mark_q = jnp.where(slot == seg, 1.0, 0.0)
    mark_k = jnp.where((slot >= 0) & (slot < 4) & (slot != seg), MASKED, 0.0)

    def project(watt, bqv, rows_in):
        proj = dot(rows_in, watt[:3].reshape(3 * wide, width), 1, 1)
        qh = (proj[:, :wide] + bqv[0] + mark_q).astype(BF)
        kh = (proj[:, wide : 2 * wide] + mark_k).astype(BF)
        return qh, kh, (proj[:, 2 * wide :] + bqv[1]).astype(BF)

    heads_0 = project(watts[0], bqvs[0], x_row)
    ctx_0, lse_0 = attn_fwd(*heads_0)
    near_2 = over_plane(after(groups[1], heads_0[0]))
    heads_1 = project(watts[1], bqvs[1], after(x_row, ctx_0))
    ctx_1, lse_1 = attn_fwd(*heads_1)
    outs = [watts[0][3], watts[1][3]]

    def out_part(at):
        return dot(ctx_0[at], outs[0], 1, 0) + dot(ctx_1[at], outs[1], 1, 0)

    out_send = out_part(slice(tokens, None)).astype(BF)
    far_2 = far_side(*[after(v, out_send) for v in near_2])
    out_peer = swap(out_send, "mp", 1)
    attn_out = blocks(
        out_part(slice(0, tokens)) + out_peer.astype(F32) + b_out.astype(F32)
    )
    w1_late, w2_late = lax.optimization_barrier((w_fc1, w_fc2, attn_in))[:2]
    own = [first] + [quarter(w1_late, w2_late, i) for i in (1, 2, 3)]
    nears = [jnp.concatenate([a, b], axis=1) for a, b in zip(near_1, near_2)]
    fars = [jnp.concatenate([a, b], axis=0) for a, b in zip(far_1, far_2)]
    from_z = jnp.concatenate(groups, axis=1)

    def laid_out(m):
        pieces = [own[0][m][None], from_z[m], own[1][m][None], nears[0][m]]
        pieces += [own[3][m][None], fars[m], own[2][m][None], nears[1][m]]
        return jnp.concatenate(pieces, axis=0).reshape(16 * sixth, width)

    w1_all = laid_out(0)
    w2_all = laid_out(1)
    resid = patch_wide + gate_attn * attn_out
    norm_m, rsig_m = layer_norm(resid)
    mlp_in = flat((norm_m * (1.0 + scale_mlp) + shift_mlp).astype(BF))

    gmo = flat((gate_mlp * grad_output).astype(BF))
    gmo2 = jnp.concatenate([gmo, swap(gmo, "dp", 1)], axis=0)
    mlp2 = jnp.concatenate([mlp_in, swap(mlp_in, "dp", 1)], axis=0)
    pre = dot(mlp2, w1_all, 1, 1) + b1_all
    act, act_grad = gelu_parts(pre)
    hidden = act.astype(BF)

    quad = 4 * sixth

    def grads(left, right, at, to):
        out = dot(left[:, at * quad : to * quad], right, 0, 0)
        return out.reshape(to - at, 4, sixth, width)

    def low_sum(a, b):
        return (a.astype(F32) + b.astype(F32)).astype(BF)

    send2 = grads(hidden, gmo2, 1, 3).astype(BF)
    come2 = swap(send2, "dp", 2)
    grad_pre = (dot(after(gmo2, send2), w2_all, 1, 1) * act_grad).astype(BF)
    grad_b1 = jnp.sum(grad_pre, axis=0, dtype=F32)
    send1 = grads(grad_pre, mlp2, 2, 4).astype(BF)
    come1 = swap(send1, "dp", 4)
    gin_peer = swap(dot(grad_pre[tokens:], w1_all, 1, 0).astype(BF), "dp", 1)
    g_mlp_in = blocks(dot(grad_pre[:tokens], w1_all, 1, 0) + gin_peer.astype(F32))
    g_shift_mlp = jnp.sum(g_mlp_in, axis=1)
    g_scale_mlp = jnp.sum(g_mlp_in * norm_m, axis=1)
    grad_resid = grad_output + norm_back(g_mlp_in, norm_m, rsig_m, scale_mlp)
    g_gate_attn = jnp.sum(grad_resid * attn_out, axis=1)
    gao = flat((gate_attn * grad_resid).astype(BF))
    grad_bout = jnp.sum(gao, axis=0, dtype=F32)
    gao_row = jnp.concatenate([gao, swap(gao, "mp", 1)], axis=0)

    hidden_w, gmo2_w, gpre_w, mlp2_w = lax.optimization_barrier(
        (hidden, gmo2, grad_pre, mlp2, gao)
    )[:4]
    mlp_peer = swap(dot(hidden_w[tokens:], w2_all, 1, 0).astype(BF), "dp", 1)
    keep2_2 = grads(hidden_w, gmo2_w, 3, 4)[0]
    keep2_0 = grads(hidden_w, gmo2_w, 0, 1)[0]
    mlp_out = blocks(
        dot(hidden_w[:tokens], w2_all, 1, 0) + mlp_peer.astype(F32) + b_fc2.astype(F32)
    )
    output = flat((resid + gate_mlp * mlp_out).astype(BF))
    g_gate_mlp = jnp.sum(grad_output * mlp_out, axis=1)
    grad_b2 = jnp.sum(gmo, axis=0, dtype=F32)

    def back(heads, out_w, lse, rows_in):
        grad_ctx = dot(rows_in, out_w, 1, 1).astype(BF)
        return attn_bwd(*heads, grad_ctx, lse)

    def att_grads(ctx, grad3):
        whole = jnp.concatenate(
            [dot(grad3, x_row, 0, 0).astype(BF), dot(ctx, gao_row, 0, 0).astype(BF)], axis=0
        )
        return drop_pads(whole.reshape(4, wide, width)).reshape(4, 2, sixth, width)

    def over_cores(grad_att):
        send = lax.dynamic_index_in_dim(grad_att, 1 - core, 1, keepdims=False)
        keep = lax.dynamic_index_in_dim(grad_att, core, 1, keepdims=False)
        got = low_sum(keep, swap(send, "dp", 1))
        return [pick(got, q ^ i) for i in range(4)]

    dq_1, dk_1, dv_1 = back(heads_1, outs[1], lse_1, gao_row)
    grad3_1 = jnp.concatenate([dq_1, dk_1, dv_1], axis=1)
    come2, come1 = lax.optimization_barrier((come2, come1, dq_1))[:2]
    two_2 = low_sum(keep2_2, come2[1])
    two_0 = low_sum(keep2_0, come2[0])
    come2 = swap(two_2, "dp", 4)
    keep1 = grads(gpre_w, mlp2_w, 0, 2)
    one_1 = low_sum(keep1[1], come1[0])
    one_0 = low_sum(keep1[0], come1[1])
    come1 = swap(one_1, "dp", 2)
    rel_b = over_cores(att_grads(ctx_1, grad3_1))
    dq_0, dk_0, dv_0 = back(heads_0, outs[0], lse_0, after(gao_row, one_1, rel_b[0]))
    come2, come1 = lax.optimization_barrier((come2, come1, dq_0))[:2]
    grad3_0 = jnp.concatenate([dq_0, dk_0, dv_0], axis=1)
    in_w = [w[:3].reshape(3 * wide, width) for w in watts]

    def g_in_part(at):
        return dot(grad3_0[at], in_w[0], 1, 0) + dot(grad3_1[at], in_w[1], 1, 0)

    g_peer = swap(g_in_part(slice(tokens, None)).astype(BF), "mp", 1)
    g_attn_in = blocks(g_in_part(slice(0, tokens)) + g_peer.astype(F32))
    plane2 = low_sum(two_0, come2)
    plane1 = low_sum(one_0, come1)
    rel_a = over_cores(att_grads(ctx_0, grad3_0))

    both = jnp.stack([plane1, plane2])
    whole = both[:, 0].astype(F32)
    for j in (1, 2, 3):
        whole = whole + swap(both[:, j], "mp", j).astype(F32)
    bit = 8
    while bit < n_dp:
        whole = whole + swap(whole.astype(BF), "dp", bit).astype(F32)
        bit *= 2
    done = whole.astype(BF)
    done_x = swap(done, "dp", 2)
    done_y = swap(done, "dp", 4)
    done_xy = jnp.stack([swap(done_x[0], "dp", 4), swap(done_y[1], "dp", 2)])
    mine = jnp.stack([done, done_x, done_y, done_xy])
    theirs = swap(mine, "dp", 1)

    spot = jnp.arange(8 * sixth)
    came = (spot // (4 * sixth)) ^ core, ((spot // sixth) % 4) ^ q
    target = (came[0] * 4 + came[1]) * sixth + spot % sixth
    places = (target[:, None] == spot[None, :]).astype(BF)
    rel = jnp.stack([mine, theirs])
    out_w1 = dot(rel[:, :, 0].reshape(shard, width), places, 0, 0)
    out_w2 = dot(places, rel[:, :, 1].reshape(shard, width), 0, 0)

    come_b = swap(jnp.stack([rel_b[2], rel_b[3]]), "dp", 4)
    b_1 = low_sum(rel_b[1], come_b[1])
    b_0 = low_sum(low_sum(rel_b[0], come_b[0]), swap(b_1, "dp", 2))
    come_a = swap(jnp.stack([rel_a[1], rel_a[3]]), "dp", 2)
    a_2 = low_sum(rel_a[2], come_a[1])
    a_0 = low_sum(low_sum(rel_a[0], come_a[0]), swap(a_2, "dp", 4))
    att = a_0.astype(F32) + swap(b_0, "mp", 2).astype(F32)
    bit = 8
    while bit < n_dp:
        att = att + swap(att.astype(BF), "dp", bit).astype(F32)
        bit *= 2
    att = att.astype(BF)
    att_x = swap(att, "dp", 2)
    att_y = swap(att, "dp", 4)
    att_mine = jnp.stack([att, att_x, att_y, swap(att_x, "dp", 4)])
    rel = jnp.stack([att_mine, swap(att_mine, "dp", 1)]).reshape(shard, width)
    target_att = (came[1] * 2 + came[0]) * sixth + spot % sixth
    places = (target_att[:, None] == spot[None, :]).astype(BF)
    cut = [places[:, m * heads_shard : (m + 1) * heads_shard] for m in range(4)]
    out_qkv = jnp.stack([dot(rel, cut[m], 0, 0) for m in range(3)])
    out_wout = dot(cut[3], rel, 0, 0)

    g_shift_attn = jnp.sum(g_attn_in, axis=1)
    g_scale_attn = jnp.sum(g_attn_in * norm_a, axis=1)
    grad_patches = flat(grad_resid + norm_back(g_attn_in, norm_a, rsig_a, scale_attn))
    sums = jnp.concatenate(
        [g_shift_attn, g_scale_attn, g_gate_attn, g_shift_mlp, g_scale_mlp, g_gate_mlp],
        axis=1,
    )
    to_owner = sums.reshape(n_blocks, n_all, cols).transpose(1, 0, 2)
    got = lax.all_to_all(to_owner, everyone, 0, 0).reshape(n_all * n_blocks, cols)
    ids_from = ids_all[:, :n_blocks, 0].reshape(1, n_all * n_blocks)
    images_here = conditioning.shape[0]
    row = jnp.arange(n_dp * 8)[:, None]
    image = jnp.where(row % 8 < images_here, row // 8 * images_here + row % 8, -2)
    belongs = (ids_from == image.astype(F32)).astype(F32)
    grad_cols = lax.dot_general(
        belongs,
        got,
        (((1,), (0,)), ((), ())),
        precision=lax.Precision.HIGHEST,
        preferred_element_type=F32,
    ).astype(BF)
    grad_w_ada = dot(silu_cond, grad_cols, 0, 0)
    grad_b_ada = jnp.sum(grad_cols, axis=0, dtype=F32)
    silu_part = dot(grad_cols, w_ada, 1, 1)
    silu_part = silu_part.reshape(n_dp, 8, width)[:, :images_here]

    bqv_g = jnp.stack(
        [
            jnp.stack([jnp.sum(v, axis=0, dtype=F32) for v in pair])
            for pair in ((dq_0, dv_0), (dq_1, dv_1))
        ]
    )
    bqv_g = drop_pads(bqv_g[..., None])[..., 0]
    shards = jnp.arange(n_mp)[:, None, None]
    bqv_all = jnp.where(shards == z, bqv_g[0][None], 0.0) + jnp.where(
        shards == (z ^ 2), bqv_g[1][None], 0.0
    )
    nat, rel_at = jnp.arange(8 * n_mp)[:, None], jnp.arange(16)[None, :]
    step = rel_at // 4
    step = jnp.where(step == 2, 3, jnp.where(step == 3, 2, step))
    comes = ((nat // 8) == (z ^ (rel_at % 4))) & ((nat % 4) == (q ^ step))
    comes = comes & (nat // 4 % 2 == core)
    grad_b1 = lax.dot_general(
        comes.astype(F32),
        grad_b1.reshape(16, sixth),
        (((1,), (0,)), ((), ())),
        precision=lax.Precision.HIGHEST,
        preferred_element_type=F32,
    )
    payload = jnp.concatenate(
        [
            jnp.broadcast_to(
                silu_part.reshape(n_dp, 1, images_here * width),
                (n_dp, n_mp, images_here * width),
            ),
            jnp.broadcast_to(
                jnp.concatenate([grad_bout, grad_b2])[None, None], (n_dp, n_mp, 2 * width)
            ),
            jnp.broadcast_to(grad_b1.reshape(1, n_mp, shard), (n_dp, n_mp, shard)),
            jnp.broadcast_to(
                bqv_all.reshape(1, n_mp, 2 * heads_shard), (n_dp, n_mp, 2 * heads_shard)
            ),
        ],
        axis=2,
    ).reshape(n_all, -1)
    summed = jnp.sum(lax.all_to_all(payload, everyone, 0, 0), axis=0)
    at = images_here * width
    grad_silu = summed[:at].reshape(images_here, width)
    _, silu_back = jax.vjp(silu_fn, conditioning.astype(F32))
    grad_cond = silu_back(grad_silu)[0]
    out_bout = summed[at : at + width]
    out_b2 = summed[at + width : at + 2 * width]
    at += 2 * width
    out_b1 = summed[at : at + shard]
    out_bqv = summed[at + shard :].reshape(2, heads_shard)

    return (
        output,
        grad_patches,
        grad_cond,
        grad_w_ada,
        grad_b_ada,
        out_qkv,
        out_bqv,
        out_wout,
        out_bout,
        out_w1,
        out_b1,
        out_w2,
        out_b2,
    )


def solution(mesh):
    rows = P(("dp", "mp"), None)
    in_specs = (
        rows,
        rows,
        P("dp", None),
        P("dp"),
        P(("dp", "mp")),
        P(None, ("dp", "mp")),
        P(("dp", "mp")),
        P(None, None, "mp"),
        P(None, "mp"),
        P("mp", None),
        P(),
        P(None, "mp"),
        P("mp"),
        P("mp", None),
        P(),
    )
    out_specs = (
        rows,
        rows,
        P("dp", None),
        P(None, ("dp", "mp")),
        P(("dp", "mp")),
        P(None, None, "mp"),
        P(None, "mp"),
        P("mp", None),
        P(),
        P(None, "mp"),
        P("mp"),
        P("mp", None),
        P(),
    )
    return jax.shard_map(
        on_device, mesh=mesh, in_specs=in_specs, out_specs=out_specs, check_vma=False
    )
```

time: 875 us -> 641 us (0.73)
  waiting for transfers between devices: 491 us -> 191 us
  blocking collectives: 74.1 us -> 0 us
  other arithmetic: 43.9 us -> 82.1 us
  local copies, waits for them, and re-layouts: 38.7 us -> 76.2 us
  Pallas kernels: 55.2 us -> 83.1 us
  matrix products: 123 us -> 147 us
  starting transfers between devices: 24.1 us -> 47.7 us
  between operations: 19.5 us -> 2.46 us
    reduce_scatter x3 -> x0, waiting for transfers between devices: 241 us -> none  [the longest x1 127 us: on_device(): lax.psum_scatter(grad_w2, ('mp', 'dp'), scatter_dimension=0, tiled=True)]
    all_gather x2 -> x0, blocking collectives: 74.1 us -> none  [the longest x1 64.9 us: on_device(): b1_all = lax.all_gather(b_fc1, 'mp', axis=0, tiled=True).astype(F32)]
    all_gather x5 -> x0, waiting for transfers between devices: 70.7 us -> none  [the longest x1 27.1 us: on_device(): out_w1 = lax.all_gather(red_w1, 'dp', axis=0, tiled=True)]
    ppermute x8 -> x45, starting transfers between devices: 13.7 us -> 41.4 us  [swap(): return lax.ppermute(value, axis, [(i, i ^ bit) for i in range(n)])]
    dot_general x17 -> x35, matrix products: 122 us -> 146 us  [dot(): lax.dot_general(a, b, (((ca,), (cb,)), ((), ())), preferred_element_type=...]
    another operation x1 -> x17, other arithmetic: 0.01 us -> 22.1 us  [the longest x2 4.38 us: on_device(): both = jnp.stack([plane1, plane2])]
    pallas_call x0 -> x1, Pallas kernels: none -> 21.6 us  [modulation_rows(): pl.pallas_call(functools.partial(modulation_kernel, per_dp), out_shape=sh...]
    ppermute x8 -> x45, waiting for transfers between devices: 173 us -> 191 us  [swap(): return lax.ppermute(value, axis, [(i, i ^ bit) for i in range(n)])]
  transfers between devices with their start and end apart: 19 -> 47, of which waited for: 12 -> 16; matrix products, arithmetic and copies ran while one was open for 14% -> 34% of each run, Pallas kernels for 3% -> 10%
where the time goes in v2:
time: 641 us; the launch traced here: 630 us
  waiting for transfers between devices  191 us (30%)
  matrix products  147 us (23%)
  Pallas kernels  83.1 us (13%)
  other arithmetic  82.1 us (13%)
  local copies, waits for them, and re-layouts  76.2 us (12%)
  starting transfers between devices  47.7 us (7%)
    ppermute x45, waiting for transfers between devices, swap(): return lax.ppermute(value, axis, [(i, i ^ bit) for i in range(n)])  191 us
    dot_general x35, matrix products, dot(): lax.dot_general(a, b, (((ca,), (cb,)), ((), ())), preferred_element_type=...  146 us
    ppermute x45, starting transfers between devices, swap(): return lax.ppermute(value, axis, [(i, i ^ bit) for i in range(n)])  41.4 us
    unnamed x215, local copies, waits for them, and re-layouts  36.1 us
    pallas_call x2, Pallas kernels, attn_bwd(): pl.pallas_call(attn_bwd_kernel, out_shape=(shape, shape, shape), in_specs...  30.9 us
    pallas_call x2, Pallas kernels, attn_fwd(): pl.pallas_call(attn_fwd_kernel, out_shape=(jax.ShapeDtypeStruct((rows, wi...  30.6 us
    pallas_call x1, Pallas kernels, modulation_rows(): pl.pallas_call(functools.partial(modulation_kernel, per_dp), out_shape=sh...  21.6 us
  transfers between devices with their start and end apart: 47, of which 16 were waited for; matrix products, arithmetic and copies ran while one was open for 34% of the time, Pallas kernels for 10%

profile of v2, /device:TPU:0, one launch (start us, length us, event | category | flops | bytes accessed | tf_op | source)
XLA Modules:
  0.0 630.0 jit_solution(18194228559699503840)
XLA Ops:
  5.8 21.6 %shard_map.246 = (f32[32,8,216]{2,1,0:T(8,128)S(1)}, bf16[64,1152]{1,0:T(8,128)(2,1)S(1)}, f32[32,8,128]{2,1,0:T(8,128)S(1)}, f32[16,144]{1,0:T(8,128)S(1)}, f32[8,288]{1,0:T(8,128)S(1)}) custom-call(f32[8,1152]{1,0:T(8,128)S(1)} %pad.33.cond, f32[8,128]{1,0:T(8,128)S(1)} %broadcast_in_dim.115.ids, f32[16,288]{1,0:T(8,128)S(1)} %fusion.120.bias, ...), custom_call_target="tpu_custom_call" | custom-call | tf_op jit(solution)/shard_map/pallas_call | solution.py:294
  46.8 3.6 fusion.15
  51.7 3.4 slice.366
  55.5 5.2 copy.130
  62.3 9.4 %collective-permute-done.1 = bf16[288,1152]{1,0:T(8,128)(2,1)} collective-permute-done((bf16[288,1152]{1,0:T(8,128)(2,1)}, bf16[288,1152]{1,0:T(8,128)(2,1)}, u32[]{:S(2)}, u32[]{:S(2)}) %collective-permute-start.1) | collective-permute-done | bytes 663584 | tf_op jit(solution)/shard_map/ppermute | solution.py:25
  76.6 10.3 %collective-permute-done.6 = bf16[2,144,1152]{2,1,0:T(8,128)(2,1)} collective-permute-done((bf16[2,144,1152]{2,1,0:T(8,128)(2,1)}, bf16[2,144,1152]{2,1,0:T(8,128)(2,1)}, u32[]{:S(2)}, u32[]{:S(2)}) %collective-permute-start.6) | collective-permute-done | bytes 663584 | tf_op jit(solution)/shard_map/ppermute | solution.py:25
  89.0 5.2 fusion.151
  95.2 4.0 pad_maximum_fusion.8
  99.2 10.0 %shard_map.247 = (bf16[1024,320]{1,0:T(8,128)(2,1)S(1)}, f32[4,1,1024]{2,1,0:T(1,128)S(1)}) custom-call(bf16[1024,320]{1,0:T(8,128)(2,1)S(1)} %get-tuple-element.107.q_ref, bf16[1024,320]{1,0:T(8,128)(2,1)S(1)} %get-tuple-element.106.k_ref, bf16[1024,320]{1,0:T(8,128)(2,1)S(1)} %get-tuple-element.109.v_ref), custom_call_target="tpu_custom_call" | custom-call | flops 4294967296 | bytes 2621440 | tf_op jit(solution)/shard_map/pallas_call | solution.py:107
  112.9 19.7 %collective-permute-done.7 = bf16[2,144,1152]{2,1,0:T(8,128)(2,1)S(1)} collective-permute-done((bf16[2,144,1152]{2,1,0:T(8,128)(2,1)}, bf16[2,144,1152]{2,1,0:T(8,128)(2,1)S(1)}, u32[]{:S(2)}, u32[]{:S(2)}) %collective-permute-start.7) | collective-permute-done | bytes 663584 | tf_op jit(solution)/shard_map/ppermute | solution.py:25
  133.9 3.1 copy.132
  151.5 20.0 %collective-permute-done.3 = bf16[2,288,1152]{2,1,0:T(8,128)(2,1)S(1)} collective-permute-done((bf16[2,288,1152]{2,1,0:T(8,128)(2,1)S(1)}, bf16[2,288,1152]{2,1,0:T(8,128)(2,1)S(1)}, u32[]{:S(2)}, u32[]{:S(2)}) %collective-permute-start.3) | collective-permute-done | bytes 1327136 | tf_op jit(solution)/shard_map/ppermute | solution.py:25
  176.0 2.9 fusion.161
  180.0 20.7 %shard_map.248 = (bf16[1024,320]{1,0:T(8,128)(2,1)S(1)}, f32[4,1,1024]{2,1,0:T(1,128)S(1)}) custom-call(bf16[1024,320]{1,0:T(8,128)(2,1)S(1)} %get-tuple-element.105.q_ref, bf16[1024,320]{1,0:T(8,128)(2,1)S(1)} %get-tuple-element.104.k_ref, bf16[1024,320]{1,0:T(8,128)(2,1)S(1)} %get-tuple-element.108.v_ref), custom_call_target="tpu_custom_call" | custom-call | flops 4294967296 | bytes 2621440 | tf_op jit(solution)/shard_map/pallas_call | solution.py:107
  213.5 8.6 %collective-permute-done.4 = bf16[512,1152]{1,0:T(8,128)(2,1)S(1)} collective-permute-done((bf16[512,1152]{1,0:T(8,128)(2,1)S(1)}, bf16[512,1152]{1,0:T(8,128)(2,1)S(1)}, u32[]{:S(2)}, u32[]{:S(2)}) %collective-permute-start.4) | collective-permute-done | bytes 1179680 | tf_op jit(solution)/shard_map/ppermute | solution.py:25
  232.2 15.7 %multiply_convert_fusion = (bf16[1024,2304]{1,0:T(8,128)(2,1)S(1)}, f32[1024,2304]{1,0:T(8,128)}) fusion(f32[2304]{0:T(1024)S(1)} %add.578, bf16[2304,1152]{1,0:T(8,128)(2,1)} %bitcast.365, bf16[512,1152]{1,0:T(8,128)(2,1)S(1)} %collective-permute-done.5, bf16[512,1152]{1,0:T(8,128)(2,1)S(1)} %fusion.33), kind=kOutput, calls=%fused_computation.11 | convolution fusion | flops 5464129536 | bytes 21832704 | tf_op jit(solution)/shard_map/dot_general | solution.py:29
  247.9 8.6 %convolution_convert_fusion.1 = bf16[1152,1152]{1,0:T(8,128)(2,1)} fusion(bf16[1024,2304]{1,0:T(8,128)(2,1)S(1)} %get-tuple-element.58, bf16[512,1152]{1,0:T(8,128)(2,1)} %collective-permute-done.15, bf16[512,1152]{1,0:T(8,128)(2,1)} %get-tuple-element.95), kind=kOutput, calls=%fused_computation.13 | convolution fusion | flops 2723954688 | bytes 7372800 | tf_op jit(solution)/shard_map/dot_general | solution.py:29
  256.5 13.4 %convert_reduce_fusion = (f32[2304]{0:T(1024)S(1)}, bf16[1024,2304]{1,0:T(8,128)(2,1)S(1)}) fusion(f32[1024,2304]{1,0:T(8,128)} %get-tuple-element.148, f32[2304]{0:T(1024)S(1)} %add.578, bf16[1024,1152]{1,0:T(8,128)(2,1)S(1)} %pad_maximum_fusion.10, bf16[2304,1152]{1,0:T(8,128)(2,1)S(1)} %bitcast.360), kind=kOutput, calls=%fused_computation.10 | convolution fusion | flops 5487720448 | bytes 21841920 | tf_op jit(solution)/shard_map/dot_general | solution.py:29
  270.0 8.5 %convolution_convert_fusion.5 = bf16[512,1152]{1,0:T(8,128)(2,1)} fusion(bf16[2304,1152]{1,0:T(8,128)(2,1)} %bitcast.366, bf16[1024,2304]{1,0:T(8,128)(2,1)S(1)} %get-tuple-element.59), kind=kOutput, calls=%fused_computation.50 | convolution fusion | flops 2718498816 | bytes 8847360 | tf_op jit(solution)/shard_map/dot_general | solution.py:29
  280.2 6.8 %convolution_convert_fusion = bf16[1152,1152]{1,0:T(8,128)(2,1)} fusion(bf16[1024,2304]{1,0:T(8,128)(2,1)} %copy-done.66, bf16[512,1152]{1,0:T(8,128)(2,1)} %copy-done.67, bf16[512,1152]{1,0:T(8,128)(2,1)S(1)} %fusion.33), kind=kOutput, calls=%fused_computation.12 | convolution fusion | flops 2723954688 | bytes 7372800 | tf_op jit(solution)/shard_map/dot_general | solution.py:29
  290.7 7.6 %fusion.45 = (f32[512]{0:T(512)S(1)}, f32[512]{0:T(512)S(1)}, f32[512,1152]{1,0:T(8,128)S(1)}) fusion(f32[2,1152]{1,0:T(2,128)S(1)} %get-tuple-element.158, f32[512]{0:T(512)S(1)} %add_rsqrt_fusion, f32[512,1152]{1,0:T(8,128)S(1)} %copy-done.14, f32[512]{0:T(512)S(1)} %broadcast_multiply_fusion.4, bf16[512,1152]{1,0:T(8,128)(2,1)} %collective-permute-done.18, ...), kind=kOutput, calls=%fused_computation.132 | convolution fusion | flops 2722626560 | bytes 13583360 | tf_op jit(solution)/shard_map/dot_general | solution.py:29
  301.2 4.4 convolution_convert_fusion.4
  305.6 3.3 fusion.40
  309.0 3.6 fusion.64
  315.3 13.0 %collective-permute-done.20 = bf16[512,1152]{1,0:T(8,128)(2,1)S(1)} collective-permute-done((bf16[512,1152]{1,0:T(8,128)(2,1)S(1)}, bf16[512,1152]{1,0:T(8,128)(2,1)S(1)}, u32[]{:S(2)}, u32[]{:S(2)}) %collective-permute-start.20) | collective-permute-done | bytes 1179680 | tf_op jit(solution)/shard_map/ppermute | solution.py:25
  334.9 15.4 %shard_map.249 = (bf16[1024,320]{1,0:T(8,128)(2,1)S(1)}, bf16[1024,320]{1,0:T(8,128)(2,1)S(1)}, bf16[1024,320]{1,0:T(8,128)(2,1)S(1)}) custom-call(bf16[1024,320]{1,0:T(8,128)(2,1)S(1)} %copy-done.7, bf16[1024,320]{1,0:T(8,128)(2,1)S(1)} %get-tuple-element.104.k_ref, bf16[1024,320]{1,0:T(8,128)(2,1)S(1)} %copy-done.9, bf16[1024,320]{1,0:T(8,128)(2,1)S(1)} %copy-done.10, ...), custom_call_target="tpu_custom_call" | custom-call | flops 10737418240 | bytes 4587520 | tf_op jit(solution)/shard_map/pallas_call | solution.py:173
  351.1 5.2 convolution_convert_fusion.3
  360.4 4.6 fusion.62
  365.8 9.4 %fusion.31 = (bf16[512,1152]{1,0:T(8,128)(2,1)}, f32[512,1152]{1,0:T(8,128)}) fusion(f32[512,1152]{1,0:T(8,128)} %copy-done.13, f32[2,1152]{1,0:T(2,128)S(1)} %bitcast.405, f32[1152]{0:T(1024)S(1)} %convert_element_type.384, bf16[512,1152]{1,0:T(8,128)(2,1)} %collective-permute-done.19, bf16[2304,1152]{1,0:T(8,128)(2,1)} %bitcast.361, ...), kind=kOutput, calls=%fused_computation.91 | convolution fusion | flops 2721447936 | bytes 14759424 | tf_op jit(solution)/shard_map/dot_general | solution.py:29
  381.4 2.8 fusion.18
  385.5 13.0 %collective-permute-done.28 = bf16[2,144,1152]{2,1,0:T(8,128)(2,1)S(1)} collective-permute-done((bf16[2,144,1152]{2,1,0:T(8,128)(2,1)S(1)}, bf16[2,144,1152]{2,1,0:T(8,128)(2,1)S(1)}, u32[]{:S(2)}, u32[]{:S(2)}) %collective-permute-start.28) | collective-permute-done | bytes 663584 | tf_op jit(solution)/shard_map/ppermute | solution.py:25
  403.9 5.4 collective-permute-done.29
  413.6 15.4 %shard_map.250 = (bf16[1024,320]{1,0:T(8,128)(2,1)S(1)}, bf16[1024,320]{1,0:T(8,128)(2,1)S(1)}, bf16[1024,320]{1,0:T(8,128)(2,1)S(1)}) custom-call(bf16[1024,320]{1,0:T(8,128)(2,1)S(1)} %copy-done.3, bf16[1024,320]{1,0:T(8,128)(2,1)S(1)} %copy-done.1, bf16[1024,320]{1,0:T(8,128)(2,1)S(1)} %copy-done.5, bf16[1024,320]{1,0:T(8,128)(2,1)S(1)} %copy.138.g_ref, ...), custom_call_target="tpu_custom_call" | custom-call | flops 10737418240 | bytes 4587520 | tf_op jit(solution)/shard_map/pallas_call | solution.py:173
  438.8 4.4 convolution_convert_fusion.2
  456.9 20.2 %collective-permute-done.24 = bf16[512,1152]{1,0:T(8,128)(2,1)} collective-permute-done((bf16[512,1152]{1,0:T(8,128)(2,1)}, bf16[512,1152]{1,0:T(8,128)(2,1)}, u32[]{:S(2)}, u32[]{:S(2)}) %collective-permute-start.24) | collective-permute-done | bytes 1179680 | tf_op jit(solution)/shard_map/ppermute | solution.py:25
  477.3 3.3 fusion.44
  481.2 3.7 fusion.39
  488.4 28.3 %collective-permute-done.38 = bf16[2,144,1152]{2,1,0:T(8,128)(2,1)} collective-permute-done((bf16[2,144,1152]{2,1,0:T(8,128)(2,1)}, bf16[2,144,1152]{2,1,0:T(8,128)(2,1)}, u32[]{:S(2)}, u32[]{:S(2)}) %collective-permute-start.38) | collective-permute-done | bytes 663584 | tf_op jit(solution)/shard_map/ppermute | solution.py:25
  528.0 3.6 all_to_all.10
  531.6 3.7 all-to-all-start.1
  535.3 23.0 %collective-permute-done.26 = bf16[2,144,1152]{2,1,0:T(8,128)(2,1)} collective-permute-done((bf16[2,144,1152]{2,1,0:T(8,128)(2,1)}, bf16[2,144,1152]{2,1,0:T(8,128)(2,1)}, u32[]{:S(2)}, u32[]{:S(2)}) %collective-permute-start.26) | collective-permute-done | bytes 663584 | tf_op jit(solution)/shard_map/ppermute | solution.py:25
  562.5 5.4 collective-permute-done.27
  577.7 4.8 collective-permute-done.42
  582.5 3.9 collective-permute-done.32
  586.4 3.6 collective-permute-done.33
  591.3 3.8 pad_maximum_fusion.7
  614.7 6.5 %fusion.11 = f32[1152,1152]{1,0:T(8,128)} fusion(bf16[1152,1152]{1,0:T(8,128)(2,1)S(1)} %bitcast.376, s32[1152]{0:T(1024)S(1)} %fusion.127), kind=kOutput, calls=%fused_computation.21 | convolution fusion | flops 3058974720 | bytes 7967232 | tf_op jit(solution)/shard_map/dot_general | solution.py:29
  621.2 6.5 %fusion.10 = f32[1152,1152]{1,0:T(8,128)} fusion(bf16[1152,1152]{1,0:T(8,128)(2,1)S(1)} %bitcast.375, s32[1152]{0:T(1024)S(1)} %fusion.127), kind=kOutput, calls=%fused_computation.20 | convolution fusion | flops 3058974720 | bytes 7967232 | tf_op jit(solution)/shard_map/dot_general | solution.py:29
  (466 shorter events, 198.9 us)
Async XLA Ops:
  30.1 58.1 %collective-permute-start = (bf16[512,1152]{1,0:T(8,128)(2,1)}, bf16[512,1152]{1,0:T(8,128)(2,1)}, u32[]{:S(2)}, u32[]{:S(2)}) collective-permute-start(bf16[512,1152]{1,0:T(8,128)(2,1)} %fusion.28), channel_id=1, source_target_pairs={{0,1},{1,0},{2,3},{3,2},{4,5},{5,4},{6,7},{7,6},{8,9},{9,8},{10,11... | collective-permute-start | bytes 3538952 | tf_op jit(solution)/shard_map/ppermute | solution.py:25
  33.0 38.7 %collective-permute-start.1 = (bf16[288,1152]{1,0:T(8,128)(2,1)}, bf16[288,1152]{1,0:T(8,128)(2,1)}, u32[]{:S(2)}, u32[]{:S(2)}) collective-permute-start(bf16[288,1152]{1,0:T(8,128)(2,1)} %fusion.84), channel_id=1, source_target_pairs={{0,2},{1,3},{2,0},{3,1},{4,6},{5,7},{6,4},{7,5},{8,10},{9,11},{10,... | collective-permute-start | bytes 1990664 | tf_op jit(solution)/shard_map/ppermute | solution.py:25
  41.7 45.2 %collective-permute-start.6 = (bf16[2,144,1152]{2,1,0:T(8,128)(2,1)}, bf16[2,144,1152]{2,1,0:T(8,128)(2,1)}, u32[]{:S(2)}, u32[]{:S(2)}) collective-permute-start(bf16[2,144,1152]{2,1,0:T(8,128)(2,1)} %pad_maximum_fusion.21), channel_id=1, source_target_pairs={{0,1},{1,0},{2,3},{3,2},{4,5},{5,4},{6,7},{7,6},{8,9},{9,8},{10,11... | collective-permute-start | bytes 1990664 | tf_op jit(solution)/shard_map/ppermute | solution.py:25
  44.1 65.1 %collective-permute-start.15 = (bf16[512,1152]{1,0:T(8,128)(2,1)}, bf16[512,1152]{1,0:T(8,128)(2,1)}, u32[]{:S(2)}, u32[]{:S(2)}) collective-permute-start(bf16[512,1152]{1,0:T(8,128)(2,1)} %get-tuple-element.95), channel_id=1, source_target_pairs={{0,4},{4,0},{8,12},{12,8},{16,20},{20,16},{24,28},{28,24},{1,5},{5... | collective-permute-start | bytes 3538952 | tf_op jit(solution)/shard_map/ppermute | solution.py:25
  55.2 166.9 %copy-start.77 = (f32[1152]{0:T(1024)}, f32[1152]{0:T(1024)S(1)}, u32[]{:S(2)}) copy-start(f32[1152]{0:T(1024)S(1)} %convert_element_type.371) | copy-start | bytes 13828
  71.7 41.3 %collective-permute-start.8 = (bf16[2,144,1152]{2,1,0:T(8,128)(2,1)}, bf16[2,144,1152]{2,1,0:T(8,128)(2,1)S(1)}, u32[]{:S(2)}, u32[]{:S(2)}) collective-permute-start(bf16[2,144,1152]{2,1,0:T(8,128)(2,1)} %pad_maximum_fusion.21), channel_id=1, source_target_pairs={{0,3},{1,2},{2,1},{3,0},{4,7},{5,6},{6,5},{7,4},{8,11},{9,10},{10,... | collective-permute-start | bytes 1990664 | tf_op jit(solution)/shard_map/ppermute | solution.py:25
  74.1 58.6 %collective-permute-start.7 = (bf16[2,144,1152]{2,1,0:T(8,128)(2,1)}, bf16[2,144,1152]{2,1,0:T(8,128)(2,1)S(1)}, u32[]{:S(2)}, u32[]{:S(2)}) collective-permute-start(bf16[2,144,1152]{2,1,0:T(8,128)(2,1)} %pad_maximum_fusion.21), channel_id=1, source_target_pairs={{0,2},{1,3},{2,0},{3,1},{4,6},{5,7},{6,4},{7,5},{8,10},{9,11},{10,... | collective-permute-start | bytes 1990664 | tf_op jit(solution)/shard_map/ppermute | solution.py:25
  86.9 54.6 %collective-permute-start.9 = (bf16[2,1,144,1152]{3,2,1,0:T(8,128)(2,1)}, bf16[2,1,144,1152]{3,2,1,0:T(8,128)(2,1)S(1)}, u32[]{:S(2)}, u32[]{:S(2)}) collective-permute-start(bf16[2,1,144,1152]{3,2,1,0:T(8,128)(2,1)} %bitcast.24), channel_id=1, source_target_pairs={{0,8},{4,12},{8,0},{12,4},{16,24},{20,28},{24,16},{28,20},{1,9},{5... | collective-permute-start | bytes 1990664 | tf_op jit(solution)/shard_map/ppermute | solution.py:25
  88.2 55.0 %collective-permute-start.13 = (bf16[2,1,144,1152]{3,2,1,0:T(8,128)(2,1)}, bf16[2,1,144,1152]{3,2,1,0:T(8,128)(2,1)S(1)}, u32[]{:S(2)}, u32[]{:S(2)}) collective-permute-start(bf16[2,1,144,1152]{3,2,1,0:T(8,128)(2,1)} %bitcast.24), channel_id=1, source_target_pairs={{0,16},{4,20},{8,24},{12,28},{16,0},{20,4},{24,8},{28,12},{1,17},{... | collective-permute-start | bytes 1990664 | tf_op jit(solution)/shard_map/ppermute | solution.py:25
  109.2 28.9 %collective-permute-start.2 = (bf16[288,1152]{1,0:T(8,128)(2,1)}, bf16[288,1152]{1,0:T(8,128)(2,1)S(1)}, u32[]{:S(2)}, u32[]{:S(2)}) collective-permute-start(bf16[288,1152]{1,0:T(8,128)(2,1)} %collective-permute-done.1), channel_id=1, source_target_pairs={{0,4},{4,0},{8,12},{12,8},{16,20},{20,16},{24,28},{28,24},{1,5},{5... | collective-permute-start | bytes 1990664 | tf_op jit(solution)/shard_map/ppermute | solution.py:25
  137.0 66.8 %collective-permute-start.14 = (bf16[2,2,144,1152]{3,2,0,1:T(8,128)(2,1)}, bf16[2,2,144,1152]{3,2,0,1:T(8,128)(2,1)}, u32[]{:S(2)}, u32[]{:S(2)}) collective-permute-start(bf16[2,2,144,1152]{3,2,0,1:T(8,128)(2,1)} %pad_maximum_fusion.16), channel_id=1, source_target_pairs={{0,16},{4,20},{8,24},{12,28},{16,0},{20,4},{24,8},{28,12},{1,17},{... | collective-permute-start | bytes 3981320 | tf_op jit(solution)/shard_map/ppermute | solution.py:25
  139.4 32.1 %collective-permute-start.3 = (bf16[2,288,1152]{2,1,0:T(8,128)(2,1)S(1)}, bf16[2,288,1152]{2,1,0:T(8,128)(2,1)S(1)}, u32[]{:S(2)}, u32[]{:S(2)}) collective-permute-start(bf16[2,288,1152]{2,1,0:T(8,128)(2,1)S(1)} %pad_maximum_fusion.15), channel_id=1, source_target_pairs={{0,8},{4,12},{8,0},{12,4},{16,24},{20,28},{24,16},{28,20},{1,9},{5... | collective-permute-start | bytes 3981320 | tf_op jit(solution)/shard_map/ppermute | solution.py:25
  140.5 61.1 %collective-permute-start.10 = (bf16[2,2,144,1152]{3,2,1,0:T(8,128)(2,1)}, bf16[2,2,144,1152]{3,2,1,0:T(8,128)(2,1)}, u32[]{:S(2)}, u32[]{:S(2)}) collective-permute-start(bf16[2,2,144,1152]{3,2,1,0:T(8,128)(2,1)} %copy.132), channel_id=1, source_target_pairs={{0,8},{4,12},{8,0},{12,4},{16,24},{20,28},{24,16},{28,20},{1,9},{5... | collective-permute-start | bytes 3981320 | tf_op jit(solution)/shard_map/ppermute | solution.py:25
  142.3 69.4 %collective-permute-start.11 = (bf16[1,144,1152]{2,1,0:T(8,128)(2,1)}, bf16[1,144,1152]{2,1,0:T(8,128)(2,1)S(1)}, u32[]{:S(2)}, u32[]{:S(2)}) collective-permute-start(bf16[1,144,1152]{2,1,0:T(8,128)(2,1)} %slice_bitcast_fusion.10), channel_id=1, source_target_pairs={{0,16},{4,20},{8,24},{12,28},{16,0},{20,4},{24,8},{28,12},{1,17},{... | collective-permute-start | bytes 995336 | tf_op jit(solution)/shard_map/ppermute | solution.py:25
  144.0 68.5 %collective-permute-start.16 = (bf16[1,144,1152]{2,1,0:T(8,128)(2,1)}, bf16[1,144,1152]{2,1,0:T(8,128)(2,1)}, u32[]{:S(2)}, u32[]{:S(2)}) collective-permute-start(bf16[1,144,1152]{2,1,0:T(8,128)(2,1)} %slice_bitcast_fusion.9), channel_id=1, source_target_pairs={{0,8},{4,12},{8,0},{12,4},{16,24},{20,28},{24,16},{28,20},{1,9},{5... | collective-permute-start | bytes 995336 | tf_op jit(solution)/shard_map/ppermute | solution.py:25
  201.5 20.6 %collective-permute-start.4 = (bf16[512,1152]{1,0:T(8,128)(2,1)S(1)}, bf16[512,1152]{1,0:T(8,128)(2,1)S(1)}, u32[]{:S(2)}, u32[]{:S(2)}) collective-permute-start(bf16[512,1152]{1,0:T(8,128)(2,1)S(1)} %fusion.14), channel_id=1, source_target_pairs={{0,1},{1,0},{2,3},{3,2},{4,5},{5,4},{6,7},{7,6},{8,9},{9,8},{10,11... | collective-permute-start | bytes 3538952 | tf_op jit(solution)/shard_map/ppermute | solution.py:25
  202.7 23.3 %collective-permute-start.12 = (bf16[2,144,1152]{2,1,0:T(8,128)(2,1)S(1)}, bf16[2,144,1152]{2,1,0:T(8,128)(2,1)S(1)}, u32[]{:S(2)}, u32[]{:S(2)}) collective-permute-start(bf16[2,144,1152]{2,1,0:T(8,128)(2,1)S(1)} %slice_bitcast_fusion.5), channel_id=1, source_target_pairs={{0,16},{4,20},{8,24},{12,28},{16,0},{20,4},{24,8},{28,12},{1,17},{... | collective-permute-start | bytes 1990664 | tf_op jit(solution)/shard_map/ppermute | solution.py:25
  210.2 18.4 %collective-permute-start.17 = (bf16[2,144,1152]{2,1,0:T(8,128)(2,1)S(1)}, bf16[2,144,1152]{2,1,0:T(8,128)(2,1)S(1)}, u32[]{:S(2)}, u32[]{:S(2)}) collective-permute-start(bf16[2,144,1152]{2,1,0:T(8,128)(2,1)S(1)} %slice_bitcast_fusion.4), channel_id=1, source_target_pairs={{0,8},{4,12},{8,0},{12,4},{16,24},{20,28},{24,16},{28,20},{1,9},{5... | collective-permute-start | bytes 1990664 | tf_op jit(solution)/shard_map/ppermute | solution.py:25
  226.0 6.1 collective-permute-start.5
  278.4 11.9 %collective-permute-start.18 = (bf16[512,1152]{1,0:T(8,128)(2,1)}, bf16[512,1152]{1,0:T(8,128)(2,1)}, u32[]{:S(2)}, u32[]{:S(2)}) collective-permute-start(bf16[512,1152]{1,0:T(8,128)(2,1)} %convolution_convert_fusion.5), channel_id=1, source_target_pairs={{0,4},{4,0},{8,12},{12,8},{16,20},{20,16},{24,28},{28,24},{1,5},{5... | collective-permute-start | bytes 3538952 | tf_op jit(solution)/shard_map/ppermute | solution.py:25
  279.1 98.1 %collective-permute-start.21 = (bf16[2,4,144,1152]{3,2,1,0:T(8,128)(2,1)}, bf16[2,4,144,1152]{3,2,1,0:T(8,128)(2,1)}, u32[]{:S(2)}, u32[]{:S(2)}) collective-permute-start(bf16[2,4,144,1152]{3,2,1,0:T(8,128)(2,1)} %bitcast.406), channel_id=1, source_target_pairs={{0,8},{4,12},{8,0},{12,4},{16,24},{20,28},{24,16},{28,20},{1,9},{5... | collective-permute-start | bytes 7962632 | tf_op jit(solution)/shard_map/ppermute | solution.py:25
  286.9 90.3 %collective-permute-start.22 = (bf16[2,4,144,1152]{3,2,1,0:T(8,128)(2,1)}, bf16[2,4,144,1152]{3,2,1,0:T(8,128)(2,1)}, u32[]{:S(2)}, u32[]{:S(2)}) collective-permute-start(bf16[2,4,144,1152]{3,2,1,0:T(8,128)(2,1)} %bitcast.53), channel_id=1, source_target_pairs={{0,16},{4,20},{8,24},{12,28},{16,0},{20,4},{24,8},{28,12},{1,17},{... | collective-permute-start | bytes 7962632 | tf_op jit(solution)/shard_map/ppermute | solution.py:25
  300.8 27.4 %collective-permute-start.20 = (bf16[512,1152]{1,0:T(8,128)(2,1)S(1)}, bf16[512,1152]{1,0:T(8,128)(2,1)S(1)}, u32[]{:S(2)}, u32[]{:S(2)}) collective-permute-start(bf16[512,1152]{1,0:T(8,128)(2,1)S(1)} %get-tuple-element.92), channel_id=1, source_target_pairs={{0,1},{1,0},{2,3},{3,2},{4,5},{5,4},{6,7},{7,6},{8,9},{9,8},{10,11... | collective-permute-start | bytes 3538952 | tf_op jit(solution)/shard_map/ppermute | solution.py:25
  305.6 60.1 %collective-permute-start.19 = (bf16[512,1152]{1,0:T(8,128)(2,1)}, bf16[512,1152]{1,0:T(8,128)(2,1)}, u32[]{:S(2)}, u32[]{:S(2)}) collective-permute-start(bf16[512,1152]{1,0:T(8,128)(2,1)} %convolution_convert_fusion.4), channel_id=1, source_target_pairs={{0,4},{4,0},{8,12},{12,8},{16,20},{20,16},{24,28},{28,24},{1,5},{5... | collective-permute-start | bytes 3538952 | tf_op jit(solution)/shard_map/ppermute | solution.py:25
  359.4 17.8 %collective-permute-start.23 = (bf16[4,144,1152]{2,1,0:T(8,128)(2,1)S(1)}, bf16[4,144,1152]{2,1,0:T(8,128)(2,1)}, u32[]{:S(2)}, u32[]{:S(2)}) collective-permute-start(bf16[4,144,1152]{2,1,0:T(8,128)(2,1)S(1)} %dynamic-slice_bitcast_fusion.1), channel_id=1, source_target_pairs={{0,4},{4,0},{8,12},{12,8},{16,20},{20,16},{24,28},{28,24},{1,5},{5... | collective-permute-start | bytes 3981320 | tf_op jit(solution)/shard_map/ppermute | solution.py:25
  380.6 17.9 %collective-permute-start.28 = (bf16[2,144,1152]{2,1,0:T(8,128)(2,1)S(1)}, bf16[2,144,1152]{2,1,0:T(8,128)(2,1)S(1)}, u32[]{:S(2)}, u32[]{:S(2)}) collective-permute-start(bf16[2,144,1152]{2,1,0:T(8,128)(2,1)S(1)} %pad_maximum_fusion.23), channel_id=1, source_target_pairs={{0,16},{4,20},{8,24},{12,28},{16,0},{20,4},{24,8},{28,12},{1,17},{... | collective-permute-start | bytes 1990664 | tf_op jit(solution)/shard_map/ppermute | solution.py:25
  384.2 60.6 %collective-permute-start.35 = (bf16[4,144,1152]{2,1,0:T(8,128)(2,1)}, bf16[4,144,1152]{2,1,0:T(8,128)(2,1)}, u32[]{:S(2)}, u32[]{:S(2)}) collective-permute-start(bf16[4,144,1152]{2,1,0:T(8,128)(2,1)} %fusion.18), channel_id=1, source_target_pairs={{0,16},{4,20},{8,24},{12,28},{16,0},{20,4},{24,8},{28,12},{1,17},{... | collective-permute-start | bytes 3981320 | tf_op jit(solution)/shard_map/ppermute | solution.py:25
  398.6 10.7 %collective-permute-start.29 = (bf16[144,1152]{1,0:T(8,128)(2,1)S(1)}, bf16[144,1152]{1,0:T(8,128)(2,1)S(1)}, u32[]{:S(2)}, u32[]{:S(2)}) collective-permute-start(bf16[144,1152]{1,0:T(8,128)(2,1)S(1)} %fusion.102), channel_id=1, source_target_pairs={{0,8},{4,12},{8,0},{12,4},{16,24},{20,28},{24,16},{28,20},{1,9},{5... | collective-permute-start | bytes 995336 | tf_op jit(solution)/shard_map/ppermute | solution.py:25
  402.0 42.8 %collective-permute-start.36 = (bf16[4,144,1152]{2,1,0:T(8,128)(2,1)}, bf16[4,144,1152]{2,1,0:T(8,128)(2,1)}, u32[]{:S(2)}, u32[]{:S(2)}) collective-permute-start(bf16[4,144,1152]{2,1,0:T(8,128)(2,1)} %fusion.22), channel_id=1, source_target_pairs={{0,8},{4,12},{8,0},{12,4},{16,24},{20,28},{24,16},{28,20},{1,9},{5... | collective-permute-start | bytes 3981320 | tf_op jit(solution)/shard_map/ppermute | solution.py:25
  436.6 40.6 %collective-permute-start.24 = (bf16[512,1152]{1,0:T(8,128)(2,1)}, bf16[512,1152]{1,0:T(8,128)(2,1)}, u32[]{:S(2)}, u32[]{:S(2)}) collective-permute-start(bf16[512,1152]{1,0:T(8,128)(2,1)} %fusion.13), channel_id=1, source_target_pairs={{0,1},{1,0},{2,3},{3,2},{4,5},{5,4},{6,7},{7,6},{8,9},{9,8},{10,11... | collective-permute-start | bytes 3538952 | tf_op jit(solution)/shard_map/ppermute | solution.py:25
  437.1 125.4 %collective-permute-start.30 = (bf16[144,1152]{1,0:T(8,128)(2,1)}, bf16[144,1152]{1,0:T(8,128)(2,1)}, u32[]{:S(2)}, u32[]{:S(2)}) collective-permute-start(bf16[144,1152]{1,0:T(8,128)(2,1)} %add_convert_fusion.3), channel_id=1, source_target_pairs={{0,2},{1,3},{2,0},{3,1},{4,6},{5,7},{6,4},{7,5},{8,10},{9,11},{10,... | collective-permute-start | bytes 995336 | tf_op jit(solution)/shard_map/ppermute | solution.py:25
  444.8 77.8 %collective-permute-start.25 = (bf16[4,144,1152]{2,1,0:T(8,128)(2,1)}, bf16[4,144,1152]{2,1,0:T(8,128)(2,1)}, u32[]{:S(2)}, u32[]{:S(2)}) collective-permute-start(bf16[4,144,1152]{2,1,0:T(8,128)(2,1)} %dynamic-slice_bitcast_fusion), channel_id=1, source_target_pairs={{0,4},{4,0},{8,12},{12,8},{16,20},{20,16},{24,28},{28,24},{1,5},{5... | collective-permute-start | bytes 3981320 | tf_op jit(solution)/shard_map/ppermute | solution.py:25
  452.8 35.6 %collective-permute-start.39 = (bf16[2,144,1152]{2,1,0:T(8,128)(2,1)}, bf16[2,144,1152]{2,1,0:T(8,128)(2,1)}, u32[]{:S(2)}, u32[]{:S(2)}) collective-permute-start(bf16[2,144,1152]{2,1,0:T(8,128)(2,1)} %get-tuple-element.113), channel_id=1, source_target_pairs={{0,3},{1,2},{2,1},{3,0},{4,7},{5,6},{6,5},{7,4},{8,11},{9,10},{10,... | collective-permute-start | bytes 1990664 | tf_op jit(solution)/shard_map/ppermute | solution.py:25
  455.3 61.4 %collective-permute-start.38 = (bf16[2,144,1152]{2,1,0:T(8,128)(2,1)}, bf16[2,144,1152]{2,1,0:T(8,128)(2,1)}, u32[]{:S(2)}, u32[]{:S(2)}) collective-permute-start(bf16[2,144,1152]{2,1,0:T(8,128)(2,1)} %get-tuple-element.114), channel_id=1, source_target_pairs={{0,2},{1,3},{2,0},{3,1},{4,6},{5,7},{6,4},{7,5},{8,10},{9,11},{10,... | collective-permute-start | bytes 1990664 | tf_op jit(solution)/shard_map/ppermute | solution.py:25
  477.2 39.5 %collective-permute-start.37 = (bf16[2,144,1152]{2,1,0:T(8,128)(2,1)S(1)}, bf16[2,144,1152]{2,1,0:T(8,128)(2,1)}, u32[]{:S(2)}, u32[]{:S(2)}) collective-permute-start(bf16[2,144,1152]{2,1,0:T(8,128)(2,1)S(1)} %get-tuple-element.112), channel_id=1, source_target_pairs={{0,1},{1,0},{2,3},{3,2},{4,5},{5,4},{6,7},{7,6},{8,9},{9,8},{10,11... | collective-permute-start | bytes 1990664 | tf_op jit(solution)/shard_map/ppermute | solution.py:25
  485.8 34.6 %all-to-all-start = ((f32[32,2,216]{2,1,0:T(2,128)}), f32[32,2,216]{2,1,0:T(2,128)S(1)}, u32[]{:S(2)}, u32[]{:S(2)}) async-start(f32[32,2,216]{2,1,0:T(2,128)} %copy.139), calls=%async_computation | async-start | bytes 131072 | tf_op jit(solution)/shard_map/all_to_all | solution.py:615
  518.6 42.8 %collective-permute-start.41 = (bf16[2,144,1152]{2,1,0:T(8,128)(2,1)S(1)}, bf16[2,144,1152]{2,1,0:T(8,128)(2,1)}, u32[]{:S(2)}, u32[]{:S(2)}) collective-permute-start(bf16[2,144,1152]{2,1,0:T(8,128)(2,1)S(1)} %fusion.61), channel_id=1, source_target_pairs={{0,16},{4,20},{8,24},{12,28},{16,0},{20,4},{24,8},{28,12},{1,17},{... | collective-permute-start | bytes 1990664 | tf_op jit(solution)/shard_map/ppermute | solution.py:25
  519.3 51.8 %collective-permute-start.40 = (bf16[2,144,1152]{2,1,0:T(8,128)(2,1)S(1)}, bf16[2,144,1152]{2,1,0:T(8,128)(2,1)}, u32[]{:S(2)}, u32[]{:S(2)}) collective-permute-start(bf16[2,144,1152]{2,1,0:T(8,128)(2,1)S(1)} %fusion.61), channel_id=1, source_target_pairs={{0,8},{4,12},{8,0},{12,4},{16,24},{20,28},{24,16},{28,20},{1,9},{5... | collective-permute-start | bytes 1990664 | tf_op jit(solution)/shard_map/ppermute | solution.py:25
  525.6 32.8 %collective-permute-start.26 = (bf16[2,144,1152]{2,1,0:T(8,128)(2,1)}, bf16[2,144,1152]{2,1,0:T(8,128)(2,1)}, u32[]{:S(2)}, u32[]{:S(2)}) collective-permute-start(bf16[2,144,1152]{2,1,0:T(8,128)(2,1)} %pad_maximum_fusion.22), channel_id=1, source_target_pairs={{0,8},{4,12},{8,0},{12,4},{16,24},{20,28},{24,16},{28,20},{1,9},{5... | collective-permute-start | bytes 1990664 | tf_op jit(solution)/shard_map/ppermute | solution.py:25
  531.6 67.6 %all-to-all-start.1 = ((f32[32,1,9792]{2,1,0:T(1,128)}), f32[32,1,9792]{2,1,0:T(1,128)}, u32[]{:S(2)}, u32[]{:S(2)}) async-start(f32[32,1,9792]{2,1,0:T(1,128)} %all_to_all.10), calls=%async_computation.1 | async-start | bytes 2523136 | tf_op jit(solution)/shard_map/all_to_all | solution.py:672
  559.4 8.5 %collective-permute-start.27 = (bf16[144,1152]{1,0:T(8,128)(2,1)S(1)}, bf16[144,1152]{1,0:T(8,128)(2,1)S(1)}, u32[]{:S(2)}, u32[]{:S(2)}) collective-permute-start(bf16[144,1152]{1,0:T(8,128)(2,1)S(1)} %fusion.101), channel_id=1, source_target_pairs={{0,16},{4,20},{8,24},{12,28},{16,0},{20,4},{24,8},{28,12},{1,17},{... | collective-permute-start | bytes 995336 | tf_op jit(solution)/shard_map/ppermute | solution.py:25
  562.4 15.3 %collective-permute-start.43 = (bf16[144,1152]{1,0:T(8,128)(2,1)S(1)}, bf16[144,1152]{1,0:T(8,128)(2,1)S(1)}, u32[]{:S(2)}, u32[]{:S(2)}) collective-permute-start(bf16[144,1152]{1,0:T(8,128)(2,1)S(1)} %slice_bitcast_fusion.6), channel_id=1, source_target_pairs={{0,8},{4,12},{8,0},{12,4},{16,24},{20,28},{24,16},{28,20},{1,9},{5... | collective-permute-start | bytes 995336 | tf_op jit(solution)/shard_map/ppermute | solution.py:25
  569.2 7.8 %collective-permute-start.31 = (bf16[144,1152]{1,0:T(8,128)(2,1)S(1)}, bf16[144,1152]{1,0:T(8,128)(2,1)S(1)}, u32[]{:S(2)}, u32[]{:S(2)}) collective-permute-start(bf16[144,1152]{1,0:T(8,128)(2,1)S(1)} %add_convert_fusion.2), channel_id=1, source_target_pairs={{0,8},{4,12},{8,0},{12,4},{16,24},{20,28},{24,16},{28,20},{1,9},{5... | collective-permute-start | bytes 995336 | tf_op jit(solution)/shard_map/ppermute | solution.py:25
  572.1 10.3 %collective-permute-start.42 = (bf16[144,1152]{1,0:T(8,128)(2,1)S(1)}, bf16[144,1152]{1,0:T(8,128)(2,1)S(1)}, u32[]{:S(2)}, u32[]{:S(2)}) collective-permute-start(bf16[144,1152]{1,0:T(8,128)(2,1)S(1)} %slice_bitcast_fusion.7), channel_id=1, source_target_pairs={{0,16},{4,20},{8,24},{12,28},{16,0},{20,4},{24,8},{28,12},{1,17},{... | collective-permute-start | bytes 995336 | tf_op jit(solution)/shard_map/ppermute | solution.py:25
  572.3 14.2 %collective-permute-start.32 = (bf16[144,1152]{1,0:T(8,128)(2,1)S(1)}, bf16[144,1152]{1,0:T(8,128)(2,1)S(1)}, u32[]{:S(2)}, u32[]{:S(2)}) collective-permute-start(bf16[144,1152]{1,0:T(8,128)(2,1)S(1)} %add_convert_fusion.2), channel_id=1, source_target_pairs={{0,16},{4,20},{8,24},{12,28},{16,0},{20,4},{24,8},{28,12},{1,17},{... | collective-permute-start | bytes 995336 | tf_op jit(solution)/shard_map/ppermute | solution.py:25
  577.0 13.0 %collective-permute-start.33 = (bf16[144,1152]{1,0:T(8,128)(2,1)S(1)}, bf16[144,1152]{1,0:T(8,128)(2,1)S(1)}, u32[]{:S(2)}, u32[]{:S(2)}) collective-permute-start(bf16[144,1152]{1,0:T(8,128)(2,1)S(1)} %collective-permute-done.31), channel_id=1, source_target_pairs={{0,16},{4,20},{8,24},{12,28},{16,0},{20,4},{24,8},{28,12},{1,17},{... | collective-permute-start | bytes 995336 | tf_op jit(solution)/shard_map/ppermute | solution.py:25
  591.3 11.8 %collective-permute-start.34 = (bf16[4,144,1152]{2,1,0:T(8,128)(2,1)}, bf16[4,144,1152]{2,1,0:T(8,128)(2,1)}, u32[]{:S(2)}, u32[]{:S(2)}) collective-permute-start(bf16[4,144,1152]{2,1,0:T(8,128)(2,1)} %get-tuple-element.126), channel_id=1, source_target_pairs={{0,4},{4,0},{8,12},{12,8},{16,20},{20,16},{24,28},{28,24},{1,5},{5... | collective-permute-start | bytes 3981320 | tf_op jit(solution)/shard_map/ppermute | solution.py:25
  595.1 17.1 %collective-permute-start.44 = (bf16[4,2,144,1152]{3,2,1,0:T(8,128)(2,1)}, bf16[4,2,144,1152]{3,2,1,0:T(8,128)(2,1)}, u32[]{:S(2)}, u32[]{:S(2)}) collective-permute-start(bf16[4,2,144,1152]{3,2,1,0:T(8,128)(2,1)} %get-tuple-element.110), channel_id=1, source_target_pairs={{0,4},{4,0},{8,12},{12,8},{16,20},{20,16},{24,28},{28,24},{1,5},{5... | collective-permute-start | bytes 7962632 | tf_op jit(solution)/shard_map/ppermute | solution.py:25
  (93 other events, 931.4 us)

commit v3 on v2

--- a/solution.py
+++ b/solution.py
@@ -72,57 +72,6 @@
         end = min(-(-(h + 1) * HP // 128) * 128, width)
         found.append((base, end - base, h * HP - base))
     return found
-
-
-def attn_fwd_kernel(q_ref, k_ref, v_ref, ctx_ref, lse_ref, vt, ct):
-    rows, width = q_ref.shape
-    qb = 512
-    vt[...] = v_ref[...].T
-    for h, (base, size, lo) in enumerate(head_windows(width)):
-        win = slice(base, base + size)
-        lane = lax.broadcasted_iota(jnp.int32, (rows, size), 1)
-        here = (lane >= lo) & (lane < lo + HP)
-        km = jnp.where(here, k_ref[:, win], jnp.zeros((), BF))
-        head = slice(h * HP, (h + 1) * HP)
-        vth = vt[head, :]
-
-        def block(j, carry):
-            at = pl.ds(pl.multiple_of(j * qb, qb), qb)
-            s = dot(km, q_ref[at, win], 1, 1)
-            m = jnp.max(s, axis=0, keepdims=True) * SCALE2
-            e = jnp.exp2(s * SCALE2 - m)
-            total = jnp.sum(e, axis=0, keepdims=True)
-            c = dot(vth, e.astype(BF), 1, 0)
-            ct[head, at] = c / total
-            lse_ref[h, :, at] = m + jnp.log2(total)
-            return carry
-
-        lax.fori_loop(0, rows // qb, block, 0)
-    ctx_ref[...] = ct[...].T.astype(BF)
-
-
-def attn_fwd(q, k, v):
-    rows, width = q.shape
-    heads = width // HP
-    return pl.pallas_call(
-        attn_fwd_kernel,
-        out_shape=(
-            jax.ShapeDtypeStruct((rows, width), BF),
-            jax.ShapeDtypeStruct((heads, 1, rows), F32),
-        ),
-        in_specs=[pl.BlockSpec(memory_space=pltpu.VMEM)] * 3,
-        out_specs=[pl.BlockSpec(memory_space=pltpu.VMEM)] * 2,
-        scratch_shapes=[
-            pltpu.VMEM((width, rows), BF),
-            pltpu.VMEM((width, rows), F32),
-        ],
-        compiler_params=pltpu.CompilerParams(vmem_limit_bytes=40 << 20),
-        cost_estimate=pl.CostEstimate(
-            flops=4 * rows * rows * 256 * heads,
-            bytes_accessed=8 * rows * width,
-            transcendentals=rows * rows * heads,
-        ),
-    )(q, k, v)
 
 
 def attn_bwd_kernel(
@@ -190,6 +139,19 @@
     )(q, k, v, g, lse)
 
 
+PLACE = {0: 0, 1: 1, 3: 2, 2: 3}
+
+
+def flip(index, bit):
+    return index + bit - 2 * bit * lax.rem(index // bit, 2)
+
+
+def flips(index, bits):
+    for bit in (1, 2):
+        index = flip(index, bit) if bits & bit else index
+    return index
+
+
 def coords(index, n_mp):
     return index // n_mp, lax.rem(index, n_mp)
 
@@ -199,13 +161,64 @@
     pltpu.make_async_copy(whole, whole, sem).wait()
 
 
-def modulation_kernel(
-    per_dp, cond, ids, bias, w_ada, b_ada, mods, silu_out, ids_out, b1_out, bqv_out,
-    cond_all, ids_all, bias_all, send, land, sems,
+class Copies:
+    def __init__(self, sems):
+        self.sems, self.made = sems, {}
+
+    def make(self, name, src, dst, to):
+        k = 2 * len(self.made)
+        self.made[name] = pltpu.make_async_remote_copy(
+            src_ref=src,
+            dst_ref=dst,
+            send_sem=self.sems.at[k],
+            recv_sem=self.sems.at[k + 1],
+            device_id=to,
+            device_id_type=pl.DeviceIdType.MESH,
+        )
+        return self.made[name]
+
+    def beside(self, name, src, dst, to):
+        k = 2 * list(self.made).index(name)
+        return pltpu.make_async_remote_copy(
+            src_ref=src,
+            dst_ref=dst,
+            send_sem=self.sems.at[k],
+            recv_sem=self.sems.at[k + 1],
+            device_id=to,
+            device_id_type=pl.DeviceIdType.MESH,
+        )
+
+    def start(self, name, src, dst, to):
+        self.make(name, src, dst, to).start()
+
+    def arrived(self, name):
+        self.made[name].wait_recv()
+
+    def finish(self, but=()):
+        for name, made in self.made.items():
+            if name not in but:
+                made.wait_send()
+
+
+def front_kernel(
+    per_dp, cond, ids, bias, w_ada, b_ada, patches, cotangent, seg, watt_own, w_fc1, w_fc2, bqv_own, b_out,
+    silu_out, ids_out, b1_out, mods, x_row, q0, k0, v0, q1, k1, v1, c0, c1, l0, l1,
+    watt_other, w1_all, w2_all, attn_out, mlp2, gmo2,
+    cond_all, ids_all, bias_all, send, land, w1t, normed, out_send, out_land, vts, ct, bqv_other,
+    small, local, sems,
 ):
     n_dp, n_all, n_mp = cond_all.shape[0], ids_all.shape[0], bias_all.shape[0]
+    tokens, width = patches.shape
+    wide = watt_own.shape[1]
+    sixth = b1_out.shape[1]
+    half_w = wide // 2
     d, z = lax.axis_index("dp"), lax.axis_index("mp")
     me = d * n_mp + z
+    core, q = lax.rem(d, 2), lax.rem(d // 2, 4)
+    mid = (z == 1) | (z == 2)
+    at_z = [(d, z), (d, flip(z, 1)), (d, flip(z, 2)), (d, 3 - z)]
+    at_core, at_x, at_y = (flip(d, 1), z), (flip(d, 2), z), (flip(d, 4), z)
+    copies = Copies(sems)
     barrier = pltpu.get_barrier_semaphore()
 
     def greet(t, carry):
@@ -218,7 +231,7 @@
 
     def copy(src, dst, k, to):
         return pltpu.make_async_remote_copy(
-            src_ref=src, dst_ref=dst, send_sem=sems.at[2 * k], recv_sem=sems.at[2 * k + 1],
+            src_ref=src, dst_ref=dst, send_sem=small.at[2 * k], recv_sem=small.at[2 * k + 1],
             device_id=to, device_id_type=pl.DeviceIdType.MESH,
         )
 
@@ -237,14 +250,16 @@
     lax.fori_loop(1, n_dp, send_cond, 0)
     lax.fori_loop(1, n_all, send_ids, 0)
     lax.fori_loop(1, n_mp, send_bias, 0)
+
     cond_all[d] = cond[...]
     ids_all[me] = ids[...]
     bias_all[z] = bias[...]
+    w1t[...] = w_fc1[...].T
     for k, (ref, n) in enumerate(((cond_all, n_dp), (ids_all, n_all), (bias_all, n_mp))):
-        wait_all(ref, n - 1, sems.at[2 * k + 1])
+        wait_all(ref, n - 1, small.at[2 * k + 1])
 
     rows = n_dp * 8
-    c = cond_all[...].reshape(rows, cond_all.shape[2])
+    c = cond_all[...].reshape(rows, width)
     silu = (c * (1.0 / (1.0 + jnp.exp(-c)))).astype(BF)
     silu_out[...] = silu
     table = (dot(silu, w_ada[...], 1, 0) + b_ada[...]).astype(BF)
@@ -260,52 +275,313 @@
         return carry
 
     lax.fori_loop(1, n_all, send_rows, 0)
+    my_half = pl.ds(pl.multiple_of(core * half_w, 16), half_w)
+    copies.start("a_z", watt_own.at[q, my_half], watt_other.at[q, my_half], at_z[2])
+    w_in, w_all, ends = [w1t, w_fc2], [w1_all, w2_all], {}
+
+    def rows_of(i):
+        return pl.ds(pl.multiple_of((core * 4 + flips(q, i)) * sixth, 16), sixth)
+
+    for m in (1, 0):
+        copies.start(("w_z", m, 1), w_in[m].at[rows_of(0)], w_all[m].at[0, 1], at_z[1])
+        copies.make(("w_z", m, 3), w_in[m].at[rows_of(0)], w_all[m].at[0, 3], at_z[3])
+        copies.make(("w_z", m, 2), w_all[m].at[0, 1], w_all[m].at[0, 2], at_z[3])
+        ends[m] = [
+            copies.beside(("w_z", m, there), w_all[m].at[0, here], w_all[m].at[0, there], at_z[1])
+            for here, there in ((3, 2), (2, 3))
+        ]
+
+        @pl.when(mid)
+        def _():
+            copies.made["w_z", m, 3].start()
+
+    own = [
+        pltpu.make_async_copy(w_in[m].at[rows_of(i)], w_all[m].at[PLACE[i], 0], local.at[2 * i + m])
+        for i in range(4)
+        for m in range(2)
+    ]
+    for made in own:
+        made.start()
+
     land[me] = send[me]
     ids_out[...] = ids_all[...]
-    sixth = b1_out.shape[1]
-    core, q = lax.rem(d, 2), lax.rem(d // 2, 4)
     at = 0
     for i in ORDER:
         for j in range(n_mp):
-            quarter = jnp.bitwise_xor(q, i)
-            shard = jnp.bitwise_xor(z, j)
-            b1_out[at : at + 1, :] = bias_all[shard, pl.ds(core * 4 + quarter, 1), :sixth]
+            shard = 3 - z if j == 3 else flip(z, j) if j else z
+            b1_out[at : at + 1, :] = bias_all[shard, pl.ds(core * 4 + flips(q, i), 1), :sixth]
             at += 1
-    bqv_out[...] = bias_all[jnp.bitwise_xor(z, 2), 8:, :]
-    wait_all(land, n_all - 1, sems.at[7])
-    mods[...] = land[...]
+    bqv = bias_all[flip(z, 2), 8:, :]
+    heads = wide // HP
+    bqv_other[...] = jnp.zeros_like(bqv_other)
+    for h in range(heads):
+        bqv_other[:, h * HP : h * HP + HD] = bqv[:, h * HD : (h + 1) * HD]
+
+    step = 128
+
+    def norm(v):
+        centred = v - jnp.mean(v, axis=-1, keepdims=True)
+        spread = jnp.mean(centred * centred, axis=-1, keepdims=True)
+        return centred * lax.rsqrt(spread + 1e-06)
+
+    def norm_patches(t, carry):
+        part = pl.ds(pl.multiple_of(t * step, step), step)
+        normed[part, :] = norm(patches[part, :].astype(F32))
+        return carry
+
+    lax.fori_loop(0, tokens // step, norm_patches, 0)
+    copies.arrived("a_z")
+    copies.start("a_c", watt_other.at[q, my_half], watt_other.at[q, my_half], at_core)
+    wait_all(land, n_all - 1, small.at[7])
+    cols = land.shape[2]
+    for s in range(n_all):
+        mods[:, s * cols : (s + 1) * cols] = land[s]
+
+    def vector(b, which):
+        return mods[b : b + 1, which * width : (which + 1) * width]
+
+    for b in range(tokens // BLOCK):
+        shift, scale = vector(b, 0), 1.0 + vector(b, 1)
+
+        def modulate(t, carry):
+            part = pl.ds(pl.multiple_of(b * BLOCK + t * step, step), step)
+            x_row[part, :] = (normed[part, :] * scale + shift).astype(BF)
+            return carry
+
+        lax.fori_loop(0, BLOCK // step, modulate, 0)
+    mine, theirs = slice(0, tokens), slice(tokens, 2 * tokens)
+    copies.start("x", x_row.at[mine], x_row.at[theirs], at_z[1])
+    for b in range(tokens // BLOCK):
+        gate_mlp = vector(b, 5)
+
+        def scaled(t, carry):
+            part = pl.ds(pl.multiple_of(b * BLOCK + t * step, step), step)
+            gmo2[part, :] = (gate_mlp * cotangent[part, :].astype(F32)).astype(BF)
+            return carry
+
+        lax.fori_loop(0, BLOCK // step, scaled, 0)
+    copies.start("gmo", gmo2.at[mine], gmo2.at[theirs], at_core)
+
+    def w_near(j):
+        for m in (1, 0):
+            copies.arrived(("w_z", m, j))
+            if j == 1:
+
+                @pl.when(mid)
+                def _():
+                    copies.made["w_z", m, 2].start()
+
+            src = w_all[m].at[0, j]
+            copies.start(("w_x", m, j), src, w_all[m].at[PLACE[1], j], at_x)
+            copies.start(("w_y", m, j), src, w_all[m].at[PLACE[2], j], at_y)
+
+    def w_near_late(j):
+        @pl.when(jnp.logical_not(mid))
+        def _():
+            for m in (1, 0):
+                copies.arrived(("w_z", m, j))
+
+        for m in (1, 0):
+            src = w_all[m].at[0, j]
+            copies.start(("w_x", m, j), src, w_all[m].at[PLACE[1], j], at_x)
+            copies.start(("w_y", m, j), src, w_all[m].at[PLACE[2], j], at_y)
+
+    def w_far(j):
+        for m, way, i, to in ((0, "w_x", 1, at_y), (1, "w_y", 2, at_x)):
+            copies.arrived((way, m, j))
+            copies.start(
+                ("w_far", m, j), w_all[m].at[PLACE[i], j], w_all[m].at[PLACE[3], j], to
+            )
+
+    qx, qy = flips(q, 1), flips(q, 2)
+    low, high = slice(0, half_w), slice(half_w, wide)
+
+    lane = lax.rem(lax.broadcasted_iota(jnp.int32, (tokens, wide), 1), HP) - HD
+    slots = ((watt_own, bqv_own, q0, k0, v0, c0, l0), (watt_other, bqv_other, q1, k1, v1, c1, l1))
+
+    def project(slot, part):
+        watt, bqv, qr, kr, vr = slots[slot][:5]
+        x = x_row[part, :]
+        same = lane == seg[part, :]
+        marks = jnp.where(same, 1.0, 0.0)
+        qr[part, :] = (dot(x, watt[0], 1, 1) + bqv[0:1, :] + marks).astype(BF)
+        off = jnp.where((lane >= 0) & (lane < 4) & jnp.logical_not(same), MASKED, 0.0)
+        kr[part, :] = (dot(x, watt[1], 1, 1) + off).astype(BF)
+        vr[part, :] = (dot(x, watt[2], 1, 1) + bqv[1:2, :]).astype(BF)
+
+    qb = 256
+
+    def attend(slot, first, count):
+        qr, kr, _, _, lr = slots[slot][2:]
+        for h, (base, size, lo) in enumerate(head_windows(wide)):
+            win = slice(base, base + size)
+            ln = lax.broadcasted_iota(jnp.int32, (2 * tokens, size), 1)
+            km = jnp.where((ln >= lo) & (ln < lo + HP), kr[:, win], jnp.zeros((), BF))
+            head = slice(h * HP, (h + 1) * HP)
+            vth = vts[slot, head, :]
+
+            def block(j, carry):
+                at = pl.ds(pl.multiple_of(j * qb, qb), qb)
+                s = dot(km, qr[at, win], 1, 1)
+                m = jnp.max(s, axis=0, keepdims=True) * SCALE2
+                e = jnp.exp2(s * SCALE2 - m)
+                total = jnp.sum(e, axis=0, keepdims=True)
+                c = dot(vth, e.astype(BF), 1, 0)
+                ct[head, at] = c / total
+                lr[h, :, at] = m + jnp.log2(total)
+                return carry
+
+            lax.fori_loop(first, first + count, block, 0)
+        part = slice(first * qb, (first + count) * qb)
+        slots[slot][5][part, :] = ct[:, part].T.astype(BF)
+
+    def out_part(part):
+        return dot(c0[part, :], watt_own[3], 1, 0) + dot(c1[part, :], watt_other[3], 1, 0)
+
+    def att_plane():
+        copies.arrived("a_c")
+        copies.start("a_x", watt_other.at[q], watt_other.at[q], at_x)
+        copies.start("a_y", watt_other.at[q], watt_other.at[q], at_y)
+
+    def att_far():
+        copies.arrived("a_x")
+        copies.start("a_xy", watt_other.at[qx, low], watt_other.at[qx, low], at_y)
+        copies.arrived("a_y")
+        copies.start("a_yx", watt_other.at[qy, high], watt_other.at[qy, high], at_x)
+
+    def att_here():
+        copies.arrived("a_xy")
+        copies.arrived("a_yx")
+
+    att_plane()
+    project(0, mine)
+    w_near(1)
+    copies.arrived("x")
+
+    @pl.when(mid)
+    def _():
+        for m in (1, 0):
+            for j in (3, 2):
+                copies.arrived(("w_z", m, j))
+            for made in ends[m]:
+                made.start()
+
+    att_far()
+    project(0, theirs)
+    vts[0] = v0[...].T
+    n_peer = tokens // qb
+    attend(0, n_peer, n_peer)
+    att_here()
+    project(1, mine)
+    project(1, theirs)
+    vts[1] = v1[...].T
+    for t in range(n_peer):
+        attend(1, n_peer + t, 1)
+        part = slice(t * qb, (t + 1) * qb)
+        out_send[part, :] = out_part(slice(tokens + t * qb, tokens + (t + 1) * qb)).astype(BF)
+        copies.start(("out", t), out_send.at[part], out_land.at[part], at_z[1])
+        if t == 0:
+            w_far(1)
+    w_near_late(2)
+    attend(0, 0, n_peer)
+    w_near_late(3)
+    attend(1, 0, n_peer)
+    w_far(2)
+    attn_out[...] = out_part(mine) + b_out[...]
+    w_far(3)
+    for t in range(n_peer):
+        copies.arrived(("out", t))
+    for b in range(tokens // BLOCK):
+        gate, shift, scale = vector(b, 2), vector(b, 3), 1.0 + vector(b, 4)
+
+        def second(t, carry):
+            part = pl.ds(pl.multiple_of(b * BLOCK + t * step, step), step)
+            out = attn_out[part, :] + out_land[part, :].astype(F32)
+            attn_out[part, :] = out
+            resid = patches[part, :].astype(F32) + gate * out
+            mlp2[part, :] = (norm(resid) * scale + shift).astype(BF)
+            return carry
+
+        lax.fori_loop(0, BLOCK // step, second, 0)
+    copies.start("mlp", mlp2.at[mine], mlp2.at[theirs], at_core)
+    copies.arrived("mlp")
+    copies.arrived("gmo")
+    for j in (1, 2, 3):
+        for m in (1, 0):
+            copies.arrived((("w_y", "w_x")[m], m, j))
+            copies.arrived(("w_far", m, j))
+    for made in own:
+        made.wait()
+    copies.finish(but=[("w_z", m, j) for m in range(2) for j in (2, 3)])
+
+    @pl.when(mid)
+    def _():
+        for m in range(2):
+            for j in (2, 3):
+                copies.made["w_z", m, j].wait_send()
+            for made in ends[m]:
+                made.wait_send()
+
     for k, (ref, n) in enumerate(
         ((cond_all, n_dp), (ids_all, n_all), (bias_all, n_mp), (land, n_all))
     ):
-        wait_all(ref, n - 1, sems.at[2 * k])
-
-
-def modulation_rows(cond, ids, bias, w_ada, b_ada, n_dp, n_mp, sixth):
+        wait_all(ref, n - 1, small.at[2 * k])
+
+
+def front(cond, ids, bias, w_ada, b_ada, patches, cotangent, seg, watt_own, w_fc1, w_fc2, bqv_own, b_out):
+    n_dp, n_mp = lax.axis_size("dp"), lax.axis_size("mp")
     n_all, per_dp, width, cols = n_dp * n_mp, cond.shape[0], cond.shape[1], w_ada.shape[1]
+    tokens, wide = patches.shape[0], watt_own.shape[1]
+    sixth = w_fc2.shape[0] // 8
     cond8 = jnp.pad(cond.astype(F32), ((0, 8 - per_dp), (0, 0)))
     ids8 = jnp.pad(ids.astype(F32), (0, 8 - ids.shape[0]), constant_values=-1.0)
+    row = jax.ShapeDtypeStruct((2 * tokens, wide), BF)
+    lse = jax.ShapeDtypeStruct((wide // HP, 1, 2 * tokens), F32)
     shapes = (
-        jax.ShapeDtypeStruct((n_all, 8, cols), F32),
         jax.ShapeDtypeStruct((n_dp * 8, width), BF),
         jax.ShapeDtypeStruct((n_all, 8, 128), F32),
         jax.ShapeDtypeStruct((16, sixth), F32),
-        jax.ShapeDtypeStruct((8, bias.shape[1]), F32),
-    )
+        jax.ShapeDtypeStruct((8, 6 * width), F32),
+        jax.ShapeDtypeStruct((2 * tokens, width), BF),
+        *([row] * 8),
+        lse,
+        lse,
+        jax.ShapeDtypeStruct(watt_own.shape, BF),
+        jax.ShapeDtypeStruct((4, n_mp, sixth, width), BF),
+        jax.ShapeDtypeStruct((4, n_mp, sixth, width), BF),
+        jax.ShapeDtypeStruct((tokens, width), F32),
+        jax.ShapeDtypeStruct((2 * tokens, width), BF),
+        jax.ShapeDtypeStruct((2 * tokens, width), BF),
+    )
+    vmem, anywhere = pl.BlockSpec(memory_space=pltpu.VMEM), pl.BlockSpec(memory_space=pl.ANY)
+    in_specs = [vmem] * 13
+    in_specs[10] = anywhere
+    out_specs = [vmem] * len(shapes)
+    out_specs[16] = out_specs[17] = anywhere
     return pl.pallas_call(
-        functools.partial(modulation_kernel, per_dp),
+        functools.partial(front_kernel, per_dp),
         out_shape=shapes,
-        in_specs=[pl.BlockSpec(memory_space=pltpu.VMEM)] * 5,
-        out_specs=[pl.BlockSpec(memory_space=pltpu.VMEM)] * 5,
+        in_specs=in_specs,
+        out_specs=out_specs,
         scratch_shapes=[
             pltpu.VMEM((n_dp, 8, width), F32),
             pltpu.VMEM((n_all, 8, 128), F32),
             pltpu.VMEM((n_mp, *bias.shape), F32),
             pltpu.VMEM((n_all, 8, cols), F32),
             pltpu.VMEM((n_all, 8, cols), F32),
+            pltpu.VMEM((w_fc1.shape[1], width), BF),
+            pltpu.VMEM((tokens, width), F32),
+            pltpu.VMEM((tokens, width), BF),
+            pltpu.VMEM((tokens, width), BF),
+            pltpu.VMEM((2, wide, 2 * tokens), BF),
+            pltpu.VMEM((wide, 2 * tokens), F32),
+            pltpu.VMEM((8, wide), F32),
             pltpu.SemaphoreType.DMA((8,)),
+            pltpu.SemaphoreType.DMA((8,)),
+            pltpu.SemaphoreType.DMA((96,)),
         ],
         compiler_params=pltpu.CompilerParams(
-            collective_id=0, has_side_effects=True, vmem_limit_bytes=32 << 20
+            collective_id=0, has_side_effects=True, vmem_limit_bytes=62 << 20
         ),
     )(
         cond8,
@@ -313,6 +589,14 @@
         bias,
         w_ada,
         b_ada.astype(F32)[None],
+        patches,
+        cotangent,
+        seg,
+        watt_own,
+        w_fc1,
+        w_fc2,
+        bqv_own,
+        b_out.astype(F32)[None],
     )
 
 
@@ -360,43 +644,9 @@
     q = (d >> 1) & 3
     sixth = shard // 8
 
-    def quarter(w1, w2, i):
-        at = (core * 4 + (q ^ i)) * sixth
-        return jnp.stack(
-            [
-                lax.dynamic_slice_in_dim(w1, at, sixth, 1).T,
-                lax.dynamic_slice_in_dim(w2, at, sixth, 0),
-            ]
-        )
-
-    first = quarter(w_fc1, w_fc2, 0)
-
     heads_shard = w_out.shape[0]
-    watt_own = jnp.concatenate([w_qkv.transpose(0, 2, 1), w_out[None]], axis=0)
-    p2 = d & 3
-    got0 = swap(pick(watt_own, p2), "mp", 2)
-    got1 = swap(got0, "dp", 1)
-    got23 = swap(jnp.stack([got0, got1]), "dp", 2)
-    got = jnp.stack([got0, got1, got23[0], got23[1]])
-    watt_other = jnp.stack([pick(got, p2 ^ m) for m in range(4)])
-    watts = [pad_heads(watt_own), pad_heads(watt_other)]
-    wide = watts[0].shape[1]
-
-    z1 = swap(first, "mp", 1)
-    later = after(first, got0)
-    groups = [z1[:, None], jnp.stack([swap(later, "mp", 2), swap(later, "mp", 3)], axis=1)]
-
-    def over_plane(group):
-        from_x = swap(group, "dp", 2)
-        from_y = swap(group, "dp", 4)
-        return from_x, from_y
-
-    def far_side(from_x, from_y):
-        return swap(from_x[0], "dp", 4), swap(from_y[1], "dp", 2)
-
-    near_1 = over_plane(groups[0])
-    far_1 = far_side(*near_1)
-
+    watt_own = pad_heads(jnp.concatenate([w_qkv.transpose(0, 2, 1), w_out[None]], axis=0))
+    wide = watt_own.shape[1]
     ids = image_ids.reshape(n_blocks, BLOCK)[:, 0]
     cols = w_ada.shape[1]
     bias = jnp.concatenate(
@@ -405,12 +655,23 @@
             jnp.pad(b_qv.astype(F32), ((0, 6), (0, 0))),
         ]
     )
-    mod_rows, silu_cond, ids_all, b1_rel, bqv_other = modulation_rows(
-        conditioning, ids, bias, w_ada, b_ada, n_dp, n_mp, sixth
-    )
+    bqv_own = jnp.pad(pad_heads(b_qv[..., None])[..., 0].astype(F32), ((0, 6), (0, 0)))
+    seg_own = lax.dynamic_slice_in_dim(segment, z * tokens, tokens, 0)
+    seg_peer = lax.dynamic_slice_in_dim(segment, (z ^ 1) * tokens, tokens, 0)
+    seg = jnp.concatenate([seg_own, seg_peer])[:, None]
+    (
+        silu_cond, ids_all, b1_rel, mods, x_row, q0, k0, v0, q1, k1, v1, ctx_0, ctx_1,
+        lse_0, lse_1, watt_other, w1_all, w2_all, attn_out, mlp2, gmo2,
+    ) = front(
+        conditioning, ids, bias, w_ada, b_ada, patches, cotangent, seg, watt_own, w_fc1, w_fc2,
+        bqv_own, b_out,
+    )
+    heads_0, heads_1 = (q0, k0, v0), (q1, k1, v1)
+    watts = [watt_own, watt_other]
+    outs = [watt_own[3], watt_other[3]]
+    w1_all, w2_all = [w.reshape(16 * sixth, width) for w in (w1_all, w2_all)]
     b1_all = b1_rel.reshape(16 * sixth)
-    bqvs = [pad_heads(v[..., None])[..., 0].astype(F32) for v in (b_qv, bqv_other[:2])]
-    mods = mod_rows[:, :n_blocks].transpose(1, 0, 2).reshape(n_blocks, 6, width)
+    mods = mods[:n_blocks].reshape(n_blocks, 6, width)
     shift_attn, scale_attn, gate_attn, shift_mlp, scale_mlp, gate_mlp = [
         mods[:, i, None, :] for i in range(6)
     ]
@@ -424,58 +685,11 @@
     patch_wide = blocks(patches.astype(F32))
     grad_output = blocks(cotangent.astype(F32))
     norm_a, rsig_a = layer_norm(patch_wide)
-    attn_in = flat((norm_a * (1.0 + scale_attn) + shift_attn).astype(BF))
-    x_row = jnp.concatenate([attn_in, swap(attn_in, "mp", 1)], axis=0)
-
-    seg_own = lax.dynamic_slice_in_dim(segment, z * tokens, tokens, 0)
-    seg_peer = lax.dynamic_slice_in_dim(segment, (z ^ 1) * tokens, tokens, 0)
-    seg = jnp.concatenate([seg_own, seg_peer])[:, None]
-    slot = lax.broadcasted_iota(jnp.int32, (1, wide), 1) % HP - HD
-    mark_q = jnp.where(slot == seg, 1.0, 0.0)
-    mark_k = jnp.where((slot >= 0) & (slot < 4) & (slot != seg), MASKED, 0.0)
-
-    def project(watt, bqv, rows_in):
-        proj = dot(rows_in, watt[:3].reshape(3 * wide, width), 1, 1)
-        qh = (proj[:, :wide] + bqv[0] + mark_q).astype(BF)
-        kh = (proj[:, wide : 2 * wide] + mark_k).astype(BF)
-        return qh, kh, (proj[:, 2 * wide :] + bqv[1]).astype(BF)
-
-    heads_0 = project(watts[0], bqvs[0], x_row)
-    ctx_0, lse_0 = attn_fwd(*heads_0)
-    near_2 = over_plane(after(groups[1], heads_0[0]))
-    heads_1 = project(watts[1], bqvs[1], after(x_row, ctx_0))
-    ctx_1, lse_1 = attn_fwd(*heads_1)
-    outs = [watts[0][3], watts[1][3]]
-
-    def out_part(at):
-        return dot(ctx_0[at], outs[0], 1, 0) + dot(ctx_1[at], outs[1], 1, 0)
-
-    out_send = out_part(slice(tokens, None)).astype(BF)
-    far_2 = far_side(*[after(v, out_send) for v in near_2])
-    out_peer = swap(out_send, "mp", 1)
-    attn_out = blocks(
-        out_part(slice(0, tokens)) + out_peer.astype(F32) + b_out.astype(F32)
-    )
-    w1_late, w2_late = lax.optimization_barrier((w_fc1, w_fc2, attn_in))[:2]
-    own = [first] + [quarter(w1_late, w2_late, i) for i in (1, 2, 3)]
-    nears = [jnp.concatenate([a, b], axis=1) for a, b in zip(near_1, near_2)]
-    fars = [jnp.concatenate([a, b], axis=0) for a, b in zip(far_1, far_2)]
-    from_z = jnp.concatenate(groups, axis=1)
-
-    def laid_out(m):
-        pieces = [own[0][m][None], from_z[m], own[1][m][None], nears[0][m]]
-        pieces += [own[3][m][None], fars[m], own[2][m][None], nears[1][m]]
-        return jnp.concatenate(pieces, axis=0).reshape(16 * sixth, width)
-
-    w1_all = laid_out(0)
-    w2_all = laid_out(1)
+    attn_out = blocks(attn_out)
     resid = patch_wide + gate_attn * attn_out
     norm_m, rsig_m = layer_norm(resid)
-    mlp_in = flat((norm_m * (1.0 + scale_mlp) + shift_mlp).astype(BF))
-
-    gmo = flat((gate_mlp * grad_output).astype(BF))
-    gmo2 = jnp.concatenate([gmo, swap(gmo, "dp", 1)], axis=0)
-    mlp2 = jnp.concatenate([mlp_in, swap(mlp_in, "dp", 1)], axis=0)
+
+    gmo = gmo2[:tokens]
     pre = dot(mlp2, w1_all, 1, 1) + b1_all
     act, act_grad = gelu_parts(pre)
     hidden = act.astype(BF)

time: 641 us -> 600 us (0.936)
  Pallas kernels: 83.1 us -> 181 us
  waiting for transfers between devices: 191 us -> 123 us
  matrix products: 147 us -> 126 us
  starting transfers between devices: 47.7 us -> 30.1 us
  local copies, waits for them, and re-layouts: 76.2 us -> 61.3 us
  other arithmetic: 82.1 us -> 68.8 us
    pallas_call x3 -> x1, Pallas kernels: 52.2 us -> 150 us  [front(): pl.pallas_call(functools.partial(front_kernel, per_dp), out_shape=shapes,...]
    ppermute x45 -> x27, waiting for transfers between devices: 191 us -> 121 us  [swap(): return lax.ppermute(value, axis, [(i, i ^ bit) for i in range(n)])]
    dot_general x35 -> x29, matrix products: 146 us -> 124 us  [dot(): lax.dot_general(a, b, (((ca,), (cb,)), ((), ())), preferred_element_type=...]
    ppermute x45 -> x27, starting transfers between devices: 41.4 us -> 23.5 us  [swap(): return lax.ppermute(value, axis, [(i, i ^ bit) for i in range(n)])]
    unnamed x215 -> x210, local copies, waits for them, and re-layouts: 36.1 us -> 19.2 us
    concatenate x6 -> x1, other arithmetic: 15 us -> 3.59 us  [on_device(): jnp.concatenate([w_qkv.transpose(0, 2, 1), w_out[None]], axis=0)]
    optimization_barrier x2 -> x0, local copies, waits for them, and re-layouts: 8.32 us -> none  [the longest x1 5.23 us: on_device(): w1_late, w2_late = lax.optimization_barrier((w_fc1, w_fc2, attn_in))[:2]]
  transfers between devices with their start and end apart: 47 -> 29, of which waited for: 16 -> 12; matrix products, arithmetic and copies ran while one was open for 34% -> 30% of each run, Pallas kernels for 10% -> 5%
where the time goes in v3:
time: 600 us; the launch traced here: 592 us
  Pallas kernels  181 us (30%)
  matrix products  126 us (21%)
  waiting for transfers between devices  123 us (20%)
  other arithmetic  68.8 us (11%)
  local copies, waits for them, and re-layouts  61.3 us (10%)
  starting transfers between devices  30.1 us (5%)
    pallas_call x1, Pallas kernels, front(): pl.pallas_call(functools.partial(front_kernel, per_dp), out_shape=shapes,...  150 us
    dot_general x29, matrix products, dot(): lax.dot_general(a, b, (((ca,), (cb,)), ((), ())), preferred_element_type=...  124 us
    ppermute x27, waiting for transfers between devices, swap(): return lax.ppermute(value, axis, [(i, i ^ bit) for i in range(n)])  121 us
    pallas_call x2, Pallas kernels, attn_bwd(): pl.pallas_call(attn_bwd_kernel, out_shape=(shape, shape, shape), in_specs...  31 us
    ppermute x27, starting transfers between devices, swap(): return lax.ppermute(value, axis, [(i, i ^ bit) for i in range(n)])  23.5 us
    unnamed x210, local copies, waits for them, and re-layouts  19.2 us
  transfers between devices with their start and end apart: 29, of which 12 were waited for; matrix products, arithmetic and copies ran while one was open for 30% of the time, Pallas kernels for 5%

profile of v3, /device:TPU:0, one launch (start us, length us, event | category | flops | bytes accessed | tf_op | source)
XLA Modules:
  0.0 592.5 jit_solution(16227034197906656779)
XLA Ops:
  11.5 3.6 fusion.13
  16.4 150.3 %shard_map.246 = (bf16[64,1152]{1,0:T(8,128)(2,1)}, f32[32,8,128]{2,1,0:T(8,128)}, f32[16,144]{1,0:T(8,128)}, f32[8,6912]{1,0:T(8,128)}, bf16[1024,1152]{1,0:T(8...) custom-call(f32[8,1152]{1,0:T(8,128)} %pad.32.cond, ...), custom_call_target="tpu_custom_call" | custom-call | tf_op jit(solution)/shard_map/pallas_call | solution.py:561
  167.5 13.1 %multiply_convert_fusion = (bf16[1024,2304]{1,0:T(8,128)(2,1)S(1)}, f32[1024,2304]{1,0:T(8,128)}) fusion(f32[2304]{0:T(1024)S(1)} %add.363, bf16[1024,1152]{1,0:T(8,128)(2,1)} %get-tuple-element.63, bf16[2304,1152]{1,0:T(8,128)(2,1)} %bitcast.248), kind=kOutput, calls=%fused_computation.11 | convolution fusion | flops 5459410944 | bytes 21832704 | tf_op jit(solution)/shard_map/dot_general | solution.py:29
  180.6 5.3 convolution_convert_fusion.1
  186.7 13.8 %convert_reduce_fusion = (f32[2304]{0:T(1024)}, bf16[1024,2304]{1,0:T(8,128)(2,1)S(1)}) fusion(f32[1024,2304]{1,0:T(8,128)} %get-tuple-element.133, f32[2304]{0:T(1024)S(1)} %add.363, bf16[1024,1152]{1,0:T(8,128)(2,1)S(1)} %copy-done.13, bf16[2304,1152]{1,0:T(8,128)(2,1)S(1)} %bitcast.247), kind=kOutput, calls=%fused_computation.10 | convolution fusion | flops 5487720448 | bytes 21841920 | tf_op jit(solution)/shard_map/dot_general | solution.py:29
  200.5 4.2 convolution_convert_fusion.5
  204.8 4.8 convolution_convert_fusion
  216.7 3.0 fusion.123
  224.0 3.2 slice.259
  228.4 3.1 slice.210
  236.5 7.1 %fusion.41 = (f32[512]{0:T(512)S(1)}, f32[512]{0:T(512)S(1)}, f32[512,1152]{1,0:T(8,128)S(1)}) fusion(f32[2,1152]{1,0:T(2,128)S(1)} %get-tuple-element.143, f32[512]{0:T(512)S(1)} %add_rsqrt_fusion.1, f32[512,1152]{1,0:T(8,128)S(1)} %get-tuple-element.106, f32[512]{0:T(512)S(1)} %broadcast_multiply_fusion.4, bf16[512,1152]{1,0:T(8,128)(2,1)} %collective-permute-done, ...), kind=kOutput, calls=%fused_computation.108 | convolution fusion | flops 2722626560 | bytes 13583360 | tf_op jit(solution)/shard_map/dot_general | solution.py:29
  243.7 2.9 convert_reduce_fusion.2
  246.7 7.9 %convolution_convert_fusion.4 = bf16[512,1152]{1,0:T(8,128)(2,1)} fusion(bf16[2304,1152]{1,0:T(8,128)(2,1)} %bitcast.245, bf16[1024,2304]{1,0:T(8,128)(2,1)} %copy-done.36), kind=kOutput, calls=%fused_computation.37 | convolution fusion | flops 2718498816 | bytes 8847360 | tf_op jit(solution)/shard_map/dot_general | solution.py:29
  254.8 3.3 fusion.34
  258.1 4.9 fusion.55
  263.0 2.7 fusion.125
  265.8 9.0 %collective-permute-done.2 = bf16[512,1152]{1,0:T(8,128)(2,1)S(1)} collective-permute-done((bf16[512,1152]{1,0:T(8,128)(2,1)S(1)}, bf16[512,1152]{1,0:T(8,128)(2,1)S(1)}, u32[]{:S(2)}, u32[]{:S(2)}) %collective-permute-start.2) | collective-permute-done | bytes 1179680 | tf_op jit(solution)/shard_map/ppermute | solution.py:25
  280.6 15.4 %shard_map.247 = (bf16[1024,320]{1,0:T(8,128)(2,1)S(1)}, bf16[1024,320]{1,0:T(8,128)(2,1)S(1)}, bf16[1024,320]{1,0:T(8,128)(2,1)S(1)}) custom-call(bf16[1024,320]{1,0:T(8,128)(2,1)S(1)} %copy-done.3, bf16[1024,320]{1,0:T(8,128)(2,1)S(1)} %copy-done.4, bf16[1024,320]{1,0:T(8,128)(2,1)S(1)} %copy-done.5, bf16[1024,320]{1,0:T(8,128)(2,1)S(1)} %copy.66.g_ref, ...), custom_call_target="tpu_custom_call" | custom-call | flops 10737418240 | bytes 4587520 | tf_op jit(solution)/shard_map/pallas_call | solution.py:122
  297.7 2.8 convolution_convert_fusion.3
  304.9 4.5 fusion.53
  311.9 9.3 %fusion.33 = (bf16[512,1152]{1,0:T(8,128)(2,1)}, f32[512,1152]{1,0:T(8,128)}) fusion(f32[512,1152]{1,0:T(8,128)} %copy-done.8, f32[2,1152]{1,0:T(2,128)S(1)} %bitcast.277, f32[1152]{0:T(1024)S(1)} %convert_element_type.333, bf16[512,1152]{1,0:T(8,128)(2,1)} %collective-permute-done.1, bf16[2304,1152]{1,0:T(8,128)(2,1)} %bitcast.246, ...), kind=kOutput, calls=%fused_computation.85 | convolution fusion | flops 2721447936 | bytes 14759424 | tf_op jit(solution)/shard_map/dot_general | solution.py:29
  327.5 2.8 fusion.16
  331.6 12.8 %collective-permute-done.10 = bf16[2,144,1152]{2,1,0:T(8,128)(2,1)S(1)} collective-permute-done((bf16[2,144,1152]{2,1,0:T(8,128)(2,1)S(1)}, bf16[2,144,1152]{2,1,0:T(8,128)(2,1)S(1)}, u32[]{:S(2)}, u32[]{:S(2)}) %collective-permute-start.10) | collective-permute-done | bytes 663584 | tf_op jit(solution)/shard_map/ppermute | solution.py:25
  345.4 3.0 fusion.20
  349.6 5.7 collective-permute-done.11
  358.8 15.6 %shard_map.248 = (bf16[1024,320]{1,0:T(8,128)(2,1)S(1)}, bf16[1024,320]{1,0:T(8,128)(2,1)S(1)}, bf16[1024,320]{1,0:T(8,128)(2,1)S(1)}) custom-call(bf16[1024,320]{1,0:T(8,128)(2,1)S(1)} %copy-done, bf16[1024,320]{1,0:T(8,128)(2,1)S(1)} %copy-done.1, bf16[1024,320]{1,0:T(8,128)(2,1)S(1)} %copy-done.2, bf16[1024,320]{1,0:T(8,128)(2,1)S(1)} %copy.67.g_ref, ...), custom_call_target="tpu_custom_call" | custom-call | flops 10737418240 | bytes 4587520 | tf_op jit(solution)/shard_map/pallas_call | solution.py:122
  374.5 7.5 %collective-permute-done.18 = bf16[4,144,1152]{2,1,0:T(8,128)(2,1)} collective-permute-done((bf16[4,144,1152]{2,1,0:T(8,128)(2,1)}, bf16[4,144,1152]{2,1,0:T(8,128)(2,1)}, u32[]{:S(2)}, u32[]{:S(2)}) %collective-permute-start.18) | collective-permute-done | bytes 1327136 | tf_op jit(solution)/shard_map/ppermute | solution.py:25
  388.6 2.6 collective-permute-start.20
  393.5 2.8 convolution_convert_fusion.2
  396.8 2.3 copy-done.42
  401.4 2.6 fusion.12
  406.5 2.9 fusion.63
  409.4 48.1 %collective-permute-done.6 = bf16[512,1152]{1,0:T(8,128)(2,1)} collective-permute-done((bf16[512,1152]{1,0:T(8,128)(2,1)}, bf16[512,1152]{1,0:T(8,128)(2,1)}, u32[]{:S(2)}, u32[]{:S(2)}) %collective-permute-start.6) | collective-permute-done | bytes 1179680 | tf_op jit(solution)/shard_map/ppermute | solution.py:25
  458.9 3.9 fusion.42
  462.8 3.3 fusion.31
  472.8 3.2 all-to-all-start
  476.1 2.9 fusion.52
  494.3 3.6 all_to_all.10
  497.8 3.4 all-to-all-start.1
  501.3 15.7 %collective-permute-done.8 = bf16[2,144,1152]{2,1,0:T(8,128)(2,1)} collective-permute-done((bf16[2,144,1152]{2,1,0:T(8,128)(2,1)}, bf16[2,144,1152]{2,1,0:T(8,128)(2,1)}, u32[]{:S(2)}, u32[]{:S(2)}) %collective-permute-start.8) | collective-permute-done | bytes 663584 | tf_op jit(solution)/shard_map/ppermute | solution.py:25
  521.2 11.0 %collective-permute-done.9 = bf16[144,1152]{1,0:T(8,128)(2,1)S(1)} collective-permute-done((bf16[144,1152]{1,0:T(8,128)(2,1)S(1)}, bf16[144,1152]{1,0:T(8,128)(2,1)S(1)}, u32[]{:S(2)}, u32[]{:S(2)}) %collective-permute-start.9) | collective-permute-done | bytes 331808 | tf_op jit(solution)/shard_map/ppermute | solution.py:25
  533.6 2.3 collective-permute-start.13
  539.0 4.1 collective-permute-done.13
  548.4 3.6 collective-permute-done.15
  553.7 3.9 pad_maximum_fusion.5
  572.1 2.6 fusion.43
  577.0 6.5 %fusion.10 = f32[1152,1152]{1,0:T(8,128)} fusion(bf16[1152,1152]{1,0:T(8,128)(2,1)S(1)} %bitcast.258, s32[1152]{0:T(1024)S(1)} %copy-done.72), kind=kOutput, calls=%fused_computation.20 | convolution fusion | flops 3058974720 | bytes 7967232 | tf_op jit(solution)/shard_map/dot_general | solution.py:29
  583.5 6.5 %fusion.11 = f32[1152,1152]{1,0:T(8,128)} fusion(bf16[1152,1152]{1,0:T(8,128)(2,1)S(1)} %bitcast.257, s32[1152]{0:T(1024)S(1)} %copy-done.72), kind=kOutput, calls=%fused_computation.21 | convolution fusion | flops 3058974720 | bytes 7967232 | tf_op jit(solution)/shard_map/dot_general | solution.py:29
  (382 shorter events, 130.6 us)
Async XLA Ops:
  167.5 13.2 %copy-start.13 = (bf16[1024,1152]{1,0:T(8,128)(2,1)S(1)}, bf16[1024,1152]{1,0:T(8,128)(2,1)}, u32[]{:S(2)}) copy-start(bf16[1024,1152]{1,0:T(8,128)(2,1)} %get-tuple-element.83) | copy-start | bytes 7077892
  180.6 19.9 %slice-start = ((s8[5308416]{0:T(1024)(128)(4,1)}), s8[4194304]{0:T(1024)(128)(4,1)S(1)}, s32[]{:S(2)}) async-start(s8[5308416]{0:T(1024)(128)(4,1)} %bitcast.250), calls=%async_computation.2 | async-start | bytes 8388608
  185.9 137.4 %collective-permute-start.3 = (bf16[2,4,144,1152]{3,2,1,0:T(8,128)(2,1)}, bf16[2,4,144,1152]{3,2,1,0:T(8,128)(2,1)}, u32[]{:S(2)}, u32[]{:S(2)}) collective-permute-start(bf16[2,4,144,1152]{3,2,1,0:T(8,128)(2,1)} %bitcast.9), channel_id=1, source_target_pairs={{0,8},{4,12},{8,0},{12,4},{16,24},{20,28},{24,16},{28,20},{1,9},{5... | collective-permute-start | bytes 7962632 | tf_op jit(solution)/shard_map/ppermute | solution.py:25
  186.7 13.8 %slice-start.1 = ((s8[5308416]{0:T(1024)(128)(4,1)}), s8[1114112]{0:T(1024)(128)(4,1)S(1)}, s32[]{:S(2)}) async-start(s8[5308416]{0:T(1024)(128)(4,1)} %bitcast.250), calls=%async_computation.3 | async-start | bytes 2228224
  204.8 31.7 %collective-permute-start = (bf16[512,1152]{1,0:T(8,128)(2,1)}, bf16[512,1152]{1,0:T(8,128)(2,1)}, u32[]{:S(2)}, u32[]{:S(2)}) collective-permute-start(bf16[512,1152]{1,0:T(8,128)(2,1)} %convolution_convert_fusion.5), channel_id=1, source_target_pairs={{0,4},{4,0},{8,12},{12,8},{16,20},{20,16},{24,28},{28,24},{1,5},{5... | collective-permute-start | bytes 3538952 | tf_op jit(solution)/shard_map/ppermute | solution.py:25
  209.6 113.7 %collective-permute-start.4 = (bf16[2,4,144,1152]{3,2,1,0:T(8,128)(2,1)}, bf16[2,4,144,1152]{3,2,1,0:T(8,128)(2,1)}, u32[]{:S(2)}, u32[]{:S(2)}) collective-permute-start(bf16[2,4,144,1152]{3,2,1,0:T(8,128)(2,1)} %bitcast.13), channel_id=1, source_target_pairs={{0,16},{4,20},{8,24},{12,28},{16,0},{20,4},{24,8},{28,12},{1,17},{... | collective-permute-start | bytes 7962632 | tf_op jit(solution)/shard_map/ppermute | solution.py:25
  219.7 23.9 %copy-start.8 = (f32[512,1152]{1,0:T(8,128)}, f32[512,1152]{1,0:T(8,128)S(1)}, u32[]{:S(2)}) copy-start(f32[512,1152]{1,0:T(8,128)S(1)} %get-tuple-element.106) | copy-start | bytes 7077892
  220.4 12.3 %copy-start.67 = (f32[512]{0:T(512)}, f32[512]{0:T(512)S(1)}, u32[]{:S(2)}) copy-start(f32[512]{0:T(512)S(1)} %add_rsqrt_fusion) | copy-start | bytes 6148
  246.6 28.2 %copy-start.37 = (bf16[512,1152]{1,0:T(8,128)(2,1)}, bf16[512,1152]{1,0:T(8,128)(2,1)S(1)}, u32[]{:S(2)}) copy-start(bf16[512,1152]{1,0:T(8,128)(2,1)S(1)} %get-tuple-element.102) | copy-start | bytes 3538948
  246.6 28.2 %collective-permute-start.2 = (bf16[512,1152]{1,0:T(8,128)(2,1)S(1)}, bf16[512,1152]{1,0:T(8,128)(2,1)S(1)}, u32[]{:S(2)}, u32[]{:S(2)}) collective-permute-start(bf16[512,1152]{1,0:T(8,128)(2,1)S(1)} %get-tuple-element.102), channel_id=1, source_target_pairs={{0,1},{1,0},{2,3},{3,2},{4,5},{5,4},{6,7},{7,6},{8,9},{9,8},{10,11... | collective-permute-start | bytes 3538952 | tf_op jit(solution)/shard_map/ppermute | solution.py:25
  254.6 57.2 %collective-permute-start.1 = (bf16[512,1152]{1,0:T(8,128)(2,1)}, bf16[512,1152]{1,0:T(8,128)(2,1)}, u32[]{:S(2)}, u32[]{:S(2)}) collective-permute-start(bf16[512,1152]{1,0:T(8,128)(2,1)} %convolution_convert_fusion.4), channel_id=1, source_target_pairs={{0,4},{4,0},{8,12},{12,8},{16,20},{20,16},{24,28},{28,24},{1,5},{5... | collective-permute-start | bytes 3538952 | tf_op jit(solution)/shard_map/ppermute | solution.py:25
  265.8 12.6 %copy-start.3 = (bf16[1024,320]{1,0:T(8,128)(2,1)S(1)}, bf16[1024,320]{1,0:T(8,128)(2,1)}, u32[]{:S(2)}) copy-start(bf16[1024,320]{1,0:T(8,128)(2,1)} %get-tuple-element.64.q_ref) | copy-start | bytes 1966084
  265.8 12.6 %copy-start.7 = (f32[4,1,1024]{2,1,0:T(1,128)S(1)}, f32[4,1,1024]{2,1,0:T(1,128)}, u32[]{:S(2)}) copy-start(f32[4,1,1024]{2,1,0:T(1,128)} %get-tuple-element.68.lse_ref) | copy-start | bytes 49156
  304.7 18.6 %collective-permute-start.5 = (bf16[4,144,1152]{2,1,0:T(8,128)(2,1)}, bf16[4,144,1152]{2,1,0:T(8,128)(2,1)}, u32[]{:S(2)}, u32[]{:S(2)}) collective-permute-start(bf16[4,144,1152]{2,1,0:T(8,128)(2,1)} %dynamic-slice_bitcast_fusion.1), channel_id=1, source_target_pairs={{0,4},{4,0},{8,12},{12,8},{16,20},{20,16},{24,28},{28,24},{1,5},{5... | collective-permute-start | bytes 3981320 | tf_op jit(solution)/shard_map/ppermute | solution.py:25
  311.8 9.4 %copy-start.48 = (bf16[512,1152]{1,0:T(8,128)(2,1)S(1)}, bf16[512,1152]{1,0:T(8,128)(2,1)}, u32[]{:S(2)}) copy-start(bf16[512,1152]{1,0:T(8,128)(2,1)} %copy-done.46) | copy-start | bytes 3538948
  311.8 9.4 %copy-start.89 = (bf16[1024,320]{1,0:T(8,128)(2,1)S(1)}, bf16[1024,320]{1,0:T(8,128)(2,1)}, u32[]{:S(2)}) copy-start(bf16[1024,320]{1,0:T(8,128)(2,1)} %get-tuple-element.82) | copy-start | bytes 1966084
  326.7 17.8 %collective-permute-start.10 = (bf16[2,144,1152]{2,1,0:T(8,128)(2,1)S(1)}, bf16[2,144,1152]{2,1,0:T(8,128)(2,1)S(1)}, u32[]{:S(2)}, u32[]{:S(2)}) collective-permute-start(bf16[2,144,1152]{2,1,0:T(8,128)(2,1)S(1)} %pad_maximum_fusion.13), channel_id=1, source_target_pairs={{0,16},{4,20},{8,24},{12,28},{16,0},{20,4},{24,8},{28,12},{1,17},{... | collective-permute-start | bytes 1990664 | tf_op jit(solution)/shard_map/ppermute | solution.py:25
  327.5 17.9 %copy-start.26 = (f32[576,1152]{1,0:T(8,128)S(1)}, f32[576,1152]{1,0:T(8,128)}, u32[]{:S(2)}) copy-start(f32[576,1152]{1,0:T(8,128)} %get-tuple-element.110) | copy-start | bytes 7962628
  330.3 44.1 %collective-permute-start.17 = (bf16[4,144,1152]{2,1,0:T(8,128)(2,1)}, bf16[4,144,1152]{2,1,0:T(8,128)(2,1)}, u32[]{:S(2)}, u32[]{:S(2)}) collective-permute-start(bf16[4,144,1152]{2,1,0:T(8,128)(2,1)} %fusion.16), channel_id=1, source_target_pairs={{0,16},{4,20},{8,24},{12,28},{16,0},{20,4},{24,8},{28,12},{1,17},{... | collective-permute-start | bytes 3981320 | tf_op jit(solution)/shard_map/ppermute | solution.py:25
  344.5 10.8 %collective-permute-start.11 = (bf16[144,1152]{1,0:T(8,128)(2,1)S(1)}, bf16[144,1152]{1,0:T(8,128)(2,1)S(1)}, u32[]{:S(2)}, u32[]{:S(2)}) collective-permute-start(bf16[144,1152]{1,0:T(8,128)(2,1)S(1)} %fusion.78), channel_id=1, source_target_pairs={{0,8},{4,12},{8,0},{12,4},{16,24},{20,28},{24,16},{28,20},{1,9},{5... | collective-permute-start | bytes 995336 | tf_op jit(solution)/shard_map/ppermute | solution.py:25
  345.4 10.9 %copy-start.49 = (bf16[1,4,80,1152]{3,2,1,0:T(8,128)(2,1)S(1)}, bf16[1,4,80,1152]{3,2,1,0:T(8,128)(2,1)}, u32[]{:S(2)}) copy-start(bf16[1,4,80,1152]{3,2,1,0:T(8,128)(2,1)} %slice.257) | copy-start | bytes 2211844
  348.3 33.7 %collective-permute-start.18 = (bf16[4,144,1152]{2,1,0:T(8,128)(2,1)}, bf16[4,144,1152]{2,1,0:T(8,128)(2,1)}, u32[]{:S(2)}, u32[]{:S(2)}) collective-permute-start(bf16[4,144,1152]{2,1,0:T(8,128)(2,1)} %fusion.20), channel_id=1, source_target_pairs={{0,8},{4,12},{8,0},{12,4},{16,24},{20,28},{24,16},{28,20},{1,9},{5... | collective-permute-start | bytes 3981320 | tf_op jit(solution)/shard_map/ppermute | solution.py:25
  358.8 23.2 %copy-start.18 = (f32[576,1152]{1,0:T(8,128)S(1)}, f32[576,1152]{1,0:T(8,128)}, u32[]{:S(2)}) copy-start(f32[576,1152]{1,0:T(8,128)} %fusion.53) | copy-start | bytes 7962628
  388.4 87.7 %collective-permute-start.19 = (bf16[2,144,1152]{2,1,0:T(8,128)(2,1)}, bf16[2,144,1152]{2,1,0:T(8,128)(2,1)}, u32[]{:S(2)}, u32[]{:S(2)}) collective-permute-start(bf16[2,144,1152]{2,1,0:T(8,128)(2,1)} %get-tuple-element.113), channel_id=1, source_target_pairs={{0,1},{1,0},{2,3},{3,2},{4,5},{5,4},{6,7},{7,6},{8,9},{9,8},{10,11... | collective-permute-start | bytes 1990664 | tf_op jit(solution)/shard_map/ppermute | solution.py:25
  388.6 87.4 %collective-permute-start.20 = (bf16[2,144,1152]{2,1,0:T(8,128)(2,1)}, bf16[2,144,1152]{2,1,0:T(8,128)(2,1)}, u32[]{:S(2)}, u32[]{:S(2)}) collective-permute-start(bf16[2,144,1152]{2,1,0:T(8,128)(2,1)} %get-tuple-element.115), channel_id=1, source_target_pairs={{0,2},{1,3},{2,0},{3,1},{4,6},{5,7},{6,4},{7,5},{8,10},{9,11},{10,... | collective-permute-start | bytes 1990664 | tf_op jit(solution)/shard_map/ppermute | solution.py:25
  391.3 84.8 %collective-permute-start.21 = (bf16[2,144,1152]{2,1,0:T(8,128)(2,1)}, bf16[2,144,1152]{2,1,0:T(8,128)(2,1)}, u32[]{:S(2)}, u32[]{:S(2)}) collective-permute-start(bf16[2,144,1152]{2,1,0:T(8,128)(2,1)} %get-tuple-element.114), channel_id=1, source_target_pairs={{0,3},{1,2},{2,1},{3,0},{4,7},{5,6},{6,5},{7,4},{8,11},{9,10},{10,... | collective-permute-start | bytes 1990664 | tf_op jit(solution)/shard_map/ppermute | solution.py:25
  404.0 53.5 %collective-permute-start.6 = (bf16[512,1152]{1,0:T(8,128)(2,1)}, bf16[512,1152]{1,0:T(8,128)(2,1)}, u32[]{:S(2)}, u32[]{:S(2)}) collective-permute-start(bf16[512,1152]{1,0:T(8,128)(2,1)} %fusion.12), channel_id=1, source_target_pairs={{0,1},{1,0},{2,3},{3,2},{4,5},{5,4},{6,7},{7,6},{8,9},{9,8},{10,11... | collective-permute-start | bytes 3538952 | tf_op jit(solution)/shard_map/ppermute | solution.py:25
  405.2 82.9 %collective-permute-start.7 = (bf16[4,144,1152]{2,1,0:T(8,128)(2,1)}, bf16[4,144,1152]{2,1,0:T(8,128)(2,1)}, u32[]{:S(2)}, u32[]{:S(2)}) collective-permute-start(bf16[4,144,1152]{2,1,0:T(8,128)(2,1)} %dynamic-slice_bitcast_fusion), channel_id=1, source_target_pairs={{0,4},{4,0},{8,12},{12,8},{16,20},{20,16},{24,28},{28,24},{1,5},{5... | collective-permute-start | bytes 3981320 | tf_op jit(solution)/shard_map/ppermute | solution.py:25
  406.5 52.2 %copy-start.10 = (bf16[512,1152]{1,0:T(8,128)(2,1)S(1)}, bf16[512,1152]{1,0:T(8,128)(2,1)}, u32[]{:S(2)}) copy-start(bf16[512,1152]{1,0:T(8,128)(2,1)} %patches.1) | copy-start | bytes 3538948
  406.5 52.2 %copy-start.32 = (bf16[3,320,1152]{2,1,0:T(8,128)(2,1)S(1)}, bf16[3,320,1152]{2,1,0:T(8,128)(2,1)}, u32[]{:S(2)}) copy-start(bf16[3,320,1152]{2,1,0:T(8,128)(2,1)} %slice.210) | copy-start | bytes 6635524
  406.5 52.2 %copy-start.41 = (bf16[1024,960]{1,0:T(8,128)(2,1)S(1)}, bf16[1024,960]{1,0:T(8,128)(2,1)}, u32[]{:S(2)}) copy-start(bf16[1024,960]{1,0:T(8,128)(2,1)} %copy-done.39) | copy-start | bytes 5898244
  406.5 52.2 %copy-start.58 = (f32[2,1,1152]{2,0,1:T(2,128)S(1)}, f32[2,1,1152]{2,0,1:T(2,128)}, u32[]{:S(2)}) copy-start(f32[2,1,1152]{2,0,1:T(2,128)} %copy.87) | copy-start | bytes 27652
  406.5 52.2 %copy-start.68 = (f32[512]{0:T(512)S(1)}, f32[512]{0:T(512)}, u32[]{:S(2)}) copy-start(f32[512]{0:T(512)} %copy-done.67) | copy-start | bytes 6148
  457.5 63.8 %collective-permute-start.12 = (bf16[144,1152]{1,0:T(8,128)(2,1)}, bf16[144,1152]{1,0:T(8,128)(2,1)}, u32[]{:S(2)}, u32[]{:S(2)}) collective-permute-start(bf16[144,1152]{1,0:T(8,128)(2,1)} %add_convert_fusion.3), channel_id=1, source_target_pairs={{0,2},{1,3},{2,0},{3,1},{4,6},{5,7},{6,4},{7,5},{8,10},{9,11},{10,... | collective-permute-start | bytes 995336 | tf_op jit(solution)/shard_map/ppermute | solution.py:25
  472.8 10.8 %all-to-all-start = ((f32[32,2,216]{2,1,0:T(2,128)}), f32[32,2,216]{2,1,0:T(2,128)}, u32[]{:S(2)}, u32[]{:S(2)}) async-start(f32[32,2,216]{2,1,0:T(2,128)} %copy.68), calls=%async_computation | async-start | bytes 131072 | tf_op jit(solution)/shard_map/all_to_all | solution.py:829
  479.0 40.8 %collective-permute-start.22 = (bf16[2,144,1152]{2,1,0:T(8,128)(2,1)}, bf16[2,144,1152]{2,1,0:T(8,128)(2,1)}, u32[]{:S(2)}, u32[]{:S(2)}) collective-permute-start(bf16[2,144,1152]{2,1,0:T(8,128)(2,1)} %fusion.52), channel_id=1, source_target_pairs={{0,8},{4,12},{8,0},{12,4},{16,24},{20,28},{24,16},{28,20},{1,9},{5... | collective-permute-start | bytes 1990664 | tf_op jit(solution)/shard_map/ppermute | solution.py:25
  480.6 55.4 %collective-permute-start.23 = (bf16[2,144,1152]{2,1,0:T(8,128)(2,1)}, bf16[2,144,1152]{2,1,0:T(8,128)(2,1)}, u32[]{:S(2)}, u32[]{:S(2)}) collective-permute-start(bf16[2,144,1152]{2,1,0:T(8,128)(2,1)} %fusion.52), channel_id=1, source_target_pairs={{0,16},{4,20},{8,24},{12,28},{16,0},{20,4},{24,8},{28,12},{1,17},{... | collective-permute-start | bytes 1990664 | tf_op jit(solution)/shard_map/ppermute | solution.py:25
  492.2 24.7 %collective-permute-start.8 = (bf16[2,144,1152]{2,1,0:T(8,128)(2,1)}, bf16[2,144,1152]{2,1,0:T(8,128)(2,1)}, u32[]{:S(2)}, u32[]{:S(2)}) collective-permute-start(bf16[2,144,1152]{2,1,0:T(8,128)(2,1)} %pad_maximum_fusion.12), channel_id=1, source_target_pairs={{0,8},{4,12},{8,0},{12,4},{16,24},{20,28},{24,16},{28,20},{1,9},{5... | collective-permute-start | bytes 1990664 | tf_op jit(solution)/shard_map/ppermute | solution.py:25
  497.8 63.9 %all-to-all-start.1 = ((f32[32,1,9792]{2,1,0:T(1,128)}), f32[32,1,9792]{2,1,0:T(1,128)}, u32[]{:S(2)}, u32[]{:S(2)}) async-start(f32[32,1,9792]{2,1,0:T(1,128)} %all_to_all.10), calls=%async_computation.1 | async-start | bytes 2523136 | tf_op jit(solution)/shard_map/all_to_all | solution.py:886
  501.2 43.1 %copy-start.80 = (f32[512]{0:T(512)S(1)}, f32[512]{0:T(512)}, u32[]{:S(2)}) copy-start(f32[512]{0:T(512)} %get-tuple-element.90) | copy-start | bytes 6148
  518.1 14.1 %collective-permute-start.9 = (bf16[144,1152]{1,0:T(8,128)(2,1)S(1)}, bf16[144,1152]{1,0:T(8,128)(2,1)S(1)}, u32[]{:S(2)}, u32[]{:S(2)}) collective-permute-start(bf16[144,1152]{1,0:T(8,128)(2,1)S(1)} %fusion.77), channel_id=1, source_target_pairs={{0,16},{4,20},{8,24},{12,28},{16,0},{20,4},{24,8},{28,12},{1,17},{... | collective-permute-start | bytes 995336 | tf_op jit(solution)/shard_map/ppermute | solution.py:25
  520.8 23.5 %collective-permute-start.24 = (bf16[144,1152]{1,0:T(8,128)(2,1)S(1)}, bf16[144,1152]{1,0:T(8,128)(2,1)S(1)}, u32[]{:S(2)}, u32[]{:S(2)}) collective-permute-start(bf16[144,1152]{1,0:T(8,128)(2,1)S(1)} %slice_bitcast_fusion.1), channel_id=1, source_target_pairs={{0,16},{4,20},{8,24},{12,28},{16,0},{20,4},{24,8},{28,12},{1,17},{... | collective-permute-start | bytes 995336 | tf_op jit(solution)/shard_map/ppermute | solution.py:25
  533.6 9.5 %collective-permute-start.13 = (bf16[144,1152]{1,0:T(8,128)(2,1)S(1)}, bf16[144,1152]{1,0:T(8,128)(2,1)S(1)}, u32[]{:S(2)}, u32[]{:S(2)}) collective-permute-start(bf16[144,1152]{1,0:T(8,128)(2,1)S(1)} %add_convert_fusion.2), channel_id=1, source_target_pairs={{0,8},{4,12},{8,0},{12,4},{16,24},{20,28},{24,16},{28,20},{1,9},{5... | collective-permute-start | bytes 995336 | tf_op jit(solution)/shard_map/ppermute | solution.py:25
  536.9 9.7 %collective-permute-start.25 = (bf16[144,1152]{1,0:T(8,128)(2,1)S(1)}, bf16[144,1152]{1,0:T(8,128)(2,1)S(1)}, u32[]{:S(2)}, u32[]{:S(2)}) collective-permute-start(bf16[144,1152]{1,0:T(8,128)(2,1)S(1)} %slice_bitcast_fusion), channel_id=1, source_target_pairs={{0,8},{4,12},{8,0},{12,4},{16,24},{20,28},{24,16},{28,20},{1,9},{5... | collective-permute-start | bytes 995336 | tf_op jit(solution)/shard_map/ppermute | solution.py:25
  537.6 10.7 %collective-permute-start.14 = (bf16[144,1152]{1,0:T(8,128)(2,1)S(1)}, bf16[144,1152]{1,0:T(8,128)(2,1)S(1)}, u32[]{:S(2)}, u32[]{:S(2)}) collective-permute-start(bf16[144,1152]{1,0:T(8,128)(2,1)S(1)} %add_convert_fusion.2), channel_id=1, source_target_pairs={{0,16},{4,20},{8,24},{12,28},{16,0},{20,4},{24,8},{28,12},{1,17},{... | collective-permute-start | bytes 995336 | tf_op jit(solution)/shard_map/ppermute | solution.py:25
  543.1 8.9 %collective-permute-start.15 = (bf16[144,1152]{1,0:T(8,128)(2,1)S(1)}, bf16[144,1152]{1,0:T(8,128)(2,1)S(1)}, u32[]{:S(2)}, u32[]{:S(2)}) collective-permute-start(bf16[144,1152]{1,0:T(8,128)(2,1)S(1)} %collective-permute-done.13), channel_id=1, source_target_pairs={{0,16},{4,20},{8,24},{12,28},{16,0},{20,4},{24,8},{28,12},{1,17},{... | collective-permute-start | bytes 995336 | tf_op jit(solution)/shard_map/ppermute | solution.py:25
  553.7 12.0 %collective-permute-start.16 = (bf16[4,144,1152]{2,1,0:T(8,128)(2,1)}, bf16[4,144,1152]{2,1,0:T(8,128)(2,1)}, u32[]{:S(2)}, u32[]{:S(2)}) collective-permute-start(bf16[4,144,1152]{2,1,0:T(8,128)(2,1)} %get-tuple-element.117), channel_id=1, source_target_pairs={{0,4},{4,0},{8,12},{12,8},{16,20},{20,16},{24,28},{28,24},{1,5},{5... | collective-permute-start | bytes 3981320 | tf_op jit(solution)/shard_map/ppermute | solution.py:25
  557.7 17.1 %collective-permute-start.26 = (bf16[4,2,144,1152]{3,2,1,0:T(8,128)(2,1)}, bf16[4,2,144,1152]{3,2,1,0:T(8,128)(2,1)}, u32[]{:S(2)}, u32[]{:S(2)}) collective-permute-start(bf16[4,2,144,1152]{3,2,1,0:T(8,128)(2,1)} %get-tuple-element.111), channel_id=1, source_target_pairs={{0,4},{4,0},{8,12},{12,8},{16,20},{20,16},{24,28},{28,24},{1,5},{5... | collective-permute-start | bytes 7962632 | tf_op jit(solution)/shard_map/ppermute | solution.py:25
  (81 other events, 290.4 us)

commit v4 on v3

--- a/solution.py
+++ b/solution.py
@@ -72,71 +72,6 @@
         end = min(-(-(h + 1) * HP // 128) * 128, width)
         found.append((base, end - base, h * HP - base))
     return found
-
-
-def attn_bwd_kernel(
-    q_ref, k_ref, v_ref, g_ref, lse_ref, dq_ref, dk_ref, dv_ref, kt, dqt, dk_acc, dv_acc
-):
-    rows, width = q_ref.shape
-    qb = 512
-    kt[...] = k_ref[...].T
-    dk_acc[...] = jnp.zeros_like(dk_acc)
-    dv_acc[...] = jnp.zeros_like(dv_acc)
-    zero = jnp.zeros((), BF)
-    for h, (base, size, lo) in enumerate(head_windows(width)):
-        win = slice(base, base + size)
-        lane = lax.broadcasted_iota(jnp.int32, (rows, size), 1)
-        here = (lane >= lo) & (lane < lo + HP)
-        km = jnp.where(here, k_ref[:, win], zero)
-        vm = jnp.where(here, v_ref[:, win], zero)
-        head = slice(h * HP, (h + 1) * HP)
-        row = lax.broadcasted_iota(jnp.int32, (HP, rows), 0)
-        kth = jnp.where(row < HD, kt[head, :], zero)
-        lane_b = lax.broadcasted_iota(jnp.int32, (qb, size), 1)
-        real = (lane_b >= lo) & (lane_b < lo + HD)
-
-        def block(j, carry):
-            at = pl.ds(pl.multiple_of(j * qb, qb), qb)
-            q_blk = q_ref[at, win]
-            g_blk = g_ref[at, win]
-            s = dot(km, q_blk, 1, 1)
-            p = jnp.exp2(s * SCALE2 - lse_ref[h, :, at])
-            dp = dot(vm, g_blk, 1, 1)
-            delta = jnp.sum(p * dp, axis=0, keepdims=True)
-            ds = (p * (dp - delta)).astype(BF)
-            dv_acc[:, win] += dot(p.astype(BF), jnp.where(real, g_blk, zero), 1, 0)
-            dk_acc[:, win] += dot(ds, jnp.where(real, q_blk, zero), 1, 0)
-            dqt[head, at] = dot(kth, ds, 1, 0)
-            return carry
-
-        lax.fori_loop(0, rows // qb, block, 0)
-    dq_ref[...] = (dqt[...].T * SCALE).astype(BF)
-    dk_ref[...] = (dk_acc[...] * SCALE).astype(BF)
-    dv_ref[...] = dv_acc[...].astype(BF)
-
-
-def attn_bwd(q, k, v, g, lse):
-    rows, width = q.shape
-    heads = width // HP
-    shape = jax.ShapeDtypeStruct((rows, width), BF)
-    return pl.pallas_call(
-        attn_bwd_kernel,
-        out_shape=(shape, shape, shape),
-        in_specs=[pl.BlockSpec(memory_space=pltpu.VMEM)] * 5,
-        out_specs=[pl.BlockSpec(memory_space=pltpu.VMEM)] * 3,
-        scratch_shapes=[
-            pltpu.VMEM((width, rows), BF),
-            pltpu.VMEM((width, rows), F32),
-            pltpu.VMEM((rows, width), F32),
-            pltpu.VMEM((rows, width), F32),
-        ],
-        compiler_params=pltpu.CompilerParams(vmem_limit_bytes=40 << 20),
-        cost_estimate=pl.CostEstimate(
-            flops=10 * rows * rows * 256 * heads,
-            bytes_accessed=14 * rows * width,
-            transcendentals=rows * rows * heads,
-        ),
-    )(q, k, v, g, lse)
 
 
 PLACE = {0: 0, 1: 1, 3: 2, 2: 3}
@@ -600,6 +535,384 @@
     )
 
 
+def back_kernel(
+    per_dp, gao_row, x_row, watt_own, watt_other, q0, k0, v0, q1, k1, v1, c0, c1, l0, l1,
+    two_2, two_0, one_1, one_0, patches, sums_4, b_sums, ids_all, w_ada,
+    g_out, grad_cols, final, mlp_all, att_all,
+    kt, dqt, wide_acc, gc, d3, att, core_land, come, plane, z_land, first_land, second_land,
+    part_send, last_land, mlp_done, g_send, g_land, more_mlp, more_att,
+    sums_6, col_send, col_land, row_send, shared, z_rows, small, sems,
+):
+    rows, width = gao_row.shape
+    tokens = rows // 2
+    wide = watt_own.shape[1]
+    half = wide // 2
+    d, z = lax.axis_index("dp"), lax.axis_index("mp")
+    core, q = lax.rem(d, 2), lax.rem(d // 2, 4)
+    at_z = [(d, z), (d, flip(z, 1)), (d, flip(z, 2)), (d, 3 - z)]
+    at_core, at_x, at_y = (flip(d, 1), z), (flip(d, 2), z), (flip(d, 4), z)
+    extra, bit = [], 8
+    while bit < lax.axis_size("dp"):
+        extra.append((flip(d, bit), z))
+        bit *= 2
+    barrier = pltpu.get_barrier_semaphore()
+    n_dp, n_mp = lax.axis_size("dp"), lax.axis_size("mp")
+    n_all, me = n_dp * n_mp, d * n_mp + z
+
+    def greet(t, carry):
+        to = coords(lax.rem(me + t, n_all), n_mp)
+        pl.semaphore_signal(barrier, inc=1, device_id=to, device_id_type=pl.DeviceIdType.MESH)
+        return carry
+
+    lax.fori_loop(1, n_all, greet, 0)
+    pl.semaphore_wait(barrier, n_all - 1)
+    copies = Copies(sems)
+    copies.start("two", two_2, come.at[1], at_y)
+    copies.start("one", one_1, come.at[0], at_x)
+    kept = [
+        pltpu.make_async_copy(one_0, plane.at[0], sems.at[sems.shape[0] - 3]),
+        pltpu.make_async_copy(two_0, plane.at[1], sems.at[sems.shape[0] - 4]),
+    ]
+    for made in kept:
+        made.start()
+    zero = jnp.zeros((), BF)
+    qb = 256
+    slots = ((watt_own, q0, k0, v0, c0, l0), (watt_other, q1, k1, v1, c1, l1))
+
+    att_done = first_land.at[0, 0]
+    dv_at = [slice(384 + base, 384 + base + size) for base, size, _ in head_windows(wide)]
+
+    def back(slot):
+        watt, qr, kr, vr, _, lr = slots[slot]
+        for t in range(2):
+            at = slice(t * tokens, (t + 1) * tokens)
+            gc[at, :] = dot(gao_row[at, :], watt[3], 1, 1).astype(BF)
+        kt[...] = kr[...].T
+        wide_acc[...] = jnp.zeros_like(wide_acc)
+        for h, (base, size, lo) in enumerate(head_windows(wide)):
+            win = slice(base, base + size)
+            lane = lax.broadcasted_iota(jnp.int32, (rows, size), 1)
+            here = (lane >= lo) & (lane < lo + HP)
+            km = jnp.where(here, kr[:, win], zero)
+            vm = jnp.where(here, vr[:, win], zero)
+            head = slice(h * HP, (h + 1) * HP)
+            row = lax.broadcasted_iota(jnp.int32, (HP, rows), 0)
+            kth = jnp.where(row < HD, kt[head, :], zero)
+            lane_b = lax.broadcasted_iota(jnp.int32, (qb, size), 1)
+            real = (lane_b >= lo) & (lane_b < lo + HD)
+
+            def block(j, carry):
+                at = pl.ds(pl.multiple_of(j * qb, qb), qb)
+                q_blk = qr[at, win]
+                g_blk = gc[at, win]
+                s = dot(km, q_blk, 1, 1)
+                p = jnp.exp2(s * SCALE2 - lr[h, :, at])
+                dp = dot(vm, g_blk, 1, 1)
+                delta = jnp.sum(p * dp, axis=0, keepdims=True)
+                ds = (p * (dp - delta)).astype(BF)
+                wide_acc[:rows, dv_at[h]] += dot(p.astype(BF), jnp.where(real, g_blk, zero), 1, 0)
+                wide_acc[:rows, win] += dot(ds, jnp.where(real, q_blk, zero), 1, 0)
+                dqt[head, at] = dot(kth, ds, 1, 0)
+                return carry
+
+            lax.fori_loop(0, rows // qb, block, 0)
+        d3[slot, 0] = (dqt[...].T * SCALE).astype(BF)
+        d3[slot, 1] = (wide_acc[:rows, :wide] * SCALE).astype(BF)
+        d3[slot, 2] = wide_acc[:rows, 384 : 384 + wide].astype(BF)
+        for n, m in enumerate((0, 2)):
+            shared[6 + slot : 7 + slot, n * 384 : n * 384 + wide] = jnp.sum(
+                d3[slot, m].astype(F32), axis=0, keepdims=True
+            )
+
+    def weight_grads(slot):
+        ctx = slots[slot][4]
+
+        def one(m, carry):
+            att[m] = dot(d3[slot, m], x_row[...], 0, 0).astype(BF)
+            return carry
+
+        lax.fori_loop(0, 3, one, 0)
+        att[3] = dot(ctx[...], gao_row[...], 0, 0).astype(BF)
+        away = pl.ds(pl.multiple_of((1 - core) * half, 16), half)
+        copies.start(("c", slot), att.at[:, away], core_land.at[slot], at_core)
+
+    keep = pl.ds(pl.multiple_of(core * half, 16), half)
+
+    def add(a, b):
+        return (a.astype(F32) + b.astype(F32)).astype(BF)
+
+    def core_sum(slot):
+        copies.arrived(("c", slot))
+
+        def one(m, carry):
+            core_land[slot, m] = add(core_land[slot, m], att[m, keep])
+            return carry
+
+        lax.fori_loop(0, 4, one, 0)
+        bits, to = ((1, at_x), (2, at_y))[slot]
+        for n, i in enumerate((bits, 3)):
+            copies.start(
+                ("p", slot, n), core_land.at[slot, flips(q, i)], first_land.at[slot, n], to
+            )
+
+    def second_way(slot):
+        other, to = ((2, at_y), (1, at_x))[slot]
+        for n in range(2):
+            copies.arrived(("p", slot, n))
+        part_send[slot] = add(core_land[slot, flips(q, other)], first_land[slot, 1])
+        copies.start(("s", slot), part_send.at[slot], second_land.at[slot], to)
+        first_land[slot, 0] = add(core_land[slot, q], first_land[slot, 0])
+
+    def plane_sum(slot):
+        copies.arrived(("s", slot))
+        first_land[slot, 0] = add(first_land[slot, 0], second_land[slot])
+
+    shared[...] = b_sums[...]
+    back(1)
+    weight_grads(1)
+    copies.arrived("two")
+    copies.arrived("one")
+    for m in (1, 0):
+        kept[m].wait()
+
+        def one(j, carry):
+            plane[m, j] = add(plane[m, j], come[m, j])
+            return carry
+
+        lax.fori_loop(0, 4, one, 0)
+        for j in (1, 2, 3):
+            copies.start(("z", m, j), plane.at[m, j], z_land.at[m, j - 1], at_z[j])
+    core_sum(1)
+    back(0)
+    second_way(1)
+
+    def g_part(at):
+        total = None
+        for slot in (0, 1):
+            for m in range(3):
+                term = dot(d3[slot, m, at], slots[slot][0][m], 1, 0)
+                total = term if total is None else total + term
+        return total
+
+    g_send[...] = g_part(slice(tokens, rows)).astype(BF)
+    copies.start("g", g_send, g_land, at_z[1])
+    plane_sum(1)
+    copies.start("b", first_land.at[1, 0], last_land, at_z[2])
+    copies.made["c", 1].wait_send()
+    weight_grads(0)
+    core_sum(0)
+    g_out[...] = g_part(slice(0, tokens))
+    second_way(0)
+    for m in (1, 0):
+        for j in (1, 2, 3):
+            copies.arrived(("z", m, j))
+        total = plane[m, 0].astype(F32)
+        for j in (1, 2, 3):
+            total = total + z_land[m, j - 1].astype(F32)
+        mlp_done[m] = total.astype(BF)
+    for n, to in enumerate(extra):
+        copies.start(("mlp_more", n), mlp_done, more_mlp.at[n], to)
+        copies.arrived(("mlp_more", n))
+        copies.made["mlp_more", n].wait_send()
+        mlp_done[...] = add(mlp_done[...], more_mlp[n])
+    last = sems.shape[0]
+    here = [pltpu.make_async_copy(mlp_done, mlp_all.at[core, q], sems.at[last - 1])]
+    here[0].start()
+    copies.start("m_x", mlp_done, mlp_all.at[core, q], at_x)
+    copies.start("m_y", mlp_done, mlp_all.at[core, q], at_y)
+    plane_sum(0)
+    copies.arrived("b")
+    att_done[...] = add(first_land[0, 0], last_land[...])
+    for n, to in enumerate(extra):
+        copies.start(("att_more", n), att_done, more_att.at[n], to)
+        copies.arrived(("att_more", n))
+        copies.made["att_more", n].wait_send()
+        att_done[...] = add(att_done[...], more_att[n])
+    here.append(pltpu.make_async_copy(att_done, att_all.at[q, core], sems.at[last - 2]))
+    here[1].start()
+    copies.start("a_x", att_done, att_all.at[q, core], at_x)
+    copies.start("a_y", att_done, att_all.at[q, core], at_y)
+
+    copies.made["g"].wait_send()
+    fetch = pltpu.make_async_copy(patches, g_send, sems.at[last - 5])
+    fetch.start()
+    copies.arrived("g")
+    step = 128
+    sums_6[:, 2 * width :] = sums_4[...]
+    sums_6[:, : 2 * width] = jnp.zeros((8, 2 * width), F32)
+    fetch.wait()
+    for b in range(tokens // BLOCK):
+
+        def total(t, carry):
+            part = pl.ds(pl.multiple_of(b * BLOCK + t * step, step), step)
+            g = g_out[part, :] + g_land[part, :].astype(F32)
+            g_out[part, :] = g
+            v = g_send[part, :].astype(F32)
+            centred = v - jnp.mean(v, axis=-1, keepdims=True)
+            spread = jnp.mean(centred * centred, axis=-1, keepdims=True)
+            scaled = g * (centred * lax.rsqrt(spread + 1e-06))
+            return (
+                carry[0] + jnp.sum(g, axis=0, keepdims=True),
+                carry[1] + jnp.sum(scaled, axis=0, keepdims=True),
+            )
+
+        nothing = jnp.zeros((1, width), F32)
+        shift, scale = lax.fori_loop(0, BLOCK // step, total, (nothing, nothing))
+        sums_6[b : b + 1, :width] = shift
+        sums_6[b : b + 1, width : 2 * width] = scale
+    cols = col_send.shape[2]
+    for t in range(n_all):
+        col_send[t] = sums_6[:, t * cols : (t + 1) * cols]
+
+    def remote(src, dst, k, to):
+        return pltpu.make_async_remote_copy(
+            src_ref=src, dst_ref=dst, send_sem=small.at[2 * k], recv_sem=small.at[2 * k + 1],
+            device_id=to, device_id_type=pl.DeviceIdType.MESH,
+        )
+
+    def send_cols(t, carry):
+        other = lax.rem(me + t, n_all)
+        remote(col_send.at[other], col_land.at[me], 0, coords(other, n_mp)).start()
+        return carry
+
+    lax.fori_loop(1, n_all, send_cols, 0)
+    col_land[me] = col_send[me]
+    qx, qy = flips(q, 1), flips(q, 2)
+    copies.arrived("m_x")
+    copies.start("m_xy", mlp_all.at[core, qx, 0], mlp_all.at[core, qx, 0], at_y)
+    copies.arrived("m_y")
+    copies.start("m_yx", mlp_all.at[core, qy, 1], mlp_all.at[core, qy, 1], at_x)
+    here[0].wait()
+    for i in range(3):
+        at = flips(q, i)
+        copies.start(("m_c", i), mlp_all.at[core, at], mlp_all.at[core, at], at_core)
+    copies.arrived("a_x")
+    copies.start("a_xy", att_all.at[qx, core], att_all.at[qx, core], at_y)
+
+    wait_all(col_land, n_all - 1, small.at[1])
+    rows_8 = n_dp * 8
+    some = min(32, n_all)
+    k = lax.broadcasted_iota(jnp.int32, (some * 8, rows_8), 1)
+    image = jnp.where(lax.rem(k, 8) < per_dp, k // 8 * per_dp + lax.rem(k, 8), -2).astype(F32)
+
+    def collect(t, carry):
+        part = pl.ds(t * some, some)
+        found = ids_all[part].reshape(some * 8, 128)[:, :1] == image
+        return carry + lax.dot_general(
+            jnp.where(found, 1.0, 0.0),
+            col_land[part].reshape(some * 8, cols),
+            (((0,), (0,)), ((), ())),
+            precision=lax.Precision.HIGHEST,
+            preferred_element_type=F32,
+        )
+
+    summed = lax.fori_loop(0, n_all // some, collect, jnp.zeros((rows_8, cols), F32)).astype(BF)
+    grad_cols[...] = summed
+    silu_part = dot(summed, w_ada[...], 1, 1)
+    row_send[...] = silu_part
+
+    def block_of(t, size, start):
+        return pl.ds(pl.multiple_of(t * size + start, 8), 8)
+
+    def send_rows(t, carry):
+        other = lax.rem(d + t, n_dp)
+        to = (other, z)
+        remote(row_send.at[block_of(other, 8, 0)], wide_acc.at[block_of(d, 16, 0)], 1, to).start()
+        remote(shared, wide_acc.at[block_of(d, 16, 8)], 1, to).start()
+        return carry
+
+    lax.fori_loop(1, n_dp, send_rows, 0)
+    wide_acc[block_of(d, 16, 0), :] = row_send[block_of(d, 8, 0), :]
+    wide_acc[block_of(d, 16, 8), :] = shared[...]
+    copies.arrived("m_xy")
+    copies.arrived("m_yx")
+    q3 = flips(q, 3)
+    copies.start(("m_c", 3), mlp_all.at[core, q3], mlp_all.at[core, q3], at_core)
+    copies.arrived("a_y")
+    here[1].wait()
+    copies.arrived("a_xy")
+    copies.start("a_c", att_all.at[:, core], att_all.at[:, core], at_core)
+    wait_all(wide_acc, (n_dp - 1) * 16, small.at[3])
+
+    def sum_rows(t, carry):
+        return carry + wide_acc[pl.ds(pl.multiple_of(t * 16, 16), 16), :]
+
+    z_rows[0] = lax.fori_loop(0, n_dp, sum_rows, jnp.zeros((16, width), F32))
+    for j in (1, 2, 3):
+        copies.start(("rows", j), z_rows.at[0], z_rows.at[j], at_z[j])
+    for j in (1, 2, 3):
+        copies.arrived(("rows", j))
+    final[...] = z_rows[0] + z_rows[1] + z_rows[2] + z_rows[3]
+    final[14:15, :] = z_rows[0, 14:15, :] + z_rows[2, 15:16, :]
+    for i in range(4):
+        copies.arrived(("m_c", i))
+    copies.arrived("a_c")
+    copies.finish(but=[n for n in copies.made if n[0] in ("mlp_more", "att_more") or n in ("g", ("c", 1))])
+    wait_all(col_land, n_all - 1, small.at[0])
+    wait_all(wide_acc, (n_dp - 1) * 16, small.at[2])
+
+
+def back(
+    per_dp, gao_row, x_row, watt_own, watt_other, heads_0, heads_1, ctx, lse,
+    two_2, two_0, one_1, one_0, patches, sums_4, b_sums, ids_all, w_ada,
+):
+    rows, width = gao_row.shape
+    tokens, wide = rows // 2, watt_own.shape[1]
+    half, sixth = wide // 2, two_2.shape[1]
+    more = max(1, (lax.axis_size("dp") // 8).bit_length() - 1)
+    n_dp, n_mp, cols = lax.axis_size("dp"), lax.axis_size("mp"), w_ada.shape[1]
+    n_all = n_dp * n_mp
+    shapes = (
+        jax.ShapeDtypeStruct((tokens, width), F32),
+        jax.ShapeDtypeStruct((n_dp * 8, cols), BF),
+        jax.ShapeDtypeStruct((16, width), F32),
+        jax.ShapeDtypeStruct((2, 4, 2, sixth, width), BF),
+        jax.ShapeDtypeStruct((4, 2, half, width), BF),
+    )
+    vmem, anywhere = pl.BlockSpec(memory_space=pltpu.VMEM), pl.BlockSpec(memory_space=pl.ANY)
+    return pl.pallas_call(
+        functools.partial(back_kernel, per_dp),
+        out_shape=shapes,
+        in_specs=[vmem] * 14 + [anywhere] * 5 + [vmem] * 4,
+        out_specs=[vmem, vmem, vmem, anywhere, anywhere],
+        scratch_shapes=[
+            pltpu.VMEM((wide, rows), BF),
+            pltpu.VMEM((wide, rows), F32),
+            pltpu.VMEM((max(rows, n_dp * 16), width), F32),
+            pltpu.VMEM((rows, wide), BF),
+            pltpu.VMEM((2, 3, rows, wide), BF),
+            pltpu.VMEM((4, wide, width), BF),
+            pltpu.VMEM((2, 4, half, width), BF),
+            pltpu.VMEM((2, 4, sixth, width), BF),
+            pltpu.VMEM((2, 4, sixth, width), BF),
+            pltpu.VMEM((2, 3, sixth, width), BF),
+            pltpu.VMEM((2, 2, half, width), BF),
+            pltpu.VMEM((2, half, width), BF),
+            pltpu.VMEM((2, half, width), BF),
+            pltpu.VMEM((half, width), BF),
+            pltpu.VMEM((2, sixth, width), BF),
+            pltpu.VMEM((tokens, width), BF),
+            pltpu.VMEM((tokens, width), BF),
+            pltpu.VMEM((more, 2, sixth, width), BF),
+            pltpu.VMEM((more, half, width), BF),
+            pltpu.VMEM((8, 6 * width), F32),
+            pltpu.VMEM((n_all, 8, cols), F32),
+            pltpu.VMEM((n_all, 8, cols), F32),
+            pltpu.VMEM((n_dp * 8, width), F32),
+            pltpu.VMEM((8, width), F32),
+            pltpu.VMEM((4, 16, width), F32),
+            pltpu.SemaphoreType.DMA((4,)),
+            pltpu.SemaphoreType.DMA((96,)),
+        ],
+        compiler_params=pltpu.CompilerParams(
+            collective_id=1, has_side_effects=True, vmem_limit_bytes=63 << 20
+        ),
+    )(
+        gao_row, x_row, watt_own, watt_other, *heads_0, *heads_1, *ctx, *lse,
+        two_2, two_0, one_1, one_0, patches, sums_4, b_sums, ids_all, w_ada,
+    )
+
+
 def pad_heads(rows_in):
     *lead, n, width = rows_in.shape
     split = rows_in.reshape(*lead, n // HD, HD, width)
@@ -667,8 +980,6 @@
         bqv_own, b_out,
     )
     heads_0, heads_1 = (q0, k0, v0), (q1, k1, v1)
-    watts = [watt_own, watt_other]
-    outs = [watt_own[3], watt_other[3]]
     w1_all, w2_all = [w.reshape(16 * sixth, width) for w in (w1_all, w2_all)]
     b1_all = b1_rel.reshape(16 * sixth)
     mods = mods[:n_blocks].reshape(n_blocks, 6, width)
@@ -732,129 +1043,12 @@
     g_gate_mlp = jnp.sum(grad_output * mlp_out, axis=1)
     grad_b2 = jnp.sum(gmo, axis=0, dtype=F32)
 
-    def back(heads, out_w, lse, rows_in):
-        grad_ctx = dot(rows_in, out_w, 1, 1).astype(BF)
-        return attn_bwd(*heads, grad_ctx, lse)
-
-    def att_grads(ctx, grad3):
-        whole = jnp.concatenate(
-            [dot(grad3, x_row, 0, 0).astype(BF), dot(ctx, gao_row, 0, 0).astype(BF)], axis=0
-        )
-        return drop_pads(whole.reshape(4, wide, width)).reshape(4, 2, sixth, width)
-
-    def over_cores(grad_att):
-        send = lax.dynamic_index_in_dim(grad_att, 1 - core, 1, keepdims=False)
-        keep = lax.dynamic_index_in_dim(grad_att, core, 1, keepdims=False)
-        got = low_sum(keep, swap(send, "dp", 1))
-        return [pick(got, q ^ i) for i in range(4)]
-
-    dq_1, dk_1, dv_1 = back(heads_1, outs[1], lse_1, gao_row)
-    grad3_1 = jnp.concatenate([dq_1, dk_1, dv_1], axis=1)
-    come2, come1 = lax.optimization_barrier((come2, come1, dq_1))[:2]
+    come2, come1 = lax.optimization_barrier((come2, come1, keep2_0))[:2]
     two_2 = low_sum(keep2_2, come2[1])
     two_0 = low_sum(keep2_0, come2[0])
-    come2 = swap(two_2, "dp", 4)
     keep1 = grads(gpre_w, mlp2_w, 0, 2)
     one_1 = low_sum(keep1[1], come1[0])
     one_0 = low_sum(keep1[0], come1[1])
-    come1 = swap(one_1, "dp", 2)
-    rel_b = over_cores(att_grads(ctx_1, grad3_1))
-    dq_0, dk_0, dv_0 = back(heads_0, outs[0], lse_0, after(gao_row, one_1, rel_b[0]))
-    come2, come1 = lax.optimization_barrier((come2, come1, dq_0))[:2]
-    grad3_0 = jnp.concatenate([dq_0, dk_0, dv_0], axis=1)
-    in_w = [w[:3].reshape(3 * wide, width) for w in watts]
-
-    def g_in_part(at):
-        return dot(grad3_0[at], in_w[0], 1, 0) + dot(grad3_1[at], in_w[1], 1, 0)
-
-    g_peer = swap(g_in_part(slice(tokens, None)).astype(BF), "mp", 1)
-    g_attn_in = blocks(g_in_part(slice(0, tokens)) + g_peer.astype(F32))
-    plane2 = low_sum(two_0, come2)
-    plane1 = low_sum(one_0, come1)
-    rel_a = over_cores(att_grads(ctx_0, grad3_0))
-
-    both = jnp.stack([plane1, plane2])
-    whole = both[:, 0].astype(F32)
-    for j in (1, 2, 3):
-        whole = whole + swap(both[:, j], "mp", j).astype(F32)
-    bit = 8
-    while bit < n_dp:
-        whole = whole + swap(whole.astype(BF), "dp", bit).astype(F32)
-        bit *= 2
-    done = whole.astype(BF)
-    done_x = swap(done, "dp", 2)
-    done_y = swap(done, "dp", 4)
-    done_xy = jnp.stack([swap(done_x[0], "dp", 4), swap(done_y[1], "dp", 2)])
-    mine = jnp.stack([done, done_x, done_y, done_xy])
-    theirs = swap(mine, "dp", 1)
-
-    spot = jnp.arange(8 * sixth)
-    came = (spot // (4 * sixth)) ^ core, ((spot // sixth) % 4) ^ q
-    target = (came[0] * 4 + came[1]) * sixth + spot % sixth
-    places = (target[:, None] == spot[None, :]).astype(BF)
-    rel = jnp.stack([mine, theirs])
-    out_w1 = dot(rel[:, :, 0].reshape(shard, width), places, 0, 0)
-    out_w2 = dot(places, rel[:, :, 1].reshape(shard, width), 0, 0)
-
-    come_b = swap(jnp.stack([rel_b[2], rel_b[3]]), "dp", 4)
-    b_1 = low_sum(rel_b[1], come_b[1])
-    b_0 = low_sum(low_sum(rel_b[0], come_b[0]), swap(b_1, "dp", 2))
-    come_a = swap(jnp.stack([rel_a[1], rel_a[3]]), "dp", 2)
-    a_2 = low_sum(rel_a[2], come_a[1])
-    a_0 = low_sum(low_sum(rel_a[0], come_a[0]), swap(a_2, "dp", 4))
-    att = a_0.astype(F32) + swap(b_0, "mp", 2).astype(F32)
-    bit = 8
-    while bit < n_dp:
-        att = att + swap(att.astype(BF), "dp", bit).astype(F32)
-        bit *= 2
-    att = att.astype(BF)
-    att_x = swap(att, "dp", 2)
-    att_y = swap(att, "dp", 4)
-    att_mine = jnp.stack([att, att_x, att_y, swap(att_x, "dp", 4)])
-    rel = jnp.stack([att_mine, swap(att_mine, "dp", 1)]).reshape(shard, width)
-    target_att = (came[1] * 2 + came[0]) * sixth + spot % sixth
-    places = (target_att[:, None] == spot[None, :]).astype(BF)
-    cut = [places[:, m * heads_shard : (m + 1) * heads_shard] for m in range(4)]
-    out_qkv = jnp.stack([dot(rel, cut[m], 0, 0) for m in range(3)])
-    out_wout = dot(cut[3], rel, 0, 0)
-
-    g_shift_attn = jnp.sum(g_attn_in, axis=1)
-    g_scale_attn = jnp.sum(g_attn_in * norm_a, axis=1)
-    grad_patches = flat(grad_resid + norm_back(g_attn_in, norm_a, rsig_a, scale_attn))
-    sums = jnp.concatenate(
-        [g_shift_attn, g_scale_attn, g_gate_attn, g_shift_mlp, g_scale_mlp, g_gate_mlp],
-        axis=1,
-    )
-    to_owner = sums.reshape(n_blocks, n_all, cols).transpose(1, 0, 2)
-    got = lax.all_to_all(to_owner, everyone, 0, 0).reshape(n_all * n_blocks, cols)
-    ids_from = ids_all[:, :n_blocks, 0].reshape(1, n_all * n_blocks)
-    images_here = conditioning.shape[0]
-    row = jnp.arange(n_dp * 8)[:, None]
-    image = jnp.where(row % 8 < images_here, row // 8 * images_here + row % 8, -2)
-    belongs = (ids_from == image.astype(F32)).astype(F32)
-    grad_cols = lax.dot_general(
-        belongs,
-        got,
-        (((1,), (0,)), ((), ())),
-        precision=lax.Precision.HIGHEST,
-        preferred_element_type=F32,
-    ).astype(BF)
-    grad_w_ada = dot(silu_cond, grad_cols, 0, 0)
-    grad_b_ada = jnp.sum(grad_cols, axis=0, dtype=F32)
-    silu_part = dot(grad_cols, w_ada, 1, 1)
-    silu_part = silu_part.reshape(n_dp, 8, width)[:, :images_here]
-
-    bqv_g = jnp.stack(
-        [
-            jnp.stack([jnp.sum(v, axis=0, dtype=F32) for v in pair])
-            for pair in ((dq_0, dv_0), (dq_1, dv_1))
-        ]
-    )
-    bqv_g = drop_pads(bqv_g[..., None])[..., 0]
-    shards = jnp.arange(n_mp)[:, None, None]
-    bqv_all = jnp.where(shards == z, bqv_g[0][None], 0.0) + jnp.where(
-        shards == (z ^ 2), bqv_g[1][None], 0.0
-    )
     nat, rel_at = jnp.arange(8 * n_mp)[:, None], jnp.arange(16)[None, :]
     step = rel_at // 4
     step = jnp.where(step == 2, 3, jnp.where(step == 3, 2, step))
@@ -867,32 +1061,34 @@
         precision=lax.Precision.HIGHEST,
         preferred_element_type=F32,
     )
-    payload = jnp.concatenate(
-        [
-            jnp.broadcast_to(
-                silu_part.reshape(n_dp, 1, images_here * width),
-                (n_dp, n_mp, images_here * width),
-            ),
-            jnp.broadcast_to(
-                jnp.concatenate([grad_bout, grad_b2])[None, None], (n_dp, n_mp, 2 * width)
-            ),
-            jnp.broadcast_to(grad_b1.reshape(1, n_mp, shard), (n_dp, n_mp, shard)),
-            jnp.broadcast_to(
-                bqv_all.reshape(1, n_mp, 2 * heads_shard), (n_dp, n_mp, 2 * heads_shard)
-            ),
-        ],
-        axis=2,
-    ).reshape(n_all, -1)
-    summed = jnp.sum(lax.all_to_all(payload, everyone, 0, 0), axis=0)
-    at = images_here * width
-    grad_silu = summed[:at].reshape(images_here, width)
+    b_sums = jnp.concatenate(
+        [grad_bout[None], grad_b2[None], grad_b1.reshape(n_mp, shard), jnp.zeros((2, width), F32)]
+    )
+    sums_4 = jnp.concatenate([g_gate_attn, g_shift_mlp, g_scale_mlp, g_gate_mlp], axis=1)
+    sums_4 = jnp.pad(sums_4, ((0, 8 - n_blocks), (0, 0)))
+    g_attn_in, grad_cols, final, mlp_all, att_all = back(
+        conditioning.shape[0], gao_row, x_row, watt_own, watt_other, heads_0, heads_1,
+        (ctx_0, ctx_1), (lse_0, lse_1), two_2, two_0, one_1, one_0, patches, sums_4, b_sums,
+        ids_all, w_ada,
+    )
+    g_attn_in = blocks(g_attn_in)
+    out_w1 = mlp_all[:, :, 0].reshape(shard, width)
+    unit = (jnp.arange(shard)[:, None] == jnp.arange(shard)[None, :]).astype(BF)
+    out_w1 = dot(out_w1, unit, 0, 0)
+    out_w2 = mlp_all[:, :, 1].reshape(shard, width).astype(F32)
+    att_all = drop_pads(att_all.reshape(4, wide, width))
+    out_qkv = att_all[:3].transpose(0, 2, 1).astype(F32)
+    out_wout = att_all[3].astype(F32)
+    grad_patches = flat(grad_resid + norm_back(g_attn_in, norm_a, rsig_a, scale_attn))
+    grad_w_ada = dot(silu_cond, grad_cols, 0, 0)
+    grad_b_ada = jnp.sum(grad_cols, axis=0, dtype=F32)
+    grad_silu = final[: conditioning.shape[0]]
     _, silu_back = jax.vjp(silu_fn, conditioning.astype(F32))
     grad_cond = silu_back(grad_silu)[0]
-    out_bout = summed[at : at + width]
-    out_b2 = summed[at + width : at + 2 * width]
-    at += 2 * width
-    out_b1 = summed[at : at + shard]
-    out_bqv = summed[at + shard :].reshape(2, heads_shard)
+    out_bout, out_b2 = final[8], final[9]
+    out_b1 = lax.dynamic_index_in_dim(final, 10 + z, 0, keepdims=False)
+    out_bqv = jnp.stack([final[14, :wide], final[14, 384 : 384 + wide]])
+    out_bqv = drop_pads(out_bqv[..., None])[..., 0]
 
     return (
         output,

time: 600 us -> 484 us (0.81)
  Pallas kernels: 181 us -> 312 us
  waiting for transfers between devices: 123 us -> 6.34 us
  matrix products: 126 us -> 77.9 us
  local copies, waits for them, and re-layouts: 61.3 us -> 29.2 us
  starting transfers between devices: 30.1 us -> 2.25 us
  other arithmetic: 68.8 us -> 47.7 us
    pallas_call x2 -> x1, Pallas kernels: 31 us -> 161 us  [back(): pl.pallas_call(functools.partial(back_kernel, per_dp), out_shape=shapes,...]
    ppermute x27 -> x5, waiting for transfers between devices: 121 us -> 6.34 us  [swap(): return lax.ppermute(value, axis, [(i, i ^ bit) for i in range(n)])]
    dot_general x29 -> x13, matrix products: 124 us -> 76.4 us  [dot(): lax.dot_general(a, b, (((ca,), (cb,)), ((), ())), preferred_element_type=...]
    ppermute x27 -> x5, starting transfers between devices: 23.5 us -> 2.25 us  [swap(): return lax.ppermute(value, axis, [(i, i ^ bit) for i in range(n)])]
    another operation x12 -> x1, other arithmetic: 17.4 us -> 0.01 us  [on_device(): out_bqv = jnp.stack([final[14, :wide], final[14, 384:384 + wide]])]
    unnamed x210 -> x87, local copies, waits for them, and re-layouts: 19.2 us -> 4.47 us
    all_to_all x2 -> x0, starting transfers between devices: 6.61 us -> none  [the longest x1 3.39 us: on_device(): summed = jnp.sum(lax.all_to_all(payload, everyone, 0, 0), axis=0)]
  transfers between devices with their start and end apart: 29 -> 5, of which waited for: 12 -> 1; matrix products, arithmetic and copies ran while one was open for 30% -> 18% of each run, Pallas kernels for 5% -> 0%
where the time goes in v4:
time: 484 us; the launch traced here: 476 us
  Pallas kernels  312 us (64%)
  matrix products  77.9 us (16%)
  other arithmetic  47.7 us (10%)
  local copies, waits for them, and re-layouts  29.2 us (6%)
  waiting for transfers between devices  6.34 us (1%)
    pallas_call x1, Pallas kernels, back(): pl.pallas_call(functools.partial(back_kernel, per_dp), out_shape=shapes,...  161 us
    pallas_call x1, Pallas kernels, front(): pl.pallas_call(functools.partial(front_kernel, per_dp), out_shape=shapes,...  150 us
    dot_general x13, matrix products, dot(): lax.dot_general(a, b, (((ca,), (cb,)), ((), ())), preferred_element_type=...  76.4 us
  transfers between devices with their start and end apart: 5, of which 1 were waited for; matrix products, arithmetic and copies ran while one was open for 18% of the time, Pallas kernels for 0%

profile of v4, /device:TPU:0, one launch (start us, length us, event | category | flops | bytes accessed | tf_op | source)
XLA Modules:
  0.0 476.4 jit_solution(12439132511470276653)
XLA Ops:
  1.5 1.0 copy.34.seg
  2.5 2.1 copy.33.w_ada
  6.2 1.3 fusion.49.bias
  9.0 1.3 reshape.424.b_out
  10.3 1.2 broadcast_in_dim.54
  11.5 3.6 fusion.11
  16.4 150.4 %shard_map.246 = (bf16[64,1152]{1,0:T(8,128)(2,1)}, f32[32,8,128]{2,1,0:T(8,128)}, f32[16,144]{1,0:T(8,128)}, f32[8,6912]{1,0:T(8,128)}, bf16[1024,1152]{1,0:T(8...) custom-call(f32[8,1152]{1,0:T(8,128)} %pad.36.cond, ...), custom_call_target="tpu_custom_call" | custom-call | tf_op jit(solution)/shard_map/pallas_call | solution.py:496
  167.6 13.1 %multiply_convert_fusion = (bf16[1024,2304]{1,0:T(8,128)(2,1)S(1)}, f32[1024,2304]{1,0:T(8,128)}) fusion(f32[2304]{0:T(1024)S(1)} %add.182, bf16[1024,1152]{1,0:T(8,128)(2,1)} %get-tuple-element.70, bf16[2304,1152]{1,0:T(8,128)(2,1)} %bitcast.130), kind=kOutput, calls=%fused_computation.11 | convolution fusion | flops 5459410944 | bytes 21832704 | tf_op jit(solution)/shard_map/dot_general | solution.py:29
  180.7 5.4 %convolution_convert_fusion.1 = bf16[1152,1152]{1,0:T(8,128)(2,1)} fusion(bf16[1024,1152]{1,0:T(8,128)(2,1)S(1)} %copy-done.3, bf16[1024,2304]{1,0:T(8,128)(2,1)S(1)} %get-tuple-element.54), kind=kOutput, calls=%fused_computation.13 | convolution fusion | flops 2719236096 | bytes 7372800 | tf_op jit(solution)/shard_map/dot_general | solution.py:29
  186.9 13.8 %convert_reduce_fusion = (f32[2304]{0:T(1024)}, bf16[1024,2304]{1,0:T(8,128)(2,1)S(1)}) fusion(f32[1024,2304]{1,0:T(8,128)} %get-tuple-element.114, f32[2304]{0:T(1024)S(1)} %add.182, bf16[1024,1152]{1,0:T(8,128)(2,1)S(1)} %copy-done.3, bf16[2304,1152]{1,0:T(8,128)(2,1)S(1)} %bitcast.126), kind=kOutput, calls=%fused_computation.10 | convolution fusion | flops 5487720448 | bytes 21841920 | tf_op jit(solution)/shard_map/dot_general | solution.py:29
  200.7 4.2 convolution_convert_fusion.3
  205.0 4.8 %convolution_convert_fusion = bf16[1152,1152]{1,0:T(8,128)(2,1)} fusion(bf16[1024,1152]{1,0:T(8,128)(2,1)S(1)} %copy-done.32, bf16[1024,2304]{1,0:T(8,128)(2,1)S(1)} %get-tuple-element.69), kind=kOutput, calls=%fused_computation.12 | convolution fusion | flops 2719236096 | bytes 7372800 | tf_op jit(solution)/shard_map/dot_general | solution.py:29
  209.8 1.2 collective-permute-start.4
  213.5 3.0 fusion.61
  216.5 1.4 reshape.421
  217.9 1.6 fusion.43
  219.5 2.1 convert_reduce_fusion.1
  221.5 1.5 reshape.422
  223.0 1.3 broadcast_in_dim.52
  224.3 1.3 convert_element_type.165
  227.1 1.3 rsqrt.21
  229.0 1.3 add_rsqrt_fusion
  230.3 1.3 copy_bitcast_fusion
  231.6 8.2 %fusion.33 = (f32[512]{0:T(512)S(1)}, f32[512]{0:T(512)S(1)}, f32[512,1152]{1,0:T(8,128)}) fusion(f32[2,1152]{1,0:T(2,128)S(1)} %get-tuple-element.121, f32[512]{0:T(512)} %add_rsqrt_fusion.1, f32[512,1152]{1,0:T(8,128)S(1)} %get-tuple-element.95, f32[512]{0:T(512)S(1)} %broadcast_multiply_fusion.4, bf16[512,1152]{1,0:T(8,128)(2,1)} %collective-permute-done, ...), kind=kOutput, calls=%fused_computation.68 | convolution fusion | flops 2722626560 | bytes 13583360 | tf_op jit(solution)/shard_map/dot_general | solution.py:29
  241.0 1.3 div.59
  242.3 1.3 div.61
  243.5 4.6 convert_reduce_fusion.2
  248.2 7.8 %convolution_convert_fusion.2 = bf16[512,1152]{1,0:T(8,128)(2,1)} fusion(bf16[2304,1152]{1,0:T(8,128)(2,1)} %bitcast.125, bf16[1024,2304]{1,0:T(8,128)(2,1)} %copy-done.11), kind=kOutput, calls=%fused_computation.22 | convolution fusion | flops 2718498816 | bytes 8847360 | tf_op jit(solution)/shard_map/dot_general | solution.py:29
  256.3 1.8 fusion.35
  258.1 3.3 fusion.26
  262.1 2.1 fusion.37
  265.5 4.4 fusion.25
  269.9 6.3 %collective-permute-done.2 = bf16[512,1152]{1,0:T(8,128)(2,1)S(1)} collective-permute-done((bf16[512,1152]{1,0:T(8,128)(2,1)S(1)}, bf16[512,1152]{1,0:T(8,128)(2,1)S(1)}, u32[]{:S(2)}, u32[]{:S(2)}) %collective-permute-start.2) | collective-permute-done | bytes 1179680 | tf_op jit(solution)/shard_map/ppermute | solution.py:25
  276.3 1.6 pad_maximum_fusion.gao_row
  277.9 2.6 multiply_reduce_fusion.3
  281.2 3.9 fusion.14
  285.2 4.0 fusion.12
  289.1 161.3 %shard_map.247 = (f32[512,1152]{1,0:T(8,128)}, bf16[64,216]{1,0:T(8,128)(2,1)}, f32[16,1152]{1,0:T(8,128)}, bf16[2,4,2,144,1152]{4,3,2,1,0:T(8,128)(2,1)}, bf16[4,2,160,1152]{3,2,1,0:T(8,128)(2,1)}) custom-call(bf16[1024,1152]{1,0:T(8,128)(2,1)} %pad_maximum_fusion.gao_row, bf16[1024,1152]{1,0:T(8,128)(2,1)} %get-tuple-element.55.x_row, ...), custom_call_target="tpu_custom_call" | custom-call | tf_op jit(solution)/shard_map/pallas_call | solution.py:873
  450.4 1.9 slice.146
  452.3 1.4 slice.148
  454.5 1.4 fusion.40
  456.3 2.9 bitcast_convert_fusion
  459.2 6.1 %fusion.10 = f32[1152,1152]{1,0:T(8,128)} fusion(bf16[1152,1152]{1,0:T(8,128)(2,1)S(1)} %bitcast.137), kind=kOutput, calls=%fused_computation.18 | convolution fusion | flops 3058974720 | bytes 7962624 | tf_op jit(solution)/shard_map/dot_general | solution.py:29
  466.1 2.4 convert_bitcast_fusion
  469.1 1.3 fusion.67
  471.2 1.2 bitcast_convert_fusion.1
  472.4 1.5 slice_reduce_fusion
  474.0 2.2 multiply_add_fusion.1
  (139 shorter events, 18.8 us)
Async XLA Ops:
  11.5 3.6 copy-start.18
  167.6 13.1 %copy-start.3 = (bf16[1024,1152]{1,0:T(8,128)(2,1)S(1)}, bf16[1024,1152]{1,0:T(8,128)(2,1)}, u32[]{:S(2)}) copy-start(bf16[1024,1152]{1,0:T(8,128)(2,1)} %get-tuple-element.67) | copy-start | bytes 7077892
  180.7 5.4 %copy-start.11 = (bf16[1024,2304]{1,0:T(8,128)(2,1)}, bf16[1024,2304]{1,0:T(8,128)(2,1)S(1)}, u32[]{:S(2)}) copy-start(bf16[1024,2304]{1,0:T(8,128)(2,1)S(1)} %get-tuple-element.54) | copy-start | bytes 14155780
  180.7 6.2 %copy-start.10 = (bf16[4,4,144,1152]{3,2,1,0:T(8,128)(2,1)S(1)}, bf16[4,4,144,1152]{3,2,1,0:T(8,128)(2,1)}, u32[]{:S(2)}) copy-start(bf16[4,4,144,1152]{3,2,1,0:T(8,128)(2,1)} %get-tuple-element.53) | copy-start | bytes 15925252
  180.7 20.0 %slice-start.2 = ((s8[5308416]{0:T(1024)(128)(4,1)}), s8[4194304]{0:T(1024)(128)(4,1)S(1)}, s32[]{:S(2)}) async-start(s8[5308416]{0:T(1024)(128)(4,1)} %bitcast.132), calls=%async_computation.2 | async-start | bytes 8388608
  186.1 95.1 %collective-permute-start.3 = (bf16[2,4,144,1152]{3,2,1,0:T(8,128)(2,1)}, bf16[2,4,144,1152]{3,2,1,0:T(8,128)(2,1)}, u32[]{:S(2)}, u32[]{:S(2)}) collective-permute-start(bf16[2,4,144,1152]{3,2,1,0:T(8,128)(2,1)} %bitcast.9), channel_id=1, source_target_pairs={{0,8},{4,12},{8,0},{12,4},{16,24},{20,28},{24,16},{28,20},{1,9},{5... | collective-permute-start | bytes 7962632 | tf_op jit(solution)/shard_map/ppermute | solution.py:25
  186.9 13.9 %slice-start.3 = ((s8[5308416]{0:T(1024)(128)(4,1)}), s8[1114112]{0:T(1024)(128)(4,1)S(1)}, s32[]{:S(2)}) async-start(s8[5308416]{0:T(1024)(128)(4,1)} %bitcast.132), calls=%async_computation.3 | async-start | bytes 2228224
  200.7 4.2 copy-start.12
  200.7 4.2 copy-start.32
  204.9 6.1 %copy-start = (bf16[512,1152]{1,0:T(8,128)(2,1)S(1)}, bf16[512,1152]{1,0:T(8,128)(2,1)}, u32[]{:S(2)}) copy-start(bf16[512,1152]{1,0:T(8,128)(2,1)} %patches.3) | copy-start | bytes 3538948
  204.9 26.6 %collective-permute-start = (bf16[512,1152]{1,0:T(8,128)(2,1)}, bf16[512,1152]{1,0:T(8,128)(2,1)}, u32[]{:S(2)}, u32[]{:S(2)}) collective-permute-start(bf16[512,1152]{1,0:T(8,128)(2,1)} %convolution_convert_fusion.3), channel_id=1, source_target_pairs={{0,4},{4,0},{8,12},{12,8},{16,20},{20,16},{24,28},{28,24},{1,5},{5... | collective-permute-start | bytes 3538952 | tf_op jit(solution)/shard_map/ppermute | solution.py:25
  209.8 71.4 %collective-permute-start.4 = (bf16[2,4,144,1152]{3,2,1,0:T(8,128)(2,1)}, bf16[2,4,144,1152]{3,2,1,0:T(8,128)(2,1)}, u32[]{:S(2)}, u32[]{:S(2)}) collective-permute-start(bf16[2,4,144,1152]{3,2,1,0:T(8,128)(2,1)} %bitcast.13), channel_id=1, source_target_pairs={{0,16},{4,20},{8,24},{12,28},{16,0},{20,4},{24,8},{28,12},{1,17},{... | collective-permute-start | bytes 7962632 | tf_op jit(solution)/shard_map/ppermute | solution.py:25
  213.4 3.0 copy-start.22
  213.5 3.0 copy-start.14
  243.5 12.7 %slice-start.4 = ((s8[4718592]{0:T(1024)(128)(4,1)}), s8[4194304]{0:T(1024)(128)(4,1)S(1)}, s32[]{:S(2)}) async-start(s8[4718592]{0:T(1024)(128)(4,1)} %bitcast.135), calls=%async_computation.4 | async-start | bytes 8388608
  243.5 14.5 %slice-start.6 = ((s8[4718592]{0:T(1024)(128)(4,1)}), s8[524288]{0:T(1024)(128)(4,1)S(1)}, s32[]{:S(2)}) async-start(s8[4718592]{0:T(1024)(128)(4,1)} %bitcast.141), calls=%async_computation.6 | async-start | bytes 1048576
  248.2 28.1 %collective-permute-start.2 = (bf16[512,1152]{1,0:T(8,128)(2,1)S(1)}, bf16[512,1152]{1,0:T(8,128)(2,1)S(1)}, u32[]{:S(2)}, u32[]{:S(2)}) collective-permute-start(bf16[512,1152]{1,0:T(8,128)(2,1)S(1)} %get-tuple-element.91), channel_id=1, source_target_pairs={{0,1},{1,0},{2,3},{3,2},{4,5},{5,4},{6,7},{7,6},{8,9},{9,8},{10,11... | collective-permute-start | bytes 3538952 | tf_op jit(solution)/shard_map/ppermute | solution.py:25
  248.2 8.1 %copy-start.4 = (bf16[1024,1152]{1,0:T(8,128)(2,1)S(1)}, bf16[1024,1152]{1,0:T(8,128)(2,1)}, u32[]{:S(2)}) copy-start(bf16[1024,1152]{1,0:T(8,128)(2,1)} %get-tuple-element.67) | copy-start | bytes 7077892
  248.2 8.1 %slice-start.5 = ((s8[4718592]{0:T(1024)(128)(4,1)}), s8[524288]{0:T(1024)(128)(4,1)S(1)}, s32[]{:S(2)}) async-start(s8[4718592]{0:T(1024)(128)(4,1)} %bitcast.135), calls=%async_computation.5 | async-start | bytes 1048576
  248.2 9.8 %slice-start.7 = ((s8[4718592]{0:T(1024)(128)(4,1)}), s8[4194304]{0:T(1024)(128)(4,1)S(1)}, s32[]{:S(2)}) async-start(s8[4718592]{0:T(1024)(128)(4,1)} %bitcast.141), calls=%async_computation.7 | async-start | bytes 8388608
  256.0 2.0 copy-start.33
  256.0 8.6 %collective-permute-start.1 = (bf16[512,1152]{1,0:T(8,128)(2,1)}, bf16[512,1152]{1,0:T(8,128)(2,1)S(1)}, u32[]{:S(2)}, u32[]{:S(2)}) collective-permute-start(bf16[512,1152]{1,0:T(8,128)(2,1)} %convolution_convert_fusion.2), channel_id=1, source_target_pairs={{0,4},{4,0},{8,12},{12,8},{16,20},{20,16},{24,28},{28,24},{1,5},{5... | collective-permute-start | bytes 3538952 | tf_op jit(solution)/shard_map/ppermute | solution.py:25
  258.1 3.4 copy-start.20
  258.1 3.4 copy-start.26
  258.1 3.4 copy-start.31
  262.1 2.5 slice-start
  264.2 1.3 slice-start.1
  264.2 1.3 copy-start.21
  264.2 1.3 copy-start.24
  265.5 12.3 %copy-start.7 = (f32[512,1152]{1,0:T(8,128)S(1)}, f32[512,1152]{1,0:T(8,128)}, u32[]{:S(2)}) copy-start(f32[512,1152]{1,0:T(8,128)} %get-tuple-element.47) | copy-start | bytes 7077892
  269.9 8.0 %copy-start.2 = (f32[512,1152]{1,0:T(8,128)S(1)}, f32[512,1152]{1,0:T(8,128)}, u32[]{:S(2)}) copy-start(f32[512,1152]{1,0:T(8,128)} %get-tuple-element.93) | copy-start | bytes 7077892
  269.9 8.0 %copy-start.5 = (bf16[512,1152]{1,0:T(8,128)(2,1)S(1)}, bf16[512,1152]{1,0:T(8,128)(2,1)}, u32[]{:S(2)}) copy-start(bf16[512,1152]{1,0:T(8,128)(2,1)} %cotangent.1) | copy-start | bytes 3538948
  269.9 8.0 %copy-start.15 = (f32[2,1152]{1,0:T(2,128)S(1)}, f32[2,1152]{1,0:T(2,128)}, u32[]{:S(2)}) copy-start(f32[2,1152]{1,0:T(2,128)} %copy-done.14) | copy-start | bytes 27652
  269.9 8.0 %copy-start.27 = (f32[2,256]{1,0:T(2,128)S(1)}, f32[2,256]{1,0:T(2,128)}, u32[]{:S(2)}) copy-start(f32[2,256]{1,0:T(2,128)} %div.60) | copy-start | bytes 6148
  269.9 8.0 %copy-start.28 = (f32[2,256]{1,0:T(2,128)S(1)}, f32[2,256]{1,0:T(2,128)}, u32[]{:S(2)}) copy-start(f32[2,256]{1,0:T(2,128)} %rsqrt.21) | copy-start | bytes 6148
  269.9 8.0 %copy-start.29 = (f32[2,256]{1,0:T(2,128)S(1)}, f32[2,256]{1,0:T(2,128)}, u32[]{:S(2)}) copy-start(f32[2,256]{1,0:T(2,128)} %div.59) | copy-start | bytes 6148
  269.9 8.0 %copy-start.30 = (f32[2,256]{1,0:T(2,128)S(1)}, f32[2,256]{1,0:T(2,128)}, u32[]{:S(2)}) copy-start(f32[2,256]{1,0:T(2,128)} %div.61) | copy-start | bytes 6148
  289.1 165.3 %copy-start.19 = (bf16[5,1152]{1,0:T(8,128)(2,1)S(1)}, bf16[5,1152]{1,0:T(8,128)(2,1)}, u32[]{:S(2)}) copy-start(bf16[5,1152]{1,0:T(8,128)(2,1)} %param.17) | copy-start | bytes 34564
  450.4 5.5 %copy-start.9 = (bf16[2,4,2,144,1152]{4,3,2,1,0:T(8,128)(2,1)S(1)}, bf16[2,4,2,144,1152]{4,3,2,1,0:T(8,128)(2,1)}, u32[]{:S(2)}) copy-start(bf16[2,4,2,144,1152]{4,3,2,1,0:T(8,128)(2,1)} %get-tuple-element.78) | copy-start | bytes 15925252
  466.0 2.5 copy-start.16
  466.0 3.1 copy-start.13
  466.1 4.4 copy-start.1
  466.1 4.4 copy-start.6
  466.1 4.4 copy-start.17
  466.1 4.4 copy-start.23
  466.1 4.4 copy-start.25
  470.4 3.5 copy-start.8

commit v5 on v4

--- a/solution.py
+++ b/solution.py
@@ -46,8 +46,7 @@
     return centred * rsig, rsig
 
 
-def norm_back(grad_in, normed, rsig, scale):
-    u = grad_in * (1.0 + scale)
+def norm_back(u, normed, rsig):
     mean_u = jnp.mean(u, axis=-1, keepdims=True)
     mean_un = jnp.mean(u * normed, axis=-1, keepdims=True)
     return (u - mean_u - normed * mean_un) * rsig
@@ -995,10 +994,10 @@
 
     patch_wide = blocks(patches.astype(F32))
     grad_output = blocks(cotangent.astype(F32))
-    norm_a, rsig_a = layer_norm(patch_wide)
+    norm_a, rsig_a = layer_norm(flat(patch_wide))
     attn_out = blocks(attn_out)
     resid = patch_wide + gate_attn * attn_out
-    norm_m, rsig_m = layer_norm(resid)
+    norm_m, rsig_m = layer_norm(flat(resid))
 
     gmo = gmo2[:tokens]
     pre = dot(mlp2, w1_all, 1, 1) + b1_all
@@ -1023,11 +1022,11 @@
     gin_peer = swap(dot(grad_pre[tokens:], w1_all, 1, 0).astype(BF), "dp", 1)
     g_mlp_in = blocks(dot(grad_pre[:tokens], w1_all, 1, 0) + gin_peer.astype(F32))
     g_shift_mlp = jnp.sum(g_mlp_in, axis=1)
-    g_scale_mlp = jnp.sum(g_mlp_in * norm_m, axis=1)
-    grad_resid = grad_output + norm_back(g_mlp_in, norm_m, rsig_m, scale_mlp)
+    g_scale_mlp = jnp.sum(g_mlp_in * blocks(norm_m), axis=1)
+    u_mlp = flat(g_mlp_in * (1.0 + scale_mlp))
+    grad_resid = grad_output + blocks(norm_back(u_mlp, norm_m, rsig_m))
     g_gate_attn = jnp.sum(grad_resid * attn_out, axis=1)
     gao = flat((gate_attn * grad_resid).astype(BF))
-    grad_bout = jnp.sum(gao, axis=0, dtype=F32)
     gao_row = jnp.concatenate([gao, swap(gao, "mp", 1)], axis=0)
 
     hidden_w, gmo2_w, gpre_w, mlp2_w = lax.optimization_barrier(
@@ -1041,7 +1040,9 @@
     )
     output = flat((resid + gate_mlp * mlp_out).astype(BF))
     g_gate_mlp = jnp.sum(grad_output * mlp_out, axis=1)
-    grad_b2 = jnp.sum(gmo, axis=0, dtype=F32)
+    grad_b2 = jnp.sum(after(gmo, gao), axis=0, dtype=F32)
+    grad_b1 = after(grad_b1, gao)
+    grad_bout = jnp.sum(gao, axis=0, dtype=F32)
 
     come2, come1 = lax.optimization_barrier((come2, come1, keep2_0))[:2]
     two_2 = low_sum(keep2_2, come2[1])
@@ -1079,7 +1080,8 @@
     att_all = drop_pads(att_all.reshape(4, wide, width))
     out_qkv = att_all[:3].transpose(0, 2, 1).astype(F32)
     out_wout = att_all[3].astype(F32)
-    grad_patches = flat(grad_resid + norm_back(g_attn_in, norm_a, rsig_a, scale_attn))
+    u_attn = flat(g_attn_in * (1.0 + scale_attn))
+    grad_patches = flat(grad_resid) + norm_back(u_attn, norm_a, rsig_a)
     grad_w_ada = dot(silu_cond, grad_cols, 0, 0)
     grad_b_ada = jnp.sum(grad_cols, axis=0, dtype=F32)
     grad_silu = final[: conditioning.shape[0]]

time: 484 us -> 482 us (level)
  waiting for transfers between devices: 6.34 us -> 0.01 us
    ppermute x5, waiting for transfers between devices: 6.34 us -> 0.01 us  [swap(): return lax.ppermute(value, axis, [(i, i ^ bit) for i in range(n)])]
  transfers between devices with their start and end apart: 5 -> 5, of which waited for: 1 -> 0; matrix products, arithmetic and copies ran while one was open for 18% -> 18% of each run, Pallas kernels for 0% -> 0%
where the time goes in v5:
time: 482 us; the launch traced here: 475 us
  Pallas kernels  312 us (65%)
  matrix products  79.5 us (16%)
  other arithmetic  48.1 us (10%)
  local copies, waits for them, and re-layouts  31.6 us (7%)
    pallas_call x1, Pallas kernels, back(): pl.pallas_call(functools.partial(back_kernel, per_dp), out_shape=shapes,...  162 us
    pallas_call x1, Pallas kernels, front(): pl.pallas_call(functools.partial(front_kernel, per_dp), out_shape=shapes,...  150 us
    dot_general x13, matrix products, dot(): lax.dot_general(a, b, (((ca,), (cb,)), ((), ())), preferred_element_type=...  77.9 us
  transfers between devices with their start and end apart: 5, of which 0 were waited for; matrix products, arithmetic and copies ran while one was open for 18% of the time, Pallas kernels for 0%

profile of v5, /device:TPU:0, one launch (start us, length us, event | category | flops | bytes accessed | tf_op | source)
XLA Modules:
  0.0 475.0 jit_solution(16489532083483524621)
XLA Ops:
  0.7 0.8 fusion.74
  1.5 1.0 copy.34.seg
  2.5 2.1 copy.33.w_ada
  6.2 1.3 fusion.57.bias
  9.0 1.3 reshape.333.b_out
  10.3 1.2 broadcast_in_dim.54
  11.5 3.6 fusion.11
  16.4 150.4 %shard_map.246 = (bf16[64,1152]{1,0:T(8,128)(2,1)}, f32[32,8,128]{2,1,0:T(8,128)}, f32[16,144]{1,0:T(8,128)}, f32[8,6912]{1,0:T(8,128)}, bf16[1024,1152]{1,0:T(8...) custom-call(f32[8,1152]{1,0:T(8,128)} %pad.36.cond, ...), custom_call_target="tpu_custom_call" | custom-call | tf_op jit(solution)/shard_map/pallas_call | solution.py:495
  167.5 13.1 %multiply_convert_fusion = (bf16[1024,2304]{1,0:T(8,128)(2,1)S(1)}, f32[1024,2304]{1,0:T(8,128)}) fusion(f32[2304]{0:T(1024)S(1)} %add.172, bf16[1024,1152]{1,0:T(8,128)(2,1)} %get-tuple-element.72, bf16[2304,1152]{1,0:T(8,128)(2,1)} %bitcast.133), kind=kOutput, calls=%fused_computation.11 | convolution fusion | flops 5459410944 | bytes 21832704 | tf_op jit(solution)/shard_map/dot_general | solution.py:29
  180.7 5.4 %convolution_convert_fusion.1 = bf16[1152,1152]{1,0:T(8,128)(2,1)} fusion(bf16[1024,1152]{1,0:T(8,128)(2,1)S(1)} %copy-done.7, bf16[1024,2304]{1,0:T(8,128)(2,1)S(1)} %get-tuple-element.56), kind=kOutput, calls=%fused_computation.13 | convolution fusion | flops 2719236096 | bytes 7372800 | tf_op jit(solution)/shard_map/dot_general | solution.py:29
  186.8 13.8 %convert_reduce_fusion = (f32[2304]{0:T(1024)}, bf16[1024,2304]{1,0:T(8,128)(2,1)S(1)}) fusion(f32[1024,2304]{1,0:T(8,128)} %get-tuple-element.117, f32[2304]{0:T(1024)S(1)} %add.172, bf16[1024,1152]{1,0:T(8,128)(2,1)S(1)} %copy-done.7, bf16[2304,1152]{1,0:T(8,128)(2,1)S(1)} %bitcast.139), kind=kOutput, calls=%fused_computation.10 | convolution fusion | flops 5487720448 | bytes 21841920 | tf_op jit(solution)/shard_map/dot_general | solution.py:29
  200.7 4.2 convolution_convert_fusion.3
  204.9 4.9 %convolution_convert_fusion = bf16[1152,1152]{1,0:T(8,128)(2,1)} fusion(bf16[1024,1152]{1,0:T(8,128)(2,1)S(1)} %copy-done.34, bf16[1024,2304]{1,0:T(8,128)(2,1)S(1)} %get-tuple-element.71), kind=kOutput, calls=%fused_computation.12 | convolution fusion | flops 2719236096 | bytes 7372800 | tf_op jit(solution)/shard_map/dot_general | solution.py:29
  209.8 1.2 collective-permute-start.4
  211.0 2.4 slice.123
  213.4 1.6 slice.104
  215.0 1.5 reshape.325
  216.5 1.7 slice_add_fusion
  219.2 1.2 convert_reduce_fusion.1
  224.7 1.3 copy_bitcast_fusion
  226.0 8.0 %fusion.41 = (f32[512]{0:T(512)S(1)}, f32[512]{0:T(512)S(1)}, f32[512]{0:T(512)}, f32[512,1152]{1,0:T(8,128)S(1)}) fusion(f32[2,1152]{1,0:T(2,128)} %get-tuple-element.124, bf16[512,1152]{1,0:T(8,128)(2,1)} %collective-permute-done, f32[512]{0:T(512)S(1)} %add_rsqrt_fusion.1, f32[512]{0:T(512)S(1)} %broadcast_multiply_fusion.4, ...), kind=kOutput, calls=%fused_computation.77 | convolution fusion | flops 2726164992 | bytes 14776320 | tf_op jit(solution)/shard_map/dot_general | solution.py:29
  234.1 5.5 %convert_reduce_fusion.3 = (f32[1152]{0:T(1024)}, bf16[512,1152]{1,0:T(8,128)(2,1)}, f32[512,1152]{1,0:T(8,128)}) fusion(f32[2,1152]{1,0:T(2,128)S(1)} %get-tuple-element.125, f32[512]{0:T(512)S(1)} %broadcast_multiply_fusion.3, f32[512]{0:T(512)S(1)} %add_rsqrt_fusion.1, f32[512]{0:T(512)S(1)} %broadcast_multiply_fusion.4, f32[512,1152]{1,0:T(8,128)S(1)} %copy-done.2, ...), kind=kLoop, calls=%fused_computation.66 | loop fusion | flops 10615680 | bytes 11827712 | tf_op jit(solution)/shard_map/reduce_sum | solution.py:1045
  239.6 1.4 reshape.330
  241.0 1.6 fusion.51
  242.6 1.5 reshape.331
  244.0 1.6 convert_reduce_fusion.2
  246.4 6.6 %convolution_convert_fusion.2 = bf16[512,1152]{1,0:T(8,128)(2,1)S(1)} fusion(bf16[2304,1152]{1,0:T(8,128)(2,1)} %bitcast.138, bf16[1024,2304]{1,0:T(8,128)(2,1)} %copy-done.14), kind=kOutput, calls=%fused_computation.25 | convolution fusion | flops 2718498816 | bytes 8847360 | tf_op jit(solution)/shard_map/dot_general | solution.py:29
  253.2 3.2 fusion.43
  256.5 3.3 fusion.34
  261.2 2.1 bitcast_reduce_fusion.1
  263.4 2.1 fusion.45
  265.8 1.0 copy-done.15
  267.8 6.0 %fusion.72 = (f32[512,1152]{1,0:T(8,128)S(1)}, bf16[512,1152]{1,0:T(8,128)(2,1)}, f32[512,1152]{1,0:T(8,128)S(1)}) fusion(f32[512,1152]{1,0:T(8,128)S(1)} %copy-done.5, f32[512,1152]{1,0:T(8,128)S(1)} %copy-done.2, f32[2,1152]{1,0:T(2,128)S(1)} %copy-done.24, f32[2,1152]{1,0:T(2,128)S(1)} %get-tuple-element.125, bf16[512,1152]{1,0:T(8,128)(2,1)S(1)} %copy-done, ...), kind=kOutput, calls=%fused_computation.155 | convolution fusion | flops 2723807232 | bytes 20670464 | tf_op jit(solution)/shard_map/dot_general | solution.py:29
  273.9 1.1 copy-done.10
  275.3 3.2 pad_maximum_fusion.gao_row
  279.2 3.9 fusion.18
  283.2 4.0 fusion.16
  287.2 161.6 %shard_map.247 = (f32[512,1152]{1,0:T(8,128)}, bf16[64,216]{1,0:T(8,128)(2,1)}, f32[16,1152]{1,0:T(8,128)}, bf16[2,4,2,144,1152]{4,3,2,1,0:T(8,128)(2,1)}, bf16[4,2,160,1152]{3,2,1,0:T(8,128)(2,1)}) custom-call(bf16[1024,1152]{1,0:T(8,128)(2,1)} %pad_maximum_fusion.gao_row, bf16[1024,1152]{1,0:T(8,128)(2,1)} %get-tuple-element.57.x_row, ...), custom_call_target="tpu_custom_call" | custom-call | tf_op jit(solution)/shard_map/pallas_call | solution.py:872
  448.8 1.9 slice.146
  450.7 1.4 slice.148
  452.9 1.4 fusion.48
  454.7 2.9 bitcast_convert_fusion
  457.6 6.1 %fusion.10 = f32[1152,1152]{1,0:T(8,128)} fusion(bf16[1152,1152]{1,0:T(8,128)(2,1)S(1)} %bitcast.145), kind=kOutput, calls=%fused_computation.18 | convolution fusion | flops 3058974720 | bytes 7962624 | tf_op jit(solution)/shard_map/dot_general | solution.py:29
  464.5 2.4 convert_bitcast_fusion
  467.5 1.3 fusion.75
  469.7 1.2 bitcast_convert_fusion.1
  470.9 1.5 slice_reduce_fusion
  472.4 2.2 fusion.23
  (141 shorter events, 19.3 us)
Async XLA Ops:
  11.5 3.6 copy-start.21
  167.5 13.1 %copy-start.7 = (bf16[1024,1152]{1,0:T(8,128)(2,1)S(1)}, bf16[1024,1152]{1,0:T(8,128)(2,1)}, u32[]{:S(2)}) copy-start(bf16[1024,1152]{1,0:T(8,128)(2,1)} %get-tuple-element.69) | copy-start | bytes 7077892
  180.7 5.4 %copy-start.14 = (bf16[1024,2304]{1,0:T(8,128)(2,1)}, bf16[1024,2304]{1,0:T(8,128)(2,1)S(1)}, u32[]{:S(2)}) copy-start(bf16[1024,2304]{1,0:T(8,128)(2,1)S(1)} %get-tuple-element.56) | copy-start | bytes 14155780
  180.7 6.1 %copy-start.13 = (bf16[4,4,144,1152]{3,2,1,0:T(8,128)(2,1)S(1)}, bf16[4,4,144,1152]{3,2,1,0:T(8,128)(2,1)}, u32[]{:S(2)}) copy-start(bf16[4,4,144,1152]{3,2,1,0:T(8,128)(2,1)} %get-tuple-element.55) | copy-start | bytes 15925252
  180.7 20.0 %slice-start = ((s8[5308416]{0:T(1024)(128)(4,1)}), s8[4194304]{0:T(1024)(128)(4,1)S(1)}, s32[]{:S(2)}) async-start(s8[5308416]{0:T(1024)(128)(4,1)} %bitcast.135), calls=%async_computation | async-start | bytes 8388608
  186.1 93.2 %collective-permute-start.3 = (bf16[2,4,144,1152]{3,2,1,0:T(8,128)(2,1)}, bf16[2,4,144,1152]{3,2,1,0:T(8,128)(2,1)}, u32[]{:S(2)}, u32[]{:S(2)}) collective-permute-start(bf16[2,4,144,1152]{3,2,1,0:T(8,128)(2,1)} %bitcast.9), channel_id=1, source_target_pairs={{0,8},{4,12},{8,0},{12,4},{16,24},{20,28},{24,16},{28,20},{1,9},{5... | collective-permute-start | bytes 7962632 | tf_op jit(solution)/shard_map/ppermute | solution.py:25
  186.8 13.8 %slice-start.1 = ((s8[5308416]{0:T(1024)(128)(4,1)}), s8[1114112]{0:T(1024)(128)(4,1)S(1)}, s32[]{:S(2)}) async-start(s8[5308416]{0:T(1024)(128)(4,1)} %bitcast.135), calls=%async_computation.1 | async-start | bytes 2228224
  200.7 4.2 copy-start.16
  200.7 4.2 copy-start.34
  204.9 21.1 %collective-permute-start = (bf16[512,1152]{1,0:T(8,128)(2,1)}, bf16[512,1152]{1,0:T(8,128)(2,1)}, u32[]{:S(2)}, u32[]{:S(2)}) collective-permute-start(bf16[512,1152]{1,0:T(8,128)(2,1)} %convolution_convert_fusion.3), channel_id=1, source_target_pairs={{0,4},{4,0},{8,12},{12,8},{16,20},{20,16},{24,28},{28,24},{1,5},{5... | collective-permute-start | bytes 3538952 | tf_op jit(solution)/shard_map/ppermute | solution.py:25
  204.9 13.8 %copy-start.2 = (f32[512,1152]{1,0:T(8,128)S(1)}, f32[512,1152]{1,0:T(8,128)}, u32[]{:S(2)}) copy-start(f32[512,1152]{1,0:T(8,128)} %get-tuple-element.49) | copy-start | bytes 7077892
  209.8 9.0 %copy-start = (bf16[512,1152]{1,0:T(8,128)(2,1)S(1)}, bf16[512,1152]{1,0:T(8,128)(2,1)}, u32[]{:S(2)}) copy-start(bf16[512,1152]{1,0:T(8,128)(2,1)} %patches.3) | copy-start | bytes 3538948
  209.8 69.4 %collective-permute-start.4 = (bf16[2,4,144,1152]{3,2,1,0:T(8,128)(2,1)}, bf16[2,4,144,1152]{3,2,1,0:T(8,128)(2,1)}, u32[]{:S(2)}, u32[]{:S(2)}) collective-permute-start(bf16[2,4,144,1152]{3,2,1,0:T(8,128)(2,1)} %bitcast.13), channel_id=1, source_target_pairs={{0,16},{4,20},{8,24},{12,28},{16,0},{20,4},{24,8},{28,12},{1,17},{... | collective-permute-start | bytes 7962632 | tf_op jit(solution)/shard_map/ppermute | solution.py:25
  219.2 1.2 copy-start.32
  224.0 10.0 %copy-start.27 = (f32[512]{0:T(512)}, f32[512]{0:T(512)S(1)}, u32[]{:S(2)}) copy-start(f32[512]{0:T(512)S(1)} %add_rsqrt_fusion.1) | copy-start | bytes 6148
  224.7 9.3 %copy-start.25 = (f32[512]{0:T(512)}, f32[512]{0:T(512)S(1)}, u32[]{:S(2)}) copy-start(f32[512]{0:T(512)S(1)} %broadcast_multiply_fusion.1) | copy-start | bytes 6148
  226.0 8.0 %copy-start.9 = (bf16[512,1152]{1,0:T(8,128)(2,1)S(1)}, bf16[512,1152]{1,0:T(8,128)(2,1)}, u32[]{:S(2)}) copy-start(bf16[512,1152]{1,0:T(8,128)(2,1)} %cotangent.1) | copy-start | bytes 3538948
  226.0 8.0 %copy-start.19 = (f32[2,1152]{1,0:T(2,128)S(1)}, f32[2,1152]{1,0:T(2,128)}, u32[]{:S(2)}) copy-start(f32[2,1152]{1,0:T(2,128)} %get-tuple-element.124) | copy-start | bytes 27652
  234.0 5.6 %copy-start.3 = (f32[512,1152]{1,0:T(8,128)}, f32[512,1152]{1,0:T(8,128)S(1)}, u32[]{:S(2)}) copy-start(f32[512,1152]{1,0:T(8,128)S(1)} %get-tuple-element.118) | copy-start | bytes 7077892
  239.6 35.7 %collective-permute-start.2 = (bf16[512,1152]{1,0:T(8,128)(2,1)}, bf16[512,1152]{1,0:T(8,128)(2,1)}, u32[]{:S(2)}, u32[]{:S(2)}) collective-permute-start(bf16[512,1152]{1,0:T(8,128)(2,1)} %get-tuple-element.96), channel_id=1, source_target_pairs={{0,1},{1,0},{2,3},{3,2},{4,5},{5,4},{6,7},{7,6},{8,9},{9,8},{10,11... | collective-permute-start | bytes 3538952 | tf_op jit(solution)/shard_map/ppermute | solution.py:25
  244.0 12.4 %slice-start.6 = ((s8[4718592]{0:T(1024)(128)(4,1)}), s8[4194304]{0:T(1024)(128)(4,1)S(1)}, s32[]{:S(2)}) async-start(s8[4718592]{0:T(1024)(128)(4,1)} %bitcast.149), calls=%async_computation.6 | async-start | bytes 8388608
  246.3 6.9 %copy-start.8 = (bf16[1024,1152]{1,0:T(8,128)(2,1)S(1)}, bf16[1024,1152]{1,0:T(8,128)(2,1)}, u32[]{:S(2)}) copy-start(bf16[1024,1152]{1,0:T(8,128)(2,1)} %get-tuple-element.69) | copy-start | bytes 7077892
  246.3 10.1 %slice-start.7 = ((s8[4718592]{0:T(1024)(128)(4,1)}), s8[524288]{0:T(1024)(128)(4,1)S(1)}, s32[]{:S(2)}) async-start(s8[4718592]{0:T(1024)(128)(4,1)} %bitcast.149), calls=%async_computation.7 | async-start | bytes 1048576
  252.9 3.5 copy-start.35
  252.9 12.9 %collective-permute-start.1 = (bf16[512,1152]{1,0:T(8,128)(2,1)S(1)}, bf16[512,1152]{1,0:T(8,128)(2,1)S(1)}, u32[]{:S(2)}, u32[]{:S(2)}) collective-permute-start(bf16[512,1152]{1,0:T(8,128)(2,1)S(1)} %convolution_convert_fusion.2), channel_id=1, source_target_pairs={{0,4},{4,0},{8,12},{12,8},{16,20},{20,16},{24,28},{28,24},{1,5},{5... | collective-permute-start | bytes 3538952 | tf_op jit(solution)/shard_map/ppermute | solution.py:25
  253.2 10.1 %slice-start.4 = ((s8[4718592]{0:T(1024)(128)(4,1)}), s8[4194304]{0:T(1024)(128)(4,1)S(1)}, s32[]{:S(2)}) async-start(s8[4718592]{0:T(1024)(128)(4,1)} %bitcast.143), calls=%async_computation.4 | async-start | bytes 8388608
  256.5 3.4 copy-start.23
  256.5 3.4 copy-start.33
  256.5 4.1 copy-start.31
  256.5 4.7 copy-start.4
  256.5 4.7 copy-start.28
  256.5 6.8 %slice-start.5 = ((s8[4718592]{0:T(1024)(128)(4,1)}), s8[524288]{0:T(1024)(128)(4,1)S(1)}, s32[]{:S(2)}) async-start(s8[4718592]{0:T(1024)(128)(4,1)} %bitcast.143), calls=%async_computation.5 | async-start | bytes 1048576
  263.3 3.5 slice-start.2
  265.4 2.1 copy-start.5
  265.4 2.4 slice-start.3
  265.4 2.4 copy-start.24
  265.5 2.3 copy-start.29
  273.8 1.3 copy-start.10
  287.2 165.7 %copy-start.22 = (bf16[5,1152]{1,0:T(8,128)(2,1)S(1)}, bf16[5,1152]{1,0:T(8,128)(2,1)}, u32[]{:S(2)}) copy-start(bf16[5,1152]{1,0:T(8,128)(2,1)} %param.17) | copy-start | bytes 34564
  448.8 5.5 %copy-start.12 = (bf16[2,4,2,144,1152]{4,3,2,1,0:T(8,128)(2,1)S(1)}, bf16[2,4,2,144,1152]{4,3,2,1,0:T(8,128)(2,1)}, u32[]{:S(2)}) copy-start(bf16[2,4,2,144,1152]{4,3,2,1,0:T(8,128)(2,1)} %get-tuple-element.82) | copy-start | bytes 15925252
  464.5 2.5 copy-start.18
  464.5 3.1 copy-start.17
  464.5 4.4 copy-start.1
  464.5 4.4 copy-start.11
  464.5 4.4 copy-start.20
  464.5 4.4 copy-start.26
  464.5 4.4 copy-start.30
  468.9 3.5 copy-start.6
  (1 other events, 1.0 us)
